TPU v7x, 32 devices: a whole 2x2x4 slice. The times are simulated.
32 devices in a mesh: lat: 16 (over z, y, x), lev: 2 (over core).
Axes of the slice: x: 2, y: 2, z: 4, core: 2. Of those that a mesh axis runs over, the one named last changes fastest.
Arguments:
- winds: float32 [2, 8, 512, 1440], P(None, 'lev', 'lat'), may hold values from -6 to 6
- thickness: float32 [8, 512, 1440], P('lev', 'lat'), may hold values from 0.5 to 2
- cutoff: int32 [512], P('lat'), may hold values from 1 to 720, as said below
Outputs:
- new_winds: float32 [2, 8, 512, 1440], P(None, 'lev', 'lat')
- new_thickness: float32 [8, 512, 1440], P('lev', 'lat')
Inputs may be any that keep to these rules, and one draw needn't show every extreme that they name: Rows outside the 96 latitudes nearest each pole have a cutoff of half of 1440; rows inside have smaller cutoffs.
All inputs are finite; a program needn't handle non-finite values.
Results may differ from a plain program's by a relative error of at most 0.0003.
Values sent between devices are 32-bit elements; how exact they have to be, the bound alone decides.
No kernel may reach another device: no remote copies, remote signals or barrier semaphores. Data moves between devices by JAX's collectives and lax.ppermute only.
A program may use at most 64 MiB of HBM per device.

v0:
```python
import functools
import math

import jax
import jax.numpy as jnp
import ml_dtypes
import numpy as np
from jax import lax
from jax.experimental import pallas as pl
from jax.experimental.pallas import tpu as pltpu
from jax.sharding import PartitionSpec as P

time_step = 0.2
coriolis = 1.0
RADIX = 12
LANES = 128
WIDE = 2 * LANES
HALF_ROOT3 = math.sqrt(3.0) / 2.0
f32 = jnp.float32
bf16 = jnp.bfloat16


def filter_tables(lon):
    chunk = lon // RADIX
    half = RADIX // 2
    table = np.zeros((half, WIDE, WIDE), np.float64)
    wave = np.zeros((half, WIDE), np.float64)
    point = np.arange(chunk, dtype=np.float64)
    unit = 2.0 * math.pi / lon

    def real_class(residue, at):
        column = at
        for q in range(chunk):
            m = RADIX * q + residue
            if m > lon // 2:
                break
            single = m == 0 or 2 * m == lon
            weight = math.sqrt((1.0 if single else 2.0) / (chunk * RADIX))
            for values in (np.cos, np.sin):
                if single and values is np.sin:
                    continue
                table[0, at : at + chunk, column] = weight * values(unit * ((m * point) % lon))
                wave[0, column] = m
                column += 1

    real_class(0, 0)
    real_class(half, LANES)
    weight = math.sqrt(2.0 / (chunk * RADIX))
    for k in range(1, half):
        for q in range(chunk):
            m = RADIX * q + k
            c = weight * np.cos(unit * ((m * point) % lon))
            s = weight * np.sin(unit * ((m * point) % lon))
            table[k, :chunk, q], table[k, LANES : LANES + chunk, q] = c, s
            table[k, :chunk, LANES + q], table[k, LANES : LANES + chunk, LANES + q] = -s, c
            wave[k, q] = wave[k, LANES + q] = min(m, lon - m)
    high = table.astype(np.float32).astype(ml_dtypes.bfloat16)
    low = (table - high.astype(np.float64)).astype(np.float32).astype(ml_dtypes.bfloat16)
    return high, low, wave.astype(np.float32)


def split_radix(c):
    s = [c[j] + c[j + 6] for j in range(6)]
    d = [c[j] - c[j + 6] for j in range(6)]
    t = [s[j] + s[j + 3] for j in range(3)]
    e = [s[j] - s[j + 3] for j in range(3)]
    t12 = t[1] + t[2]
    e12 = e[1] - e[2]
    y0 = t[0] + t12
    y4 = (t[0] - 0.5 * t12, HALF_ROOT3 * (t[2] - t[1]))
    y6 = e[0] - e12
    y2 = (e[0] + 0.5 * e12, -HALF_ROOT3 * (e[1] + e[2]))
    p, q = d[1] - d[5], d[2] - d[4]
    r, w = d[1] + d[5], d[2] + d[4]
    y3 = (d[0] - q, d[3] - r)
    u, v = d[0] + 0.5 * q, -0.5 * r - d[3]
    sp, sw = HALF_ROOT3 * p, HALF_ROOT3 * w
    y1 = (u + sp, v - sw)
    y5 = (u - sp, v + sw)
    return [(y0, y6), y1, y2, y3, y4, y5]


def join_radix(z):
    (z0, z6), (r1, i1), (r2, i2), (r3, i3), (r4, i4), (r5, i5) = z
    hp, sp = z0 - 0.5 * r4, HALF_ROOT3 * i4
    p = [z0 + r4, hp - sp, hp + sp]
    hq, sq = z6 - 0.5 * r2, HALF_ROOT3 * i2
    q = [z6 + r2, -hq - sq, hq - sq]
    e = [p[j] + q[j] for j in range(3)] + [p[j] - q[j] for j in range(3)]
    a, b, c, d = r1 + r5, HALF_ROOT3 * (r1 - r5), i1 + i5, HALF_ROOT3 * (i1 - i5)
    g = r3 - 0.5 * a
    f = -0.5 * c - i3
    o = [a + r3, b + f, -g - d, i3 - c, g - d, f - b]
    return [e[j] + o[j] for j in range(6)] + [e[j] - o[j] for j in range(6)]


def rolled(x, left):
    shift = (-left) % LANES
    return x if shift == 0 else pltpu.roll(x, shift, 1)


def lane_index(rows=8):
    return lax.broadcasted_iota(jnp.int32, (rows, LANES), 1)


def two_parts(x):
    high = x.astype(bf16)
    return high, (x - high.astype(f32)).astype(bf16)


def filter_kernel(
    lon, lat_total, winds, thick, cutoff, high_hbm, low_hbm, wave, out, column, trig,
    x, high, low, yh, yl, z, cut, sem,
):
    levels, rows = x.shape[1:3]
    tiles = out.shape[2]
    groups = rows // 8
    chunk = lon // RADIX
    gap = LANES - chunk
    tail = lon - (tiles - 1) * LANES
    half = RADIX // 2
    span = levels * rows
    copies = [
        pltpu.make_async_copy(winds.at[0], x.at[0], sem.at[0]),
        pltpu.make_async_copy(winds.at[1], x.at[1], sem.at[1]),
        pltpu.make_async_copy(thick, x.at[2], sem.at[2]),
    ]
    for copy in copies:
        copy.start()
    tables = [
        pltpu.make_async_copy(high_hbm, high, sem.at[3]),
        pltpu.make_async_copy(low_hbm, low, sem.at[4]),
    ]

    least = cutoff[0]
    for r in range(1, rows):
        least = jnp.minimum(least, cutoff[r])
    filtering = least < lon // 2

    @pl.when(filtering)
    def _():
        for copy in tables:
            copy.start()

    first = lax.axis_index("lat") * rows
    index = (first + lax.broadcasted_iota(jnp.int32, (rows, LANES), 0)).astype(f32)
    centre = (index + 0.5) * (math.pi / lat_total) - 0.5 * math.pi
    trig[0] = jnp.sin(centre)
    trig[1] = jnp.cos(centre)
    trig[2] = jnp.sin(index * (math.pi / lat_total))
    trig[3] = jnp.sin((index + 1.0) * (math.pi / lat_total))
    lane, lane16 = lane_index(), lane_index(16)

    def tiles_of(f, l, at):
        got = [x[f, l, at, pl.ds(LANES * j, LANES)] for j in range(tiles - 1)]
        last = x[f, l, at, pl.ds(LANES * (tiles - 1), tail)]
        if tail < LANES:
            last = jnp.concatenate([last, jnp.zeros((at.size, LANES - tail), f32)], axis=1)
        return got + [last]

    @pl.when(jnp.logical_not(filtering))
    def _():
        for copy in copies:
            copy.wait()

        def keep(n, _):
            f, l = n // levels, n % levels
            for g in range(groups):
                v = tiles_of(f, l, pl.ds(8 * g, 8))
                v[-1] = jnp.where(lane < tail, v[-1], rolled(v[0], LANES - tail))
                for j in range(tiles):
                    out[f, l, j, pl.ds(8 + 8 * g, 8), :] = v[j]
            return 0

        lax.fori_loop(0, 3 * levels, keep, 0)

    @pl.when(filtering)
    def _():
        for r in range(rows):
            cut[pl.ds(r, 1), :] = jnp.full((1, LANES), cutoff[r].astype(f32), f32)

        for f in range(3):
            copies[f].wait()

            def forward(l, _, f=f):
                for g in range(rows // 16):
                    v = tiles_of(f, l, pl.ds(16 * g, 16))
                    at = pl.ds(pl.multiple_of(f * span + l * rows + 16 * g, 16), 16)
                    c = []
                    for j in range(RADIX):
                        turn = gap * j
                        here = jnp.where(lane16 < LANES - turn, v[j], v[j - 1]) if turn else v[j]
                        c.append(rolled(here, -turn))
                    c[-1] = jnp.where(lane16 < chunk, c[-1], 0.0)
                    for t, pair in enumerate(split_radix(c)):
                        for part in range(2):
                            hi, lo = two_parts(pair[part])
                            yh[t, at, LANES * part : LANES * (part + 1)] = hi
                            yl[t, at, LANES * part : LANES * (part + 1)] = lo
                return 0

            lax.fori_loop(0, levels, forward, 0)
        for copy in tables:
            copy.wait()

        def product(a, b, side):
            return lax.dot_general(a, b, (((1,), (side,)), ((), ())), preferred_element_type=f32)

        def three(ah, al, t, side):
            th, tl = high[t], low[t]
            return product(ah, th, side) + (product(al, th, side) + product(ah, tl, side))

        kept = jnp.concatenate([cut[...], cut[...]], axis=1)
        for t in range(half):
            coeffs = three(yh[t], yl[t], t, 0).reshape(3 * levels, rows, WIDE)
            coeffs = jnp.where(wave[t : t + 1][None] <= kept[None], coeffs, 0.0)
            ch, cl = two_parts(coeffs.reshape(3 * span, WIDE))
            z[t] = three(ch, cl, t, 1)

        def backward(n, _):
            f, l = n // levels, n % levels
            for g in range(groups):
                at = pl.ds(pl.multiple_of(n * rows + 8 * g, 8), 8)
                c = join_radix([(z[t, at, :LANES], z[t, at, LANES:]) for t in range(half)])
                c = [rolled(c[j % RADIX], gap * j) for j in range(RADIX + 1)]
                for j in range(tiles):
                    out[f, l, j, pl.ds(8 + 8 * g, 8), :] = jnp.where(
                        lane < LANES - gap * (j + 1), c[j], c[j + 1]
                    )
            return 0

        lax.fori_loop(0, 3 * levels, backward, 0)

    for j in range(tiles):
        at = pl.ds(8, rows)
        total = out[2, 0, j, at, :]
        for l in range(1, levels):
            total = total + out[2, l, j, at, :]
        column[j] = total


def filtered_fields(winds, thick, cutoff, lat_total):
    levels, rows, lon = thick.shape
    tiles = -(-lon // LANES)
    assert lon % RADIX == 0 and lon // RADIX <= LANES and tiles == RADIX and rows % 16 == 0
    high, low, wave = filter_tables(lon)
    half = RADIX // 2
    count = 3 * levels * rows
    shape = jax.ShapeDtypeStruct
    vmem = pl.BlockSpec(memory_space=pltpu.VMEM)
    hbm = pl.BlockSpec(memory_space=pltpu.HBM)
    return pl.pallas_call(
        functools.partial(filter_kernel, lon, lat_total),
        out_shape=[
            shape((3, levels, tiles, rows + 16, LANES), f32),
            shape((tiles, rows, LANES), f32),
            shape((4, rows, LANES), f32),
        ],
        in_specs=[hbm, hbm, pl.BlockSpec(memory_space=pltpu.SMEM), hbm, hbm, vmem],
        out_specs=[vmem, vmem, vmem],
        scratch_shapes=[
            pltpu.VMEM((3, levels, rows, lon), f32),
            pltpu.VMEM((half, WIDE, WIDE), bf16),
            pltpu.VMEM((half, WIDE, WIDE), bf16),
            pltpu.VMEM((half, count, WIDE), bf16),
            pltpu.VMEM((half, count, WIDE), bf16),
            pltpu.VMEM((half, count, WIDE), f32),
            pltpu.VMEM((rows, LANES), f32),
            pltpu.SemaphoreType.DMA((5,)),
        ],
        compiler_params=pltpu.CompilerParams(vmem_limit_bytes=40 << 20),
        name="filter",
    )(winds, thick, cutoff, jnp.asarray(high), jnp.asarray(low), jnp.asarray(wave))


def pack_kernel(fields, below, first, last):
    levels, tiles = fields.shape[1:3]
    rows = below.shape[1]
    each = 2 * levels + 1
    for j in range(tiles):
        for out, at in ((first, 0), (last, rows - 1)):
            for l in range(levels):
                out[pl.ds(each * j + l, 1), :] = fields[1, l, j, pl.ds(8 + at, 1), :]
                out[pl.ds(each * j + levels + l, 1), :] = fields[2, l, j, pl.ds(8 + at, 1), :]
            out[pl.ds(each * j + 2 * levels, 1), :] = below[j, pl.ds(at, 1), :]


def packed_edges(fields, below):
    levels, tiles = fields.shape[1:3]
    vmem = pl.BlockSpec(memory_space=pltpu.VMEM)
    edge = jax.ShapeDtypeStruct((tiles * (2 * levels + 1), LANES), f32)
    return pl.pallas_call(
        pack_kernel, out_shape=[edge, edge], in_specs=[vmem, vmem], out_specs=[vmem, vmem], name="pack"
    )(fields, below)


def step_kernel(
    lon, lat_count, lev_count, fields, below, before, after, trig, winds_hbm, thick_hbm, winds, thick, sem
):
    levels, tiles = fields.shape[1:3]
    rows = below.shape[1]
    groups = rows // 8
    each = 2 * levels + 1
    tail = lon - (tiles - 1) * LANES
    lane = lane_index()
    row = lax.broadcasted_iota(jnp.int32, (8, LANES), 0)
    place = lax.axis_index("lat")
    has_before = jnp.where(place > 0, 1.0, 0.0)
    has_after = jnp.where(place < lat_count - 1, 1.0, 0.0)

    def east(v):
        r = [rolled(a, 1) for a in v]
        return [jnp.where(lane < LANES - 1, r[j], r[j + 1]) for j in range(tiles - 1)] + [r[-1]]

    def west(v):
        r = [rolled(a, -1) for a in v]
        wrapped = [rolled(v[-1], tail - 1)] + r[:-1]
        return [jnp.where(lane > 0, r[j], wrapped[j]) for j in range(tiles)]

    def halo(ref, j, slot, present):
        return jnp.broadcast_to(ref[pl.ds(each * j + slot, 1), :], (8, LANES)) * present

    def beside(load, g, j, slot, toward):
        if toward < 0:
            value = load(8 * g - 1)
            return jnp.where(row > 0, value, halo(before, j, slot, has_before)) if g == 0 else value
        value = load(8 * g + 1)
        return jnp.where(row < 7, value, halo(after, j, slot, has_after)) if g == groups - 1 else value

    copies = []
    for g in range(groups):
        at = pl.ds(8 * g, 8)
        sine, cosine = trig[0, at, :], trig[1, at, :]
        south, north = trig[2, at, :], trig[3, at, :]
        sum_x, sum_y = None, None
        s = [below[j, at, :] for j in range(tiles)]
        se, sw = east(s), west(s)
        sum_x = [a - b for a, b in zip(se, sw)]
        sum_y = []
        for j in range(tiles):
            if g == 0:
                up = jnp.where(row > 0, pltpu.roll(s[j], 1, 0), halo(before, j, 2 * levels, has_before))
            else:
                up = below[j, pl.ds(8 * g - 1, 8), :]
            if g == groups - 1:
                down = jnp.where(row < 7, pltpu.roll(s[j], 7, 0), halo(after, j, 2 * levels, has_after))
            else:
                down = below[j, pl.ds(8 * g + 1, 8), :]
            sum_y.append(down - up)
        for l in reversed(range(levels)):
            u, v, h = ([fields[f, l, j, pl.ds(8 + 8 * g, 8), :] for j in range(tiles)] for f in range(3))
            he, hw, ue = east(h), west(h), east(u)
            flux = [(h[j] + he[j]) * (u[j] + ue[j]) for j in range(tiles)]
            flux_west = west(flux)
            for j in range(tiles):

                def rows_of(f, j=j, l=l):
                    return lambda at: fields[f, l, j, pl.ds(8 + at, 8), :]

                v_up, v_down = (beside(rows_of(1), g, j, l, to) for to in (-1, 1))
                h_up, h_down = (beside(rows_of(2), g, j, levels + l, to) for to in (-1, 1))
                merid = (h[j] + h_down) * (v[j] + v_down) * north - (h_up + h[j]) * (v_up + v[j]) * south
                dx, dy = he[j] - hw[j], h_down - h_up
                new_h = h[j] - (0.25 * time_step) * (flux[j] - flux_west[j] + merid)
                new_u = u[j] - time_step * (0.5 * (sum_x[j] + 0.5 * dx) - coriolis * sine * v[j])
                new_v = v[j] - time_step * (0.5 * cosine * (sum_y[j] + 0.5 * dy) + coriolis * sine * u[j])
                sum_x[j] = sum_x[j] + dx
                sum_y[j] = sum_y[j] + dy
                wide = LANES if j < tiles - 1 else tail
                here = pl.ds(LANES * j, wide)
                thick[l, at, here] = new_h[:, :wide]
                winds[0, l, at, here] = new_u[:, :wide]
                winds[1, l, at, here] = new_v[:, :wide]
        copies += [
            pltpu.make_async_copy(winds.at[:, :, at], winds_hbm.at[:, :, at], sem.at[2 * g]),
            pltpu.make_async_copy(thick.at[:, at], thick_hbm.at[:, at], sem.at[2 * g + 1]),
        ]
        copies[-2].start()
        copies[-1].start()
    for copy in copies:
        copy.wait()


def stepped(fields, below, before, after, trig, lon, lat_count, lev_count):
    levels, tiles = fields.shape[1:3]
    rows = below.shape[1]
    shape = jax.ShapeDtypeStruct
    vmem = pl.BlockSpec(memory_space=pltpu.VMEM)
    hbm = pl.BlockSpec(memory_space=pltpu.HBM)
    return pl.pallas_call(
        functools.partial(step_kernel, lon, lat_count, lev_count),
        out_shape=[shape((2, levels, rows, lon), f32), shape((levels, rows, lon), f32)],
        in_specs=[vmem] * 5,
        out_specs=[hbm, hbm],
        scratch_shapes=[
            pltpu.VMEM((2, levels, rows, lon), f32),
            pltpu.VMEM((levels, rows, lon), f32),
            pltpu.SemaphoreType.DMA((2 * (rows // 8),)),
        ],
        compiler_params=pltpu.CompilerParams(vmem_limit_bytes=40 << 20),
        name="step",
    )(fields, below, before, after, trig)


def per_device(winds, thick, cutoff):
    lat_count, lev_count = lax.axis_size("lat"), lax.axis_size("lev")
    levels, rows, lon = thick.shape
    fields, column, trig = filtered_fields(winds, thick, cutoff, rows * lat_count)
    below = jnp.zeros_like(column)
    place = lax.axis_index("lev")
    for hop in range(1, lev_count):
        got = lax.ppermute(column, "lev", [(i, (i - hop) % lev_count) for i in range(lev_count)])
        below = below + jnp.where(place + hop < lev_count, got, 0.0)
    first, last = packed_edges(fields, below)
    up = [(i, (i + 1) % lat_count) for i in range(lat_count)]
    before = lax.ppermute(last, "lat", up)
    after = lax.ppermute(first, "lat", [(j, i) for i, j in up])
    return tuple(stepped(fields, below, before, after, trig, lon, lat_count, lev_count))


def solution(mesh):
    return jax.shard_map(
        per_device,
        mesh=mesh,
        in_specs=(P(None, "lev", "lat", None), P("lev", "lat", None), P("lat")),
        out_specs=(P(None, "lev", "lat", None), P("lev", "lat", None)),
        check_vma=False,
    )
```

profile of v0, /device:TPU:0, one launch (start us, length us, event | category | flops | bytes accessed | tf_op | source)
XLA Modules:
  0.0 34.7 jit_solution(1249186691254344997)
XLA Ops:
  0.6 0.0 copy-start.3
  0.6 1.4 %copy-done.3 = f32[2,4,32,1440]{3,2,1,0:T(8,128)S(1)} copy-done((f32[2,4,32,1440]{3,2,1,0:T(8,128)S(1)}, f32[2,4,32,1440]{3,2,1,0:T(8,128)}, u32[]{:S(2)}) %copy-start.3) | copy-done | bytes 1474584
  2.0 0.0 copy-start.4
  2.0 1.1 %copy-done.4 = f32[4,32,1440]{2,1,0:T(8,128)S(1)} copy-done((f32[4,32,1440]{2,1,0:T(8,128)S(1)}, f32[4,32,1440]{2,1,0:T(8,128)}, u32[]{:S(2)}) %copy-start.4) | copy-done | bytes 737304
  3.2 0.0 copy-start.5
  3.2 1.1 %copy-done.5 = bf16[6,256,256]{2,1,0:T(8,128)(2,1)S(1)} copy-done((bf16[6,256,256]{2,1,0:T(8,128)(2,1)S(1)}, bf16[6,256,256]{2,1,0:T(8,128)(2,1)}, u32[]{:S(2)}) %copy-start.5) | copy-done | bytes 786456
  4.3 0.0 copy-start.6
  4.3 1.1 %copy-done.6 = bf16[6,256,256]{2,1,0:T(8,128)(2,1)S(1)} copy-done((bf16[6,256,256]{2,1,0:T(8,128)(2,1)S(1)}, bf16[6,256,256]{2,1,0:T(8,128)(2,1)}, u32[]{:S(2)}) %copy-start.6) | copy-done | bytes 786456
  5.4 0.0 copy-start.9
  5.4 0.7 %copy-done.9 = f32[6,256]{1,0:T(8,128)S(1)} copy-done((f32[6,256]{1,0:T(8,128)S(1)}, f32[6,256]{1,0:T(8,128)}, u32[]{:S(2)}) %copy-start.9) | copy-done | bytes 6168
  6.1 0.0 copy-start.10
  6.1 0.7 %copy-done.10 = s32[32]{0:T(128)S(1)} copy-done((s32[32]{0:T(128)S(1)}, s32[32]{0:T(128)}, u32[]{:S(2)}) %copy-start.10) | copy-done | bytes 152
  6.8 6.7 %filter.1 = (f32[3,4,12,48,128]{4,3,2,1,0:T(8,128)S(1)}, f32[12,32,128]{2,1,0:T(8,128)S(1)}, f32[4,32,128]{2,1,0:T(8,128)S(1)}) custom-call(f32[2,4,32,1440]{3,2,1,0:T(8,128)S(1)} %copy-done.3, f32[4,32,1440]{2,1,0:T(8,128)S(1)} %copy-done.4, s32[32]{0:T(128)S(1)} %copy-done.10, bf16[6,256,256]{2,1,0:T(8,128)(2,1)S(1)} %copy-done.6, ...), custom_call_target="tpu_custom_call" | custom-call | tf_op jit(solution)/shard_map/filter/pallas_call | solution.py:252
  13.5 0.0 copy-start
  13.5 1.7 %copy-done = f32[3,4,12,48,128]{4,3,2,1,0:T(8,128)} copy-done((f32[3,4,12,48,128]{4,3,2,1,0:T(8,128)}, f32[3,4,12,48,128]{4,3,2,1,0:T(8,128)S(1)}, u32[]{:S(2)}) %copy-start) | copy-done | bytes 3538968
  15.2 0.0 copy-start.7
  15.2 0.6 %copy-done.7 = f32[4,32,128]{2,1,0:T(8,128)} copy-done((f32[4,32,128]{2,1,0:T(8,128)}, f32[4,32,128]{2,1,0:T(8,128)S(1)}, u32[]{:S(2)}) %copy-start.7) | copy-done | bytes 65560
  15.9 0.5 %collective-permute-start = (f32[12,32,128]{2,1,0:T(8,128)S(1)}, f32[12,32,128]{2,1,0:T(8,128)S(1)}, u32[]{:S(2)}, u32[]{:S(2)}) collective-permute-start(f32[12,32,128]{2,1,0:T(8,128)S(1)} %get-tuple-element.8), channel_id=1, source_target_pairs={{0,1},{1,0},{2,3},{3,2},{4,5},{5,4},{6,7},{7,6},{8,9},{9,8},{10,11... | collective-permute-start | bytes 589832 | tf_op jit(solution)/shard_map/ppermute | solution.py:412
  16.3 1.1 %collective-permute-done = f32[12,32,128]{2,1,0:T(8,128)S(1)} collective-permute-done((f32[12,32,128]{2,1,0:T(8,128)S(1)}, f32[12,32,128]{2,1,0:T(8,128)S(1)}, u32[]{:S(2)}, u32[]{:S(2)}) %collective-permute-start) | collective-permute-done | bytes 196640 | tf_op jit(solution)/shard_map/ppermute | solution.py:412
  17.4 0.7 %broadcast_select_fusion.below = f32[12,32,128]{2,1,0:T(8,128)} fusion(f32[12,32,128]{2,1,0:T(8,128)S(1)} %collective-permute-done, pred[]{:T(512)S(6)} %lt.3), kind=kLoop, calls=%fused_computation | loop fusion | flops 49152 | bytes 393217 | tf_op jit(solution)/shard_map/jit(_where)/select_n | solution.py:413
  18.1 0.0 copy-start.1
  18.1 2.9 %pack.1 = (f32[108,128]{1,0:T(8,128)}, f32[108,128]{1,0:T(8,128)}) custom-call(f32[3,4,12,48,128]{4,3,2,1,0:T(8,128)} %copy-done, f32[12,32,128]{2,1,0:T(8,128)} %broadcast_select_fusion.below), custom_call_target="tpu_custom_call" | custom-call | tf_op jit(solution)/shard_map/pack/pallas_call | solution.py:292
  21.0 2.9 %collective-permute-start.1 = (f32[108,128]{1,0:T(8,128)}, f32[108,128]{1,0:T(8,128)S(1)}, u32[]{:S(2)}, u32[]{:S(2)}) collective-permute-start(f32[108,128]{1,0:T(8,128)} %get-tuple-element.9), channel_id=1, source_target_pairs={{0,2},{2,4},{4,6},{6,8},{8,10},{10,12},{12,14},{14,16},{16,18},{18... | collective-permute-start | bytes 165896 | tf_op jit(solution)/shard_map/ppermute | solution.py:416
  23.8 4.0 %collective-permute-start.2 = (f32[108,128]{1,0:T(8,128)}, f32[108,128]{1,0:T(8,128)S(1)}, u32[]{:S(2)}, u32[]{:S(2)}) collective-permute-start(f32[108,128]{1,0:T(8,128)} %get-tuple-element.10), channel_id=1, source_target_pairs={{2,0},{4,2},{6,4},{8,6},{10,8},{12,10},{14,12},{16,14},{18,16},{20... | collective-permute-start | bytes 165896 | tf_op jit(solution)/shard_map/ppermute | solution.py:417
  27.8 2.4 %collective-permute-done.1.before = f32[108,128]{1,0:T(8,128)S(1)} collective-permute-done((f32[108,128]{1,0:T(8,128)}, f32[108,128]{1,0:T(8,128)S(1)}, u32[]{:S(2)}, u32[]{:S(2)}) %collective-permute-start.1) | collective-permute-done | bytes 55328 | tf_op jit(solution)/shard_map/ppermute | solution.py:416
  30.2 0.0 collective-permute-done.2.after
  30.2 0.0 copy-done.1
  30.2 0.0 copy-start.2
  30.2 0.9 %copy-done.2 = f32[12,32,128]{2,1,0:T(8,128)S(1)} copy-done((f32[12,32,128]{2,1,0:T(8,128)S(1)}, f32[12,32,128]{2,1,0:T(8,128)}, u32[]{:S(2)}) %copy-start.2) | copy-done | bytes 196632
  31.2 0.0 copy-start.8
  31.2 0.8 %copy-done.8 = f32[4,32,128]{2,1,0:T(8,128)S(1)} copy-done((f32[4,32,128]{2,1,0:T(8,128)S(1)}, f32[4,32,128]{2,1,0:T(8,128)}, u32[]{:S(2)}) %copy-start.8) | copy-done | bytes 65560
  32.0 2.7 %step.1 = (f32[2,4,32,1440]{3,2,1,0:T(8,128)}, f32[4,32,1440]{2,1,0:T(8,128)}) custom-call(f32[3,4,12,48,128]{4,3,2,1,0:T(8,128)S(1)} %copy-done.1, f32[12,32,128]{2,1,0:T(8,128)S(1)} %copy-done.2, f32[108,128]{1,0:T(8,128)S(1)} %collective-permute-done.1.before, f32[108,128]{1,0:T(8,128)S(1)} %collective-permute-done.2.after, f32[4,32,128]{2,1,0:T(8,128)S(1)} %copy-done.8), custom_call_target="tpu_custom_call" | custom-call | tf_op jit(solution)/shard_map/step/pallas_call | solution.py:390
Async XLA Ops:
  0.6 1.4 %copy-start.3 = (f32[2,4,32,1440]{3,2,1,0:T(8,128)S(1)}, f32[2,4,32,1440]{3,2,1,0:T(8,128)}, u32[]{:S(2)}) copy-start(f32[2,4,32,1440]{3,2,1,0:T(8,128)} %winds.1) | copy-start | bytes 4423684
  2.0 1.1 %copy-start.4 = (f32[4,32,1440]{2,1,0:T(8,128)S(1)}, f32[4,32,1440]{2,1,0:T(8,128)}, u32[]{:S(2)}) copy-start(f32[4,32,1440]{2,1,0:T(8,128)} %thick.1) | copy-start | bytes 2211844
  3.2 1.1 %copy-start.5 = (bf16[6,256,256]{2,1,0:T(8,128)(2,1)S(1)}, bf16[6,256,256]{2,1,0:T(8,128)(2,1)}, u32[]{:S(2)}) copy-start(bf16[6,256,256]{2,1,0:T(8,128)(2,1)} %constant.17.clone.low_hbm) | copy-start | bytes 2359300
  4.3 1.1 %copy-start.6 = (bf16[6,256,256]{2,1,0:T(8,128)(2,1)S(1)}, bf16[6,256,256]{2,1,0:T(8,128)(2,1)}, u32[]{:S(2)}) copy-start(bf16[6,256,256]{2,1,0:T(8,128)(2,1)} %constant.16.clone.high_hbm) | copy-start | bytes 2359300
  5.4 0.7 %copy-start.9 = (f32[6,256]{1,0:T(8,128)S(1)}, f32[6,256]{1,0:T(8,128)}, u32[]{:S(2)}) copy-start(f32[6,256]{1,0:T(8,128)} %constant.18.clone.wave) | copy-start | bytes 18436
  6.1 0.7 %copy-start.10 = (s32[32]{0:T(128)S(1)}, s32[32]{0:T(128)}, u32[]{:S(2)}) copy-start(s32[32]{0:T(128)} %cutoff.1) | copy-start | bytes 388
  13.5 1.7 %copy-start = (f32[3,4,12,48,128]{4,3,2,1,0:T(8,128)}, f32[3,4,12,48,128]{4,3,2,1,0:T(8,128)S(1)}, u32[]{:S(2)}) copy-start(f32[3,4,12,48,128]{4,3,2,1,0:T(8,128)S(1)} %get-tuple-element.7.fields) | copy-start | bytes 10616836
  15.2 0.6 %copy-start.7 = (f32[4,32,128]{2,1,0:T(8,128)}, f32[4,32,128]{2,1,0:T(8,128)S(1)}, u32[]{:S(2)}) copy-start(f32[4,32,128]{2,1,0:T(8,128)S(1)} %get-tuple-element.11.trig) | copy-start | bytes 196612
  15.9 1.5 %collective-permute-start = (f32[12,32,128]{2,1,0:T(8,128)S(1)}, f32[12,32,128]{2,1,0:T(8,128)S(1)}, u32[]{:S(2)}, u32[]{:S(2)}) collective-permute-start(f32[12,32,128]{2,1,0:T(8,128)S(1)} %get-tuple-element.8), channel_id=1, source_target_pairs={{0,1},{1,0},{2,3},{3,2},{4,5},{5,4},{6,7},{7,6},{8,9},{9,8},{10,11... | collective-permute-start | bytes 589832 | tf_op jit(solution)/shard_map/ppermute | solution.py:412
  18.1 12.2 %copy-start.1 = (f32[3,4,12,48,128]{4,3,2,1,0:T(8,128)S(1)}, f32[3,4,12,48,128]{4,3,2,1,0:T(8,128)}, u32[]{:S(2)}) copy-start(f32[3,4,12,48,128]{4,3,2,1,0:T(8,128)} %copy-done) | copy-start | bytes 10616836
  21.0 9.3 %collective-permute-start.1 = (f32[108,128]{1,0:T(8,128)}, f32[108,128]{1,0:T(8,128)S(1)}, u32[]{:S(2)}, u32[]{:S(2)}) collective-permute-start(f32[108,128]{1,0:T(8,128)} %get-tuple-element.9), channel_id=1, source_target_pairs={{0,2},{2,4},{4,6},{6,8},{8,10},{10,12},{12,14},{14,16},{16,18},{18... | collective-permute-start | bytes 165896 | tf_op jit(solution)/shard_map/ppermute | solution.py:416
  23.8 6.4 %collective-permute-start.2 = (f32[108,128]{1,0:T(8,128)}, f32[108,128]{1,0:T(8,128)S(1)}, u32[]{:S(2)}, u32[]{:S(2)}) collective-permute-start(f32[108,128]{1,0:T(8,128)} %get-tuple-element.10), channel_id=1, source_target_pairs={{2,0},{4,2},{6,4},{8,6},{10,8},{12,10},{14,12},{16,14},{18,16},{20... | collective-permute-start | bytes 165896 | tf_op jit(solution)/shard_map/ppermute | solution.py:417
  30.2 0.9 %copy-start.2 = (f32[12,32,128]{2,1,0:T(8,128)S(1)}, f32[12,32,128]{2,1,0:T(8,128)}, u32[]{:S(2)}) copy-start(f32[12,32,128]{2,1,0:T(8,128)} %broadcast_select_fusion.below) | copy-start | bytes 589828
  31.2 0.8 %copy-start.8 = (f32[4,32,128]{2,1,0:T(8,128)S(1)}, f32[4,32,128]{2,1,0:T(8,128)}, u32[]{:S(2)}) copy-start(f32[4,32,128]{2,1,0:T(8,128)} %copy-done.7) | copy-start | bytes 196612
where the time goes:
time: 35.1 us; the launch traced here: 34.7 us
  Pallas kernels  12.3 us (35%)
  local copies, waits for them, and re-layouts  10.3 us (29%)
  starting transfers between devices  7.31 us (21%)
  waiting for transfers between devices  3.5 us (10%)
  other arithmetic  0.69 us (2%)
  between operations  0.67 us (2%)
    unnamed x22, local copies, waits for them, and re-layouts  10.3 us
    pallas_call x1, Pallas kernels, filtered_fields(): pl.pallas_call(functools.partial(filter_kernel, lon, lat_total), out_shap...  6.69 us
    ppermute x1, starting transfers between devices, per_device(): after = lax.ppermute(first, 'lat', [(j, i) for i, j in up])  4 us
    pallas_call x1, Pallas kernels, packed_edges(): pl.pallas_call(pack_kernel, out_shape=[edge, edge], in_specs=[vmem, vmem]...  2.87 us
    ppermute x1, starting transfers between devices, per_device(): before = lax.ppermute(last, 'lat', up)  2.86 us
    pallas_call x1, Pallas kernels, stepped(): pl.pallas_call(functools.partial(step_kernel, lon, lat_count, lev_count),...  2.73 us
    ppermute x1, waiting for transfers between devices, per_device(): before = lax.ppermute(last, 'lat', up)  2.42 us
    ppermute x1, waiting for transfers between devices, per_device(): lax.ppermute(column, 'lev', [(i, (i - hop) % lev_count) for i in range(le...  1.07 us
  transfers between devices with their start and end apart: 3, of which 2 were waited for; matrix products, arithmetic and copies ran while one was open for 0% of the time, Pallas kernels for 0%

commit v1 on v0

v1 whole, which is shorter than its diff:
```python
import functools
import math

import jax
import jax.numpy as jnp
import ml_dtypes
import numpy as np
from jax import lax
from jax.experimental import pallas as pl
from jax.experimental.pallas import tpu as pltpu
from jax.sharding import PartitionSpec as P

time_step = 0.2
coriolis = 1.0
RADIX = 12
LANES = 128
WIDE = 2 * LANES
HALF_ROOT3 = math.sqrt(3.0) / 2.0
f32 = jnp.float32
bf16 = jnp.bfloat16


def waves(lon, t):
    at = lax.broadcasted_iota(jnp.int32, (1, WIDE), 1)
    second = at >= LANES
    q = jnp.where(second, at - LANES, at)
    if t == 0:
        m = jnp.where(second, RADIX * (q >> 1) + RADIX // 2, RADIX * ((q + 1) >> 1))
    else:
        m = RADIX * q + t
        m = jnp.minimum(m, lon - m)
    return m.astype(f32)


def filter_tables(lon):
    chunk = lon // RADIX
    half = RADIX // 2
    table = np.zeros((half, WIDE, WIDE), np.float64)
    point = np.arange(chunk, dtype=np.float64)
    unit = 2.0 * math.pi / lon

    def real_class(residue, at):
        column = at
        for m in range(residue, lon // 2 + 1, RADIX):
            single = m == 0 or 2 * m == lon
            weight = math.sqrt((1.0 if single else 2.0) / lon)
            for values in (np.cos, np.sin)[: 1 if single else 2]:
                table[0, at : at + chunk, column] = weight * values(unit * ((m * point) % lon))
                column += 1

    real_class(0, 0)
    real_class(half, LANES)
    weight = math.sqrt(2.0 / lon)
    for k in range(1, half):
        for q in range(chunk):
            m = RADIX * q + k
            c = weight * np.cos(unit * ((m * point) % lon))
            s = weight * np.sin(unit * ((m * point) % lon))
            table[k, :chunk, q], table[k, LANES : LANES + chunk, q] = c, s
            table[k, :chunk, LANES + q], table[k, LANES : LANES + chunk, LANES + q] = -s, c
    high = table.astype(np.float32).astype(ml_dtypes.bfloat16)
    low = (table - high.astype(np.float64)).astype(np.float32).astype(ml_dtypes.bfloat16)
    return np.stack([high, low], axis=1)


def split_radix(c):
    s = [c[j] + c[j + 6] for j in range(6)]
    d = [c[j] - c[j + 6] for j in range(6)]
    t = [s[j] + s[j + 3] for j in range(3)]
    e = [s[j] - s[j + 3] for j in range(3)]
    t12 = t[1] + t[2]
    e12 = e[1] - e[2]
    y0 = t[0] + t12
    y4 = (t[0] - 0.5 * t12, HALF_ROOT3 * (t[2] - t[1]))
    y6 = e[0] - e12
    y2 = (e[0] + 0.5 * e12, -HALF_ROOT3 * (e[1] + e[2]))
    p, q = d[1] - d[5], d[2] - d[4]
    r, w = d[1] + d[5], d[2] + d[4]
    y3 = (d[0] - q, d[3] - r)
    u, v = d[0] + 0.5 * q, -0.5 * r - d[3]
    sp, sw = HALF_ROOT3 * p, HALF_ROOT3 * w
    y1 = (u + sp, v - sw)
    y5 = (u - sp, v + sw)
    return [(y0, y6), y1, y2, y3, y4, y5]


def join_radix(z):
    (z0, z6), (r1, i1), (r2, i2), (r3, i3), (r4, i4), (r5, i5) = z
    hp, sp = z0 - 0.5 * r4, HALF_ROOT3 * i4
    p = [z0 + r4, hp - sp, hp + sp]
    hq, sq = z6 - 0.5 * r2, HALF_ROOT3 * i2
    q = [z6 + r2, -hq - sq, hq - sq]
    e = [p[j] + q[j] for j in range(3)] + [p[j] - q[j] for j in range(3)]
    a, b, c, d = r1 + r5, HALF_ROOT3 * (r1 - r5), i1 + i5, HALF_ROOT3 * (i1 - i5)
    g = r3 - 0.5 * a
    f = -0.5 * c - i3
    o = [a + r3, b + f, -g - d, i3 - c, g - d, f - b]
    return [e[j] + o[j] for j in range(6)] + [e[j] - o[j] for j in range(6)]


def rolled(x, left):
    shift = (-left) % LANES
    return x if shift == 0 else pltpu.roll(x, shift, 1)


def lane_index(rows=8):
    return lax.broadcasted_iota(jnp.int32, (rows, LANES), 1)


def two_parts(x):
    high = x.astype(bf16)
    return high, (x - high.astype(f32)).astype(bf16)


def rows_at(start, size=8):
    return pl.ds(start, size)


def edge_kernel(lat_count, winds, thick, cutoff_hbm, sent_a, sent_b, trig, cut, v, h, cutoff, sem):
    levels, lon = v.shape[1:]
    rows = thick.shape[1]
    tiles = -(-lon // LANES)
    tail = lon - (tiles - 1) * LANES
    copies = [pltpu.make_async_copy(cutoff_hbm, cutoff, sem.at[4])]
    for side, start in enumerate((0, rows - 1)):
        copies.append(pltpu.make_async_copy(winds.at[1, :, start], v.at[side], sem.at[2 * side]))
        copies.append(pltpu.make_async_copy(thick.at[:, start], h.at[side], sem.at[2 * side + 1]))
    for copy in copies:
        copy.start()

    place = lax.axis_index("lat")
    index = (place * rows + lax.broadcasted_iota(jnp.int32, (rows, LANES), 0)).astype(f32)
    step = math.pi / (lat_count * rows)
    centre = (index + 0.5) * step - 0.5 * math.pi
    trig[0] = jnp.sin(centre)
    trig[1] = jnp.cos(centre)
    trig[2] = jnp.sin(index * step)
    trig[3] = jnp.sin((index + 1.0) * step)

    copies[0].wait()
    for r in range(rows):
        cut[pl.ds(r, 1), :] = jnp.full((1, LANES), cutoff[r].astype(f32), f32)
    for copy in copies[1:]:
        copy.wait()
    last_first = 1 - place % 2
    for out, side in ((sent_a, last_first), (sent_b, 1 - last_first)):
        out[rows_at(2 * levels * tiles), :] = jnp.full((8, LANES), cutoff[side * (rows - 1)].astype(f32), f32)
        for j in range(tiles):
            wide = LANES if j < tiles - 1 else tail
            for f, block in enumerate((v, h)):
                got = block[side, :, pl.ds(LANES * j, wide)]
                if wide < LANES:
                    got = jnp.concatenate([got, jnp.zeros((levels, LANES - wide), f32)], axis=1)
                out[pl.ds((2 * j + f) * levels, levels), :] = got


def in_hbm(x):
    return pltpu.with_memory_space_constraint(x, pltpu.HBM)


def edges(winds, thick, cutoff, lat_count):
    levels, rows, lon = thick.shape
    tiles = -(-lon // LANES)
    vmem = pl.BlockSpec(memory_space=pltpu.VMEM)
    hbm = pl.BlockSpec(memory_space=pltpu.HBM)
    edge = jax.ShapeDtypeStruct((2 * levels * tiles + 8, LANES), f32)
    return pl.pallas_call(
        functools.partial(edge_kernel, lat_count),
        out_shape=[edge, edge, pltpu.VMEM((4, rows, LANES), f32), pltpu.VMEM((rows, LANES), f32)],
        in_specs=[hbm] * 3,
        out_specs=[vmem] * 4,
        scratch_shapes=[
            pltpu.VMEM((2, levels, lon), f32),
            pltpu.VMEM((2, levels, lon), f32),
            pltpu.SMEM((rows,), jnp.int32),
            pltpu.SemaphoreType.DMA((5,)),
        ],
        compiler_params=pltpu.CompilerParams(vmem_limit_bytes=16 << 20),
        name="edges",
    )(in_hbm(winds), in_hbm(thick), in_hbm(cutoff))


def forward(v, chunk, y, at):
    gap = LANES - chunk
    lane = lane_index(v[0].shape[0])
    c = []
    for j in range(RADIX):
        turn = gap * j
        here = jnp.where(lane < LANES - turn, v[j], v[j - 1]) if turn else v[j]
        c.append(rolled(here, -turn))
    c[-1] = jnp.where(lane < chunk, c[-1], 0.0)
    for t, pair in enumerate(split_radix(c)):
        for part in range(2):
            hi, lo = two_parts(pair[part])
            y[t, at, LANES * part : LANES * (part + 1)] = hi
            y[t, at, WIDE + LANES * part : WIDE + LANES * (part + 1)] = lo


def low_pass(lon, t, y, z, tables, keep):
    def three(ah, al, side):
        th, tl = tables[t, 0], tables[t, 1]
        a = jnp.concatenate([ah, al, ah], axis=1)
        b = jnp.concatenate([th, th, tl], axis=side)
        return lax.dot_general(a, b, (((1,), (side,)), ((), ())), preferred_element_type=f32)

    coeffs = three(y[t, :, :WIDE], y[t, :, WIDE:], 0)
    count, rows = coeffs.shape[0], keep.shape[0]
    coeffs = coeffs.reshape(count // rows, rows, WIDE)
    coeffs = jnp.where(waves(lon, t)[None] <= keep[None], coeffs, 0.0).reshape(count, WIDE)
    ch, cl = two_parts(coeffs)
    z[t] = three(ch, cl, 1)


def backward(z, at, chunk):
    gap = LANES - chunk
    lane = lane_index()
    c = join_radix([(z[t, at, :LANES], z[t, at, LANES:]) for t in range(RADIX // 2)])
    c = [rolled(c[j % RADIX], gap * j) for j in range(RADIX + 1)]
    return [jnp.where(lane < LANES - gap * (j + 1), c[j], c[j + 1]) for j in range(RADIX)]


def extended(v, tail):
    return v[:-1] + [jnp.where(lane_index() < tail, v[-1], rolled(v[0], LANES - tail))]


def filter_kernel(winds, thick, tables_hbm, cut, out, column, tables, x, y, z, sem):
    levels, rows, lon = x.shape[1:]
    tiles = out.shape[2]
    chunk = lon // RADIX
    tail = lon - (tiles - 1) * LANES
    span = levels * rows
    copies = [
        pltpu.make_async_copy(winds.at[0], x.at[0], sem.at[0]),
        pltpu.make_async_copy(winds.at[1], x.at[1], sem.at[1]),
        pltpu.make_async_copy(thick, x.at[2], sem.at[2]),
    ]
    fetch = pltpu.make_async_copy(tables_hbm, tables, sem.at[3])
    for copy in copies + [fetch]:
        copy.start()
    keep = cut[...]
    filtering = jnp.min(keep) < lon // 2

    def own_tiles(f, l, at):
        got = [x[f, l, at, pl.ds(LANES * j, LANES)] for j in range(tiles - 1)]
        last = x[f, l, at, pl.ds(LANES * (tiles - 1), tail)]
        return got + [jnp.concatenate([last, jnp.zeros((at.size, LANES - tail), f32)], axis=1)]

    @pl.when(jnp.logical_not(filtering))
    def _():
        for f in range(3):
            copies[f].wait()

            def as_is(l, _, f=f):
                for g in range(rows // 8):
                    v = extended(own_tiles(f, l, rows_at(8 * g)), tail)
                    for j in range(tiles):
                        out[f, l, j, rows_at(1 + 8 * g), :] = v[j]
                return 0

            lax.fori_loop(0, levels, as_is, 0)
        fetch.wait()

    @pl.when(filtering)
    def _():
        for f in range(3):
            copies[f].wait()

            def forward_level(l, _, f=f):
                for g in range(rows // 16):
                    at = pl.ds(pl.multiple_of(f * span + l * rows + 16 * g, 16), 16)
                    forward(own_tiles(f, l, rows_at(16 * g, 16)), chunk, y, at)
                return 0

            lax.fori_loop(0, levels, forward_level, 0)
        fetch.wait()
        wide = jnp.concatenate([keep, keep], axis=1)
        for t in range(RADIX // 2):
            low_pass(lon, t, y, z, tables, wide)

        def backward_level(n, _):
            f, l = n // levels, n % levels
            for g in range(rows // 8):
                v = backward(z, rows_at(pl.multiple_of(n * rows + 8 * g, 8)), chunk)
                for j in range(tiles):
                    out[f, l, j, rows_at(1 + 8 * g), :] = v[j]
            return 0

        lax.fori_loop(0, 3 * levels, backward_level, 0)

    at = pl.ds(1, rows)
    for j in range(tiles):
        column[j, at, :] = functools.reduce(jnp.add, [out[2, l, j, at, :] for l in range(levels)])


def filtered_fields(winds, thick, cut):
    levels, rows, lon = thick.shape
    tiles = -(-lon // LANES)
    assert lon % RADIX == 0 and lon // RADIX <= LANES and tiles == RADIX
    assert rows % 16 == 0
    tables = jnp.asarray(filter_tables(lon))
    half = RADIX // 2
    count = 3 * levels * rows
    vmem = pl.BlockSpec(memory_space=pltpu.VMEM)
    hbm = pl.BlockSpec(memory_space=pltpu.HBM)
    return pl.pallas_call(
        filter_kernel,
        out_shape=[
            pltpu.VMEM((3, levels, tiles, rows + 8, LANES), f32),
            pltpu.VMEM((tiles, rows + 8, LANES), f32),
            pltpu.VMEM(tables.shape, bf16),
        ],
        in_specs=[hbm, hbm, hbm, vmem],
        out_specs=[vmem] * 3,
        scratch_shapes=[
            pltpu.VMEM((3, levels, rows, lon), f32),
            pltpu.VMEM((half, count, 2 * WIDE), bf16),
            pltpu.VMEM((half, count, WIDE), f32),
            pltpu.SemaphoreType.DMA((4,)),
        ],
        compiler_params=pltpu.CompilerParams(vmem_limit_bytes=24 << 20),
        cost_estimate=pl.CostEstimate(flops=10_000_000_000, bytes_accessed=8_000_000, transcendentals=0),
        name="filter",
    )(in_hbm(winds), in_hbm(thick), in_hbm(tables), cut)


def halo_kernel(lon, lat_count, got_a, got_b, tables, _fields, _column, out, column, y, z):
    levels, tiles, rows = out.shape[1], out.shape[2], out.shape[3] - 8
    chunk = lon // RADIX
    tail = lon - (tiles - 1) * LANES
    place = lax.axis_index("lat")
    odd = place % 2
    refs = (got_a, got_b)
    at = (jnp.where(odd == 1, 0, rows + 1), jnp.where(odd == 1, rows + 1, 0))
    keep = jnp.concatenate([ref[rows_at(2 * levels * tiles), :] for ref in refs], axis=0)

    def edge_tiles(ref):
        return [ref[rows_at(2 * levels * j, 2 * levels), :] for j in range(tiles)]

    def put(side, v):
        end = jnp.where(at[side] == 0, place == 0, place == lat_count - 1)
        for j in range(tiles):
            value = jnp.where(end, 0.0, v[j])
            for f in range(2):
                lines = [value[f * levels + l : f * levels + l + 1] for l in range(levels)]
                for l in range(levels):
                    out[1 + f, l, j, pl.ds(at[side], 1), :] = lines[l]
            column[j, pl.ds(at[side], 1), :] = functools.reduce(jnp.add, lines)

    filtering = jnp.min(keep) < lon // 2

    @pl.when(jnp.logical_not(filtering))
    def _():
        for side in range(2):
            put(side, extended(edge_tiles(refs[side]), tail))

    @pl.when(filtering)
    def _():
        both = [jnp.concatenate(pair, axis=0) for pair in zip(edge_tiles(got_a), edge_tiles(got_b))]
        forward(both, chunk, y, pl.ds(0, 16))
        wide = jnp.concatenate([keep, keep], axis=1)
        for t in range(RADIX // 2):
            low_pass(lon, t, y, z, tables, wide)
        for side in range(2):
            put(side, backward(z, rows_at(8 * side), chunk))


def with_halo(fields, column, tables, got_a, got_b, lon, lat_count):
    assert 2 * fields.shape[1] == 8
    half = RADIX // 2
    vmem = pl.BlockSpec(memory_space=pltpu.VMEM)
    return pl.pallas_call(
        functools.partial(halo_kernel, lon, lat_count),
        out_shape=[pltpu.VMEM(fields.shape, f32), pltpu.VMEM(column.shape, f32)],
        in_specs=[vmem] * 5,
        out_specs=[vmem] * 2,
        scratch_shapes=[pltpu.VMEM((half, 16, 2 * WIDE), bf16), pltpu.VMEM((half, 16, WIDE), f32)],
        input_output_aliases={3: 0, 4: 1},
        compiler_params=pltpu.CompilerParams(vmem_limit_bytes=24 << 20),
        name="halo",
    )(got_a, got_b, tables, fields, column)


def step_kernel(lon, fields, trig, *refs):
    *hops, winds_hbm, thick_hbm, winds, thick, sem = refs
    levels, tiles = fields.shape[1:3]
    rows = trig.shape[1]
    tail = lon - (tiles - 1) * LANES
    lane = lane_index()
    place = lax.axis_index("lev")
    masks = [jnp.where(place + k + 1 <= len(hops), 1.0, 0.0) for k in range(len(hops))]

    def below(j, at):
        terms = [ref[j, rows_at(at), :] * mask for ref, mask in zip(hops, masks)]
        return functools.reduce(jnp.add, terms) if terms else jnp.zeros((8, LANES), f32)

    def east(v):
        r = [rolled(a, 1) for a in v]
        return [jnp.where(lane < LANES - 1, r[j], r[j + 1]) for j in range(tiles - 1)] + [r[-1]]

    def west(v):
        r = [rolled(a, -1) for a in v]
        r_before = [rolled(v[-1], tail - 1)] + r[:-1]
        return [jnp.where(lane > 0, r[j], r_before[j]) for j in range(tiles)]

    copies = []
    for g in range(rows // 8):
        at = rows_at(8 * g)
        up, here, down = 8 * g, 8 * g + 1, 8 * g + 2
        sine, cosine = trig[0, at, :], trig[1, at, :]
        south, north = trig[2, at, :], trig[3, at, :]
        s = [below(j, here) for j in range(tiles)]
        sum_x = [a - b for a, b in zip(east(s), west(s))]
        sum_y = [below(j, down) - below(j, up) for j in range(tiles)]
        for l in reversed(range(levels)):
            u, v, h = ([fields[f, l, j, rows_at(here), :] for j in range(tiles)] for f in range(3))
            he, hw, ue = east(h), west(h), east(u)
            flux = [(h[j] + he[j]) * (u[j] + ue[j]) for j in range(tiles)]
            flux_west = west(flux)
            for j in range(tiles):
                v_up, v_down = fields[1, l, j, rows_at(up), :], fields[1, l, j, rows_at(down), :]
                h_up, h_down = fields[2, l, j, rows_at(up), :], fields[2, l, j, rows_at(down), :]
                merid = (h[j] + h_down) * (v[j] + v_down) * north - (h_up + h[j]) * (v_up + v[j]) * south
                dx, dy = he[j] - hw[j], h_down - h_up
                new_h = h[j] - (0.25 * time_step) * (flux[j] - flux_west[j] + merid)
                new_u = u[j] - time_step * (0.5 * (sum_x[j] + 0.5 * dx) - coriolis * sine * v[j])
                new_v = v[j] - time_step * (0.5 * cosine * (sum_y[j] + 0.5 * dy) + coriolis * sine * u[j])
                sum_x[j] = sum_x[j] + dx
                sum_y[j] = sum_y[j] + dy
                wide = LANES if j < tiles - 1 else tail
                to = pl.ds(LANES * j, wide)
                thick[l, at, to] = new_h[:, :wide]
                winds[0, l, at, to] = new_u[:, :wide]
                winds[1, l, at, to] = new_v[:, :wide]
        copies += [
            pltpu.make_async_copy(winds.at[:, :, at], winds_hbm.at[:, :, at], sem.at[2 * g]),
            pltpu.make_async_copy(thick.at[:, at], thick_hbm.at[:, at], sem.at[2 * g + 1]),
        ]
        copies[-2].start()
        copies[-1].start()
    for copy in copies:
        copy.wait()


def stepped(fields, trig, hops, lon):
    levels = fields.shape[1]
    rows = trig.shape[1]
    shape = jax.ShapeDtypeStruct
    vmem = pl.BlockSpec(memory_space=pltpu.VMEM)
    hbm = pl.BlockSpec(memory_space=pltpu.HBM)
    return pl.pallas_call(
        functools.partial(step_kernel, lon),
        out_shape=[shape((2, levels, rows, lon), f32), shape((levels, rows, lon), f32)],
        in_specs=[vmem] * (2 + len(hops)),
        out_specs=[hbm, hbm],
        scratch_shapes=[
            pltpu.VMEM((2, levels, rows, lon), f32),
            pltpu.VMEM((levels, rows, lon), f32),
            pltpu.SemaphoreType.DMA((2 * (rows // 8),)),
        ],
        compiler_params=pltpu.CompilerParams(vmem_limit_bytes=32 << 20),
        name="step",
    )(fields, trig, *hops)


def swaps(lat_count, lev_count, first):
    pairs = []
    for i in range(lat_count):
        other = i + 1 if (i - first) % 2 == 0 else i - 1
        for l in range(lev_count):
            if 0 <= other < lat_count:
                pairs.append((i * lev_count + l, other * lev_count + l))
            else:
                pairs.append((i * lev_count + l, i * lev_count + (l + 1) % lev_count))
    return pairs


def per_device(winds, thick, cutoff):
    lat_count, lev_count = lax.axis_size("lat"), lax.axis_size("lev")
    lon = thick.shape[-1]
    sent_a, sent_b, trig, cut = edges(winds, thick, cutoff, lat_count)
    got_a = lax.ppermute(sent_a, ("lat", "lev"), swaps(lat_count, lev_count, 0))
    got_b = lax.ppermute(sent_b, ("lat", "lev"), swaps(lat_count, lev_count, 1))
    fields, column, tables = filtered_fields(winds, thick, cut)
    fields, column = with_halo(fields, column, tables, got_a, got_b, lon, lat_count)
    hops = [
        lax.ppermute(column, "lev", [(i, (i - hop) % lev_count) for i in range(lev_count)])
        for hop in range(1, lev_count)
    ]
    return tuple(stepped(fields, trig, hops, lon))


def solution(mesh):
    return jax.shard_map(
        per_device,
        mesh=mesh,
        in_specs=(P(None, "lev", "lat", None), P("lev", "lat", None), P("lat")),
        out_specs=(P(None, "lev", "lat", None), P("lev", "lat", None)),
        check_vma=False,
    )
```

time: 35.1 us -> 17.7 us (0.50)
  the two profiles are of different devices: /device:TPU:0 before, /device:TPU:27 now
where the time goes in v1:
time: 17.7 us; the launch traced here: 17.5 us
  Pallas kernels  11.9 us (67%)
  starting transfers between devices  3.79 us (21%)
  waiting for transfers between devices  1.14 us (6%)
  between operations  0.67 us (4%)
    pallas_call x1, Pallas kernels, filtered_fields(): pl.pallas_call(filter_kernel, out_shape=[pltpu.VMEM((3, levels, tiles, ro...  6.75 us
    pallas_call x1, Pallas kernels, stepped(): pl.pallas_call(functools.partial(step_kernel, lon), out_shape=[shape((2,...  2.72 us
    ppermute x1, starting transfers between devices, per_device(): got_b = lax.ppermute(sent_b, ('lat', 'lev'), swaps(lat_count, lev_count, 1))  2.17 us
    pallas_call x1, Pallas kernels, with_halo(): pl.pallas_call(functools.partial(halo_kernel, lon, lat_count), out_shape=...  1.56 us
    ppermute x1, starting transfers between devices, per_device(): lax.ppermute(column, 'lev', [(i, (i - hop) % lev_count) for i in range(le...  1.3 us
    ppermute x1, waiting for transfers between devices, per_device(): lax.ppermute(column, 'lev', [(i, (i - hop) % lev_count) for i in range(le...  1.14 us
    pallas_call x1, Pallas kernels, edges(): pl.pallas_call(functools.partial(edge_kernel, lat_count), out_shape=[edge...  0.87 us
  transfers between devices with their start and end apart: 3, of which 1 were waited for; matrix products, arithmetic and copies ran while one was open for 0% of the time, Pallas kernels for 39%

profile of v1, /device:TPU:27, one launch (start us, length us, event | category | flops | bytes accessed | tf_op | source)
XLA Modules:
  0.0 17.5 jit_solution(5212522295426962726)
XLA Ops:
  0.6 0.9 %edges.1 = (f32[104,128]{1,0:T(8,128)S(1)}, f32[104,128]{1,0:T(8,128)S(1)}, f32[4,32,128]{2,1,0:T(8,128)S(1)}, f32[32,128]{1,0:T(8,128)S(1)}) custom-call(f32[2,4,32,1440]{3,2,1,0:T(8,128)} %winds.3, f32[4,32,1440]{2,1,0:T(8,128)} %thick.3, s32[32]{0:T(128)} %cutoff_hbm.1), custom_call_target="tpu_custom_call" | custom-call | tf_op jit(solution)/shard_map/edges/pallas_call | solution.py:167
  1.5 0.3 %collective-permute-start = (f32[104,128]{1,0:T(8,128)S(1)}, f32[104,128]{1,0:T(8,128)S(1)}, u32[]{:S(2)}, u32[]{:S(2)}) collective-permute-start(f32[104,128]{1,0:T(8,128)S(1)} %get-tuple-element.11), channel_id=1, source_target_pairs={{0,2},{1,3},{2,0},{3,1},{4,6},{5,7},{6,4},{7,5},{8,10},{9,11},{10,... | collective-permute-start | bytes 159752 | tf_op jit(solution)/shard_map/ppermute | solution.py:481
  1.8 2.2 %collective-permute-start.1 = (f32[104,128]{1,0:T(8,128)S(1)}, f32[104,128]{1,0:T(8,128)S(1)}, u32[]{:S(2)}, u32[]{:S(2)}) collective-permute-start(f32[104,128]{1,0:T(8,128)S(1)} %get-tuple-element.12), channel_id=1, source_target_pairs={{0,1},{1,0},{2,4},{3,5},{4,2},{5,3},{6,8},{7,9},{8,6},{9,7},{10,12... | collective-permute-start | bytes 159752 | tf_op jit(solution)/shard_map/ppermute | solution.py:482
  4.0 6.8 %filter.1 = (f32[3,4,12,40,128]{4,3,2,1,0:T(8,128)S(1)}, f32[12,40,128]{2,1,0:T(8,128)S(1)}, bf16[6,2,256,256]{3,2,1,0:T(8,128)(2,1)S(1)}) custom-call(f32[2,4,32,1440]{3,2,1,0:T(8,128)} %winds.3, f32[4,32,1440]{2,1,0:T(8,128)} %thick.3, bf16[6,2,256,256]{3,2,1,0:T(8,128)(2,1)} %constant.2.clone.tables_hbm, f32[32,128]{1,0:T(8,128)S(1)} %get-tuple-element.13.cut), custom_call_target="tpu_custom_call" | custom-call | flops 10000000000 | bytes 8000000 | tf_op jit(solution)/shard_map/filter/pallas_call | solution.py:305
  10.8 0.0 collective-permute-done.got_a
  10.8 0.0 collective-permute-done.1.got_b
  10.8 1.6 %halo.1 = (f32[3,4,12,40,128]{4,3,2,1,0:T(8,128)S(1)}, f32[12,40,128]{2,1,0:T(8,128)S(1)}) custom-call(f32[104,128]{1,0:T(8,128)S(1)} %collective-permute-done.got_a, f32[104,128]{1,0:T(8,128)S(1)} %collective-permute-done.1.got_b, bf16[6,2,256,256]{3,2,1,0:T(8,128)(2,1)S(1)} %get-tuple-element.14.tables, ...), custom_call_target="tpu_custom_call", output_to_operand_aliasing={{0}: (3, {}), {1}: (4, {})} | custom-call | tf_op jit(solution)/shard_map/halo/pallas_call | solution.py:371
  12.3 1.3 %collective-permute-start.2 = (f32[12,40,128]{2,1,0:T(8,128)S(1)}, f32[12,40,128]{2,1,0:T(8,128)S(1)}, u32[]{:S(2)}, u32[]{:S(2)}) collective-permute-start(f32[12,40,128]{2,1,0:T(8,128)S(1)} %get-tuple-element.19), channel_id=1, source_target_pairs={{0,1},{1,0},{2,3},{3,2},{4,5},{5,4},{6,7},{7,6},{8,9},{9,8},{10,11... | collective-permute-start | bytes 737288 | tf_op jit(solution)/shard_map/ppermute | solution.py:486
  13.7 1.1 %collective-permute-done.2.refs_0_ = f32[12,40,128]{2,1,0:T(8,128)S(1)} collective-permute-done((f32[12,40,128]{2,1,0:T(8,128)S(1)}, f32[12,40,128]{2,1,0:T(8,128)S(1)}, u32[]{:S(2)}, u32[]{:S(2)}) %collective-permute-start.2) | collective-permute-done | bytes 245792 | tf_op jit(solution)/shard_map/ppermute | solution.py:486
  14.8 2.7 %step.1 = (f32[2,4,32,1440]{3,2,1,0:T(8,128)}, f32[4,32,1440]{2,1,0:T(8,128)}) custom-call(f32[3,4,12,40,128]{4,3,2,1,0:T(8,128)S(1)} %get-tuple-element.17.fields, f32[4,32,128]{2,1,0:T(8,128)S(1)} %get-tuple-element.18.trig, f32[12,40,128]{2,1,0:T(8,128)S(1)} %collective-permute-done.2.refs_0_), custom_call_target="tpu_custom_call" | custom-call | tf_op jit(solution)/shard_map/step/pallas_call | solution.py:450
Async XLA Ops:
  1.5 9.3 %collective-permute-start = (f32[104,128]{1,0:T(8,128)S(1)}, f32[104,128]{1,0:T(8,128)S(1)}, u32[]{:S(2)}, u32[]{:S(2)}) collective-permute-start(f32[104,128]{1,0:T(8,128)S(1)} %get-tuple-element.11), channel_id=1, source_target_pairs={{0,2},{1,3},{2,0},{3,1},{4,6},{5,7},{6,4},{7,5},{8,10},{9,11},{10,... | collective-permute-start | bytes 159752 | tf_op jit(solution)/shard_map/ppermute | solution.py:481
  1.8 8.9 %collective-permute-start.1 = (f32[104,128]{1,0:T(8,128)S(1)}, f32[104,128]{1,0:T(8,128)S(1)}, u32[]{:S(2)}, u32[]{:S(2)}) collective-permute-start(f32[104,128]{1,0:T(8,128)S(1)} %get-tuple-element.12), channel_id=1, source_target_pairs={{0,1},{1,0},{2,4},{3,5},{4,2},{5,3},{6,8},{7,9},{8,6},{9,7},{10,12... | collective-permute-start | bytes 159752 | tf_op jit(solution)/shard_map/ppermute | solution.py:482
  12.3 2.4 %collective-permute-start.2 = (f32[12,40,128]{2,1,0:T(8,128)S(1)}, f32[12,40,128]{2,1,0:T(8,128)S(1)}, u32[]{:S(2)}, u32[]{:S(2)}) collective-permute-start(f32[12,40,128]{2,1,0:T(8,128)S(1)} %get-tuple-element.19), channel_id=1, source_target_pairs={{0,1},{1,0},{2,3},{3,2},{4,5},{5,4},{6,7},{7,6},{8,9},{9,8},{10,11... | collective-permute-start | bytes 737288 | tf_op jit(solution)/shard_map/ppermute | solution.py:486

commit v2 on v1

v2 whole, which is shorter than its diff:
```python
import functools
import math

import jax
import jax.numpy as jnp
import ml_dtypes
import numpy as np
from jax import lax
from jax.experimental import pallas as pl
from jax.experimental.pallas import tpu as pltpu
from jax.sharding import PartitionSpec as P

time_step = 0.2
coriolis = 1.0
RADIX = 12
LANES = 128
WIDE = 2 * LANES
HALF_ROOT3 = math.sqrt(3.0) / 2.0
f32 = jnp.float32
bf16 = jnp.bfloat16


def filter_tables(lon):
    chunk, half = lon // RADIX, RADIX // 2
    point = np.arange(chunk)
    angle = 2.0 * math.pi * (np.outer(point, point) % chunk) / chunk
    table = np.zeros((WIDE, WIDE), np.float64)
    near, far = slice(0, chunk), slice(LANES, LANES + chunk)
    table[near, near], table[near, far] = np.cos(angle), np.sin(angle)
    table[far, near], table[far, far] = np.sin(angle), -np.cos(angle)
    table /= math.sqrt(lon)
    high = table.astype(np.float32).astype(ml_dtypes.bfloat16)
    low = (table - high.astype(np.float64)).astype(np.float32).astype(ml_dtypes.bfloat16)
    twiddle = np.zeros((2, 2, 8, LANES), np.float64)
    for k in range(1, half + 1):
        turn = 2.0 * math.pi * (k * point % lon) / lon
        for way, scale in enumerate((1.0, 1.0 if k == half else 2.0)):
            twiddle[way, 0, k, :chunk] = scale * np.cos(turn)
            twiddle[way, 1, k, :chunk] = scale * np.sin(turn)
    return np.stack([high, low]), twiddle.astype(np.float32)


def split_radix(c):
    s = [c[j] + c[j + 6] for j in range(6)]
    d = [c[j] - c[j + 6] for j in range(6)]
    t = [s[j] + s[j + 3] for j in range(3)]
    e = [s[j] - s[j + 3] for j in range(3)]
    t12 = t[1] + t[2]
    e12 = e[1] - e[2]
    y0 = t[0] + t12
    y4 = (t[0] - 0.5 * t12, HALF_ROOT3 * (t[2] - t[1]))
    y6 = e[0] - e12
    y2 = (e[0] + 0.5 * e12, -HALF_ROOT3 * (e[1] + e[2]))
    p, q = d[1] - d[5], d[2] - d[4]
    r, w = d[1] + d[5], d[2] + d[4]
    y3 = (d[0] - q, d[3] - r)
    u, v = d[0] + 0.5 * q, -0.5 * r - d[3]
    sp, sw = HALF_ROOT3 * p, HALF_ROOT3 * w
    y1 = (u + sp, v - sw)
    y5 = (u - sp, v + sw)
    return [(y0, y6), y1, y2, y3, y4, y5]


def join_radix(z):
    (z0, z6), (r1, i1), (r2, i2), (r3, i3), (r4, i4), (r5, i5) = z
    hp, sp = z0 - 0.5 * r4, HALF_ROOT3 * i4
    p = [z0 + r4, hp - sp, hp + sp]
    hq, sq = z6 - 0.5 * r2, HALF_ROOT3 * i2
    q = [z6 + r2, -hq - sq, hq - sq]
    e = [p[j] + q[j] for j in range(3)] + [p[j] - q[j] for j in range(3)]
    a, b, c, d = r1 + r5, HALF_ROOT3 * (r1 - r5), i1 + i5, HALF_ROOT3 * (i1 - i5)
    g = r3 - 0.5 * a
    f = -0.5 * c - i3
    o = [a + r3, b + f, -g - d, i3 - c, g - d, f - b]
    return [e[j] + o[j] for j in range(6)] + [e[j] - o[j] for j in range(6)]


def rolled(x, left):
    shift = (-left) % LANES
    return x if shift == 0 else pltpu.roll(x, shift, 1)


def lane_index(rows=8):
    return lax.broadcasted_iota(jnp.int32, (rows, LANES), 1)


def two_parts(x):
    high = x.astype(bf16)
    return high, (x - high.astype(f32)).astype(bf16)


def rows_at(start, size=8):
    return pl.ds(start, size)


def edge_kernel(lat_count, winds, thick, cutoff_hbm, sent_a, sent_b, trig, cut, v, h, cutoff, sem):
    levels, lon = v.shape[1:]
    rows = thick.shape[1]
    tiles = -(-lon // LANES)
    tail = lon - (tiles - 1) * LANES
    copies = [pltpu.make_async_copy(cutoff_hbm, cutoff, sem.at[4])]
    for side, start in enumerate((0, rows - 1)):
        copies.append(pltpu.make_async_copy(winds.at[1, :, start], v.at[side], sem.at[2 * side]))
        copies.append(pltpu.make_async_copy(thick.at[:, start], h.at[side], sem.at[2 * side + 1]))
    for copy in copies:
        copy.start()

    place = lax.axis_index("lat")
    index = (place * rows + lax.broadcasted_iota(jnp.int32, (rows, LANES), 0)).astype(f32)
    step = math.pi / (lat_count * rows)
    centre = (index + 0.5) * step - 0.5 * math.pi
    trig[0] = jnp.sin(centre)
    trig[1] = jnp.cos(centre)
    trig[2] = jnp.sin(index * step)
    trig[3] = jnp.sin((index + 1.0) * step)

    copies[0].wait()
    for r in range(rows):
        cut[pl.ds(r, 1), :] = jnp.full((1, LANES), cutoff[r].astype(f32), f32)
    for copy in copies[1:]:
        copy.wait()
    last_first = 1 - place % 2
    for out, side in ((sent_a, last_first), (sent_b, 1 - last_first)):
        limit = cutoff[side * (rows - 1)].astype(f32)
        for j in range(tiles):
            wide = LANES if j < tiles - 1 else tail
            for f, block in enumerate((v, h)):
                got = block[side, :, pl.ds(LANES * j, wide)]
                if wide < LANES:
                    got = jnp.concatenate([got, jnp.full((levels, LANES - wide), limit, f32)], axis=1)
                out[pl.ds((2 * j + f) * levels, levels), :] = got


def in_vmem(x):
    return pltpu.with_memory_space_constraint(x, pltpu.VMEM)


def in_hbm(x):
    return pltpu.with_memory_space_constraint(x, pltpu.HBM)


def edges(winds, thick, cutoff, lat_count):
    levels, rows, lon = thick.shape
    tiles = -(-lon // LANES)
    vmem = pl.BlockSpec(memory_space=pltpu.VMEM)
    hbm = pl.BlockSpec(memory_space=pltpu.HBM)
    assert lon < tiles * LANES
    edge = jax.ShapeDtypeStruct((2 * levels * tiles, LANES), f32)
    return pl.pallas_call(
        functools.partial(edge_kernel, lat_count),
        out_shape=[edge, edge, pltpu.VMEM((4, rows, LANES), f32), pltpu.VMEM((rows, LANES), f32)],
        in_specs=[hbm] * 3,
        out_specs=[vmem] * 4,
        scratch_shapes=[
            pltpu.VMEM((2, levels, lon), f32),
            pltpu.VMEM((2, levels, lon), f32),
            pltpu.SMEM((rows,), jnp.int32),
            pltpu.SemaphoreType.DMA((5,)),
        ],
        compiler_params=pltpu.CompilerParams(vmem_limit_bytes=16 << 20),
        cost_estimate=pl.CostEstimate(flops=4_000_000_000, bytes_accessed=8_000_000, transcendentals=0),
        name="edges",
    )(in_hbm(winds), in_hbm(thick), in_hbm(cutoff))


def forward(v, chunk, y, at, twiddle):
    gap, half = LANES - chunk, RADIX // 2
    lane = lane_index(v[0].shape[0])
    c = []
    for j in range(RADIX):
        turn = gap * j
        here = jnp.where(lane < LANES - turn, v[j], v[j - 1]) if turn else v[j]
        c.append(rolled(here, -turn))
    c[-1] = jnp.where(lane < chunk, c[-1], 0.0)
    (y0, y6), *pairs = split_radix(c)
    for k in range(half + 1):
        cos, sin = twiddle[0, 0, k : k + 1, :], twiddle[0, 1, k : k + 1, :]
        if k == 0:
            both = (y0, jnp.zeros_like(y0))
        elif k == half:
            both = (y6 * cos, -(y6 * sin))
        else:
            re, im = pairs[k - 1]
            both = (re * cos + im * sin, im * cos - re * sin)
        for part, value in enumerate(both):
            hi, lo = two_parts(value)
            y[k, at, LANES * part : LANES * (part + 1)] = hi
            y[k, at, WIDE + LANES * part : WIDE + LANES * (part + 1)] = lo


def three(high, low, tables):
    a = jnp.concatenate([high, low, high], axis=1)
    b = jnp.concatenate([tables[0], tables[0], tables[1]], axis=0)
    return lax.dot_general(a, b, (((1,), (0,)), ((), ())), preferred_element_type=f32)


def low_pass(lon, y, z, tables, keep):
    classes, count = y.shape[:2]
    shape = (classes, count, WIDE)
    both = y[...].reshape(classes * count, 2 * WIDE)
    coeffs = three(both[:, :WIDE], both[:, WIDE:], tables).reshape(shape)
    at = lax.broadcasted_iota(jnp.int32, (1, WIDE), 1)
    at = jnp.where(at < LANES, at, at - LANES)
    masked = []
    for k in range(classes):
        m = RADIX * at + k
        masked.append(jnp.where(jnp.minimum(m, lon - m).astype(f32) <= keep, coeffs[k], 0.0))
    high, low = two_parts(jnp.concatenate(masked, axis=0))
    z[...] = three(high, low, tables).reshape(shape)


def backward(z, at, chunk, twiddle):
    gap, half = LANES - chunk, RADIX // 2
    lane = lane_index()
    pairs = [(z[0, at, :LANES], None)]
    for k in range(1, half + 1):
        re, im = z[k, at, :LANES], z[k, at, LANES:]
        cos, sin = twiddle[1, 0, k : k + 1, :], twiddle[1, 1, k : k + 1, :]
        pairs.append((re * cos - im * sin, re * sin + im * cos if k < half else None))
    c = join_radix([(pairs[0][0], pairs[half][0])] + pairs[1:half])
    c = [rolled(c[j % RADIX], gap * j) for j in range(RADIX + 1)]
    return [jnp.where(lane < LANES - gap * (j + 1), c[j], c[j + 1]) for j in range(RADIX)]


def extended(v, tail):
    return v[:-1] + [jnp.where(lane_index() < tail, v[-1], rolled(v[0], LANES - tail))]


def filter_kernel(winds, thick, tables, twiddle, cut, out, column, y, z):
    levels, rows, lon = thick.shape
    tiles = out.shape[2]
    chunk = lon // RADIX
    tail = lon - (tiles - 1) * LANES
    order = (2, 0, 1)
    keep = cut[...]
    filtering = jnp.min(keep) < lon // 2

    def own_tiles(f, l, at):
        block, lead = (winds, (f, l)) if f < 2 else (thick, (l,))
        got = [block[(*lead, at, pl.ds(LANES * j, LANES))] for j in range(tiles - 1)]
        last = block[(*lead, at, pl.ds(LANES * (tiles - 1), tail))]
        return got + [jnp.concatenate([last, jnp.zeros((at.size, LANES - tail), f32)], axis=1)]

    @pl.when(jnp.logical_not(filtering))
    def _():
        for f in order:

            def as_is(l, _, f=f):
                for g in range(rows // 8):
                    v = extended(own_tiles(f, l, rows_at(8 * g)), tail)
                    for j in range(tiles):
                        out[f, l, j, rows_at(1 + 8 * g), :] = v[j]
                return 0

            lax.fori_loop(0, levels, as_is, 0)

    @pl.when(filtering)
    def _():
        units = y.shape[0]
        per = 3 * levels // units
        wide = jnp.concatenate([jnp.concatenate([keep, keep], axis=1)] * per, axis=0)

        def members(n):
            return [(order[(n * per + i) // levels], (n * per + i) % levels, i * rows) for i in range(per)]


        def split(n):
            for f, l, start in members(n):
                for g in range(rows // 16):
                    at = pl.ds(start + 16 * g, 16)
                    forward(own_tiles(f, l, rows_at(16 * g, 16)), chunk, y.at[n], at, twiddle)

        def join(n):
            for f, l, start in members(n):
                for g in range(rows // 8):
                    v = backward(z.at[n], rows_at(start + 8 * g), chunk, twiddle)
                    for j in range(tiles):
                        out[f, l, j, rows_at(1 + 8 * g), :] = v[j]

        split(0)
        for n in range(units):
            low_pass(lon, y.at[n], z.at[n], tables, wide)
            if n + 1 < units:
                split(n + 1)
            if n > 0:
                join(n - 1)
        join(units - 1)

    at = pl.ds(1, rows)
    for j in range(tiles):
        column[j, at, :] = functools.reduce(jnp.add, [out[2, l, j, at, :] for l in range(levels)])


def filtered_fields(winds, thick, cut, tables, twiddle):
    levels, rows, lon = thick.shape
    tiles = -(-lon // LANES)
    assert lon % RADIX == 0 and lon // RADIX <= LANES and tiles == RADIX
    assert rows % 16 == 0 and levels % 2 == 0
    classes = RADIX // 2 + 1
    per = 2
    units = 3 * levels // per
    vmem = pl.BlockSpec(memory_space=pltpu.VMEM)
    hbm = pl.BlockSpec(memory_space=pltpu.HBM)
    return pl.pallas_call(
        filter_kernel,
        out_shape=[
            pltpu.VMEM((3, levels, tiles, rows + 8, LANES), f32),
            pltpu.VMEM((tiles, rows + 8, LANES), f32),
        ],
        in_specs=[vmem] * 5,
        out_specs=[vmem] * 2,
        scratch_shapes=[
            pltpu.VMEM((units, classes, per * rows, 2 * WIDE), bf16),
            pltpu.VMEM((units, classes, per * rows, WIDE), f32),
        ],
        compiler_params=pltpu.CompilerParams(vmem_limit_bytes=24 << 20),
        cost_estimate=pl.CostEstimate(flops=10_000_000_000, bytes_accessed=8_000_000, transcendentals=0),
        name="filter",
    )(in_vmem(winds), in_vmem(thick), in_vmem(tables), in_vmem(twiddle), cut)


def halo_kernel(lon, lat_count, got_a, got_b, tables, twiddle, _fields, _column, out, column, y, z):
    levels, tiles, rows = out.shape[1], out.shape[2], out.shape[3] - 8
    chunk = lon // RADIX
    tail = lon - (tiles - 1) * LANES
    place = lax.axis_index("lat")
    odd = place % 2
    refs = (got_a, got_b)
    at = (jnp.where(odd == 1, 0, rows + 1), jnp.where(odd == 1, rows + 1, 0))
    keep = jnp.concatenate([ref[rows_at(2 * levels * (tiles - 1), 2 * levels), :] for ref in refs], axis=0)
    keep = jnp.where(lane_index(16) < tail, rolled(keep, tail), keep)

    def edge_tiles(ref):
        v = [ref[rows_at(2 * levels * j, 2 * levels), :] for j in range(tiles)]
        return v[:-1] + [jnp.where(lane_index() < tail, v[-1], 0.0)]

    def put(side, v):
        end = jnp.where(at[side] == 0, place == 0, place == lat_count - 1)
        for j in range(tiles):
            value = jnp.where(end, 0.0, v[j])
            for f in range(2):
                lines = [value[f * levels + l : f * levels + l + 1] for l in range(levels)]
                for l in range(levels):
                    out[1 + f, l, j, pl.ds(at[side], 1), :] = lines[l]
            column[j, pl.ds(at[side], 1), :] = functools.reduce(jnp.add, lines)

    filtering = jnp.min(keep) < lon // 2

    @pl.when(jnp.logical_not(filtering))
    def _():
        for side in range(2):
            put(side, extended(edge_tiles(refs[side]), tail))

    @pl.when(filtering)
    def _():
        both = [jnp.concatenate(pair, axis=0) for pair in zip(edge_tiles(got_a), edge_tiles(got_b))]
        forward(both, chunk, y, pl.ds(0, 16), twiddle)
        wide = jnp.concatenate([keep, keep], axis=1)
        low_pass(lon, y, z, tables, wide)
        for side in range(2):
            put(side, backward(z, rows_at(8 * side), chunk, twiddle))


def with_halo(fields, column, tables, twiddle, got_a, got_b, lon, lat_count):
    assert 2 * fields.shape[1] == 8
    classes = RADIX // 2 + 1
    vmem = pl.BlockSpec(memory_space=pltpu.VMEM)
    return pl.pallas_call(
        functools.partial(halo_kernel, lon, lat_count),
        out_shape=[pltpu.VMEM(fields.shape, f32), pltpu.VMEM(column.shape, f32)],
        in_specs=[vmem] * 6,
        out_specs=[vmem] * 2,
        scratch_shapes=[pltpu.VMEM((classes, 16, 2 * WIDE), bf16), pltpu.VMEM((classes, 16, WIDE), f32)],
        input_output_aliases={4: 0, 5: 1},
        compiler_params=pltpu.CompilerParams(vmem_limit_bytes=24 << 20),
        name="halo",
    )(got_a, got_b, tables, twiddle, fields, column)


def east(v):
    lane = lane_index()
    r = [rolled(a, 1) for a in v]
    return [jnp.where(lane < LANES - 1, a, b) for a, b in zip(r[:-1], r[1:])] + [r[-1]]


def west(v, tail):
    lane = lane_index()
    r = [rolled(a, -1) for a in v]
    r_before = [rolled(v[-1], tail - 1)] + r[:-1]
    return [jnp.where(lane > 0, a, b) for a, b in zip(r, r_before)]


def thickness_kernel(lon, fields, trig, thick_hbm, thick, sem):
    levels, tiles = fields.shape[1:3]
    rows = trig.shape[1]
    tail = lon - (tiles - 1) * LANES
    copies = []
    for g in range(rows // 8):
        at = rows_at(8 * g)
        up, here, down = 8 * g, 8 * g + 1, 8 * g + 2
        south, north = trig[2, at, :], trig[3, at, :]
        for l in range(levels):
            u, h = ([fields[f, l, j, rows_at(here), :] for j in range(tiles)] for f in (0, 2))
            he, ue = east(h), east(u)
            flux = [(h[j] + he[j]) * (u[j] + ue[j]) for j in range(tiles)]
            flux_west = west(flux, tail)
            for j in range(tiles):
                v_up, v, v_down = (fields[1, l, j, rows_at(r), :] for r in (up, here, down))
                h_up, h_down = (fields[2, l, j, rows_at(r), :] for r in (up, down))
                merid = (h[j] + h_down) * (v + v_down) * north - (h_up + h[j]) * (v_up + v) * south
                new = h[j] - (0.25 * time_step) * (flux[j] - flux_west[j] + merid)
                wide = LANES if j < tiles - 1 else tail
                thick[l, at, pl.ds(LANES * j, wide)] = new[:, :wide]
        copies.append(pltpu.make_async_copy(thick.at[:, at], thick_hbm.at[:, at], sem.at[g]))
        copies[-1].start()
    for copy in copies:
        copy.wait()


def winds_kernel(lon, fields, trig, *refs):
    *hops, winds_hbm, winds, sem = refs
    levels, tiles = fields.shape[1:3]
    rows = trig.shape[1]
    tail = lon - (tiles - 1) * LANES
    place = lax.axis_index("lev")
    masks = [jnp.where(place + k + 1 <= len(hops), 1.0, 0.0) for k in range(len(hops))]

    def below(j, at):
        terms = [ref[j, rows_at(at), :] * mask for ref, mask in zip(hops, masks)]
        return functools.reduce(jnp.add, terms) if terms else jnp.zeros((8, LANES), f32)

    copies = []
    for g in range(rows // 8):
        at = rows_at(8 * g)
        up, here, down = 8 * g, 8 * g + 1, 8 * g + 2
        sine, cosine = trig[0, at, :], trig[1, at, :]
        s = [below(j, here) for j in range(tiles)]
        sum_x = [a - b for a, b in zip(east(s), west(s, tail))]
        sum_y = [below(j, down) - below(j, up) for j in range(tiles)]
        for l in reversed(range(levels)):
            h = [fields[2, l, j, rows_at(here), :] for j in range(tiles)]
            he, hw = east(h), west(h, tail)
            for j in range(tiles):
                u, v = (fields[f, l, j, rows_at(here), :] for f in range(2))
                dx = he[j] - hw[j]
                dy = fields[2, l, j, rows_at(down), :] - fields[2, l, j, rows_at(up), :]
                new_u = u - time_step * (0.5 * (sum_x[j] + 0.5 * dx) - coriolis * sine * v)
                new_v = v - time_step * (0.5 * cosine * (sum_y[j] + 0.5 * dy) + coriolis * sine * u)
                sum_x[j] = sum_x[j] + dx
                sum_y[j] = sum_y[j] + dy
                wide = LANES if j < tiles - 1 else tail
                to = pl.ds(LANES * j, wide)
                winds[0, l, at, to] = new_u[:, :wide]
                winds[1, l, at, to] = new_v[:, :wide]
        copies.append(pltpu.make_async_copy(winds.at[:, :, at], winds_hbm.at[:, :, at], sem.at[g]))
        copies[-1].start()
    for copy in copies:
        copy.wait()


def step_call(kernel, name, shape, flops, lon, operands):
    rows = operands[1].shape[1]
    return pl.pallas_call(
        functools.partial(kernel, lon),
        out_shape=jax.ShapeDtypeStruct(shape, f32),
        in_specs=[pl.BlockSpec(memory_space=pltpu.VMEM)] * len(operands),
        out_specs=pl.BlockSpec(memory_space=pltpu.HBM),
        scratch_shapes=[pltpu.VMEM(shape, f32), pltpu.SemaphoreType.DMA((rows // 8,))],
        compiler_params=pltpu.CompilerParams(vmem_limit_bytes=24 << 20),
        cost_estimate=pl.CostEstimate(flops=flops, bytes_accessed=4_000_000, transcendentals=0),
        name=name,
    )(*operands)


def swaps(lat_count, lev_count, first):
    pairs = []
    for i in range(lat_count):
        other = i + 1 if (i - first) % 2 == 0 else i - 1
        for l in range(lev_count):
            if 0 <= other < lat_count:
                pairs.append((i * lev_count + l, other * lev_count + l))
            else:
                pairs.append((i * lev_count + l, i * lev_count + (l + 1) % lev_count))
    return pairs


def per_device(winds, thick, cutoff):
    lat_count, lev_count = lax.axis_size("lat"), lax.axis_size("lev")
    lon = thick.shape[-1]
    sent_a, sent_b, trig, cut = edges(winds, thick, cutoff, lat_count)
    got_a = lax.ppermute(sent_a, ("lat", "lev"), swaps(lat_count, lev_count, 0))
    got_b = lax.ppermute(sent_b, ("lat", "lev"), swaps(lat_count, lev_count, 1))
    tables, twiddle = (jnp.asarray(constant) for constant in filter_tables(lon))
    fields, column = filtered_fields(winds, thick, cut, tables, twiddle)
    fields, column = with_halo(fields, column, tables, twiddle, got_a, got_b, lon, lat_count)
    hops = [
        lax.ppermute(column, "lev", [(i, (i - hop) % lev_count) for i in range(lev_count)])
        for hop in range(1, lev_count)
    ]
    new_thick = step_call(thickness_kernel, "thickness", thick.shape, 4_000_000_000, lon, (fields, trig))
    new_winds = step_call(winds_kernel, "winds", winds.shape, 1_000_000_000, lon, (fields, trig, *hops))
    return new_winds, new_thick


def solution(mesh):
    return jax.shard_map(
        per_device,
        mesh=mesh,
        in_specs=(P(None, "lev", "lat", None), P("lev", "lat", None), P("lat")),
        out_specs=(P(None, "lev", "lat", None), P("lev", "lat", None)),
        check_vma=False,
    )
```

time: 17.7 us -> 14.5 us (0.82)
  the two profiles are of different devices: /device:TPU:27 before, /device:TPU:25 now
where the time goes in v2:
time: 14.5 us; the launch traced here: 14.4 us
  Pallas kernels  6.63 us (46%)
  starting transfers between devices  4.54 us (31%)
  waiting for transfers between devices  2.48 us (17%)
  between operations  0.71 us (5%)
    pallas_call x2, Pallas kernels, step_call(): pl.pallas_call(functools.partial(kernel, lon), out_shape=jax.ShapeDtypeSt...  3.63 us
    ppermute x1, waiting for transfers between devices, per_device(): got_b = lax.ppermute(sent_b, ('lat', 'lev'), swaps(lat_count, lev_count, 1))  2.47 us
    ppermute x1, starting transfers between devices, per_device(): lax.ppermute(column, 'lev', [(i, (i - hop) % lev_count) for i in range(le...  2.17 us
    ppermute x1, starting transfers between devices, per_device(): got_a = lax.ppermute(sent_a, ('lat', 'lev'), swaps(lat_count, lev_count, 0))  1.28 us
    pallas_call x1, Pallas kernels, filtered_fields(): pl.pallas_call(filter_kernel, out_shape=[pltpu.VMEM((3, levels, tiles, ro...  1.14 us
    ppermute x1, starting transfers between devices, per_device(): got_b = lax.ppermute(sent_b, ('lat', 'lev'), swaps(lat_count, lev_count, 1))  1.1 us
    pallas_call x1, Pallas kernels, edges(): pl.pallas_call(functools.partial(edge_kernel, lat_count), out_shape=[edge...  1.01 us
    pallas_call x1, Pallas kernels, with_halo(): pl.pallas_call(functools.partial(halo_kernel, lon, lat_count), out_shape=...  0.85 us
  transfers between devices with their start and end apart: 3, of which 1 were waited for; matrix products, arithmetic and copies ran while one was open for 0% of the time, Pallas kernels for 23%

profile of v2, /device:TPU:25, one launch (start us, length us, event | category | flops | bytes accessed | tf_op | source)
XLA Modules:
  0.0 14.4 jit_solution(4844448190262095156)
XLA Ops:
  0.6 0.0 copy-start
  0.6 0.0 copy-start.1
  0.7 0.0 copy-start.3
  0.7 0.0 copy-start.2
  0.7 1.0 %edges.1 = (f32[96,128]{1,0:T(8,128)S(1)}, f32[96,128]{1,0:T(8,128)S(1)}, f32[4,32,128]{2,1,0:T(8,128)S(1)}, f32[32,128]{1,0:T(8,128)S(1)}) custom-call(f32[2,4,32,1440]{3,2,1,0:T(8,128)} %winds.4, f32[4,32,1440]{2,1,0:T(8,128)} %thick.3, s32[32]{0:T(128)} %cutoff_hbm.1), custom_call_target="tpu_custom_call" | custom-call | flops 4000000000 | bytes 8000000 | tf_op jit(solution)/shard_map/edges/pallas_call | solution.py:149
  1.7 1.3 %collective-permute-start = (f32[96,128]{1,0:T(8,128)S(1)}, f32[96,128]{1,0:T(8,128)S(1)}, u32[]{:S(2)}, u32[]{:S(2)}) collective-permute-start(f32[96,128]{1,0:T(8,128)S(1)} %get-tuple-element.10), channel_id=1, source_target_pairs={{0,2},{1,3},{2,0},{3,1},{4,6},{5,7},{6,4},{7,5},{8,10},{9,11},{10,... | collective-permute-start | bytes 147464 | tf_op jit(solution)/shard_map/ppermute | solution.py:491
  3.0 1.1 %collective-permute-start.1 = (f32[96,128]{1,0:T(8,128)S(1)}, f32[96,128]{1,0:T(8,128)S(1)}, u32[]{:S(2)}, u32[]{:S(2)}) collective-permute-start(f32[96,128]{1,0:T(8,128)S(1)} %get-tuple-element.11), channel_id=1, source_target_pairs={{0,1},{1,0},{2,4},{3,5},{4,2},{5,3},{6,8},{7,9},{8,6},{9,7},{10,12... | collective-permute-start | bytes 147464 | tf_op jit(solution)/shard_map/ppermute | solution.py:492
  4.1 0.0 copy-done
  4.1 0.0 copy-done.1
  4.1 0.0 copy-done.3
  4.1 0.0 copy-done.2
  4.1 1.1 %filter.1 = (f32[3,4,12,40,128]{4,3,2,1,0:T(8,128)S(1)}, f32[12,40,128]{2,1,0:T(8,128)S(1)}) custom-call(f32[2,4,32,1440]{3,2,1,0:T(8,128)S(1)} %copy-done.2, f32[4,32,1440]{2,1,0:T(8,128)S(1)} %copy-done.3, bf16[2,256,256]{2,1,0:T(8,128)(2,1)S(1)} %copy-done, f32[2,2,8,128]{3,2,1,0:T(8,128)S(1)} %copy-done.1, f32[32,128]{1,0:T(8,128)S(1)} %get-tuple-element.12.cut), custom_call_target="tpu_custom_call" | custom-call | flops 10000000000 | bytes 8000000 | tf_op jit(solution)/shard_map/filter/pallas_call | solution.py:304
  5.2 0.0 collective-permute-done.got_a
  5.2 2.5 %collective-permute-done.1.got_b = f32[96,128]{1,0:T(8,128)S(1)} collective-permute-done((f32[96,128]{1,0:T(8,128)S(1)}, f32[96,128]{1,0:T(8,128)S(1)}, u32[]{:S(2)}, u32[]{:S(2)}) %collective-permute-start.1) | collective-permute-done | bytes 49184 | tf_op jit(solution)/shard_map/ppermute | solution.py:492
  7.7 0.8 %halo.1 = (f32[3,4,12,40,128]{4,3,2,1,0:T(8,128)S(1)}, f32[12,40,128]{2,1,0:T(8,128)S(1)}) custom-call(f32[96,128]{1,0:T(8,128)S(1)} %collective-permute-done.got_a, f32[96,128]{1,0:T(8,128)S(1)} %collective-permute-done.1.got_b, bf16[2,256,256]{2,1,0:T(8,128)(2,1)S(1)} %copy-done, ...), custom_call_target="tpu_custom_call", output_to_operand_aliasing={{0}: (4, {}), {1}: (5, {})} | custom-call | tf_op jit(solution)/shard_map/halo/pallas_call | solution.py:368
  8.6 2.2 %collective-permute-start.2 = (f32[12,40,128]{2,1,0:T(8,128)S(1)}, f32[12,40,128]{2,1,0:T(8,128)S(1)}, u32[]{:S(2)}, u32[]{:S(2)}) collective-permute-start(f32[12,40,128]{2,1,0:T(8,128)S(1)} %get-tuple-element.17), channel_id=1, source_target_pairs={{0,1},{1,0},{2,3},{3,2},{4,5},{5,4},{6,7},{7,6},{8,9},{9,8},{10,11... | collective-permute-start | bytes 737288 | tf_op jit(solution)/shard_map/ppermute | solution.py:497
  10.7 2.2 %thickness.1 = f32[4,32,1440]{2,1,0:T(8,128)} custom-call(f32[3,4,12,40,128]{4,3,2,1,0:T(8,128)S(1)} %get-tuple-element.15.fields, f32[4,32,128]{2,1,0:T(8,128)S(1)} %get-tuple-element.16.trig), custom_call_target="tpu_custom_call" | custom-call | flops 4000000000 | bytes 4000000 | tf_op jit(solution)/shard_map/thickness/pallas_call | solution.py:463
  12.9 0.0 collective-permute-done.2.refs_0_
  13.0 1.4 %winds.5 = f32[2,4,32,1440]{3,2,1,0:T(8,128)} custom-call(f32[3,4,12,40,128]{4,3,2,1,0:T(8,128)S(1)} %get-tuple-element.15.fields, f32[4,32,128]{2,1,0:T(8,128)S(1)} %get-tuple-element.16.trig, f32[12,40,128]{2,1,0:T(8,128)S(1)} %collective-permute-done.2.refs_0_), custom_call_target="tpu_custom_call" | custom-call | flops 1000000000 | bytes 4000000 | tf_op jit(solution)/shard_map/winds/pallas_call | solution.py:463
Async XLA Ops:
  0.6 3.4 %copy-start = (bf16[2,256,256]{2,1,0:T(8,128)(2,1)S(1)}, bf16[2,256,256]{2,1,0:T(8,128)(2,1)}, u32[]{:S(2)}) copy-start(bf16[2,256,256]{2,1,0:T(8,128)(2,1)} %constant.4.clone.tables) | copy-start | bytes 786436
  0.6 3.4 %copy-start.1 = (f32[2,2,8,128]{3,2,1,0:T(8,128)S(1)}, f32[2,2,8,128]{3,2,1,0:T(8,128)}, u32[]{:S(2)}) copy-start(f32[2,2,8,128]{3,2,1,0:T(8,128)} %constant.5.clone.twiddle) | copy-start | bytes 49156
  0.7 3.4 %copy-start.3 = (f32[4,32,1440]{2,1,0:T(8,128)S(1)}, f32[4,32,1440]{2,1,0:T(8,128)}, u32[]{:S(2)}) copy-start(f32[4,32,1440]{2,1,0:T(8,128)} %thick.3) | copy-start | bytes 2211844
  0.7 3.4 %copy-start.2 = (f32[2,4,32,1440]{3,2,1,0:T(8,128)S(1)}, f32[2,4,32,1440]{3,2,1,0:T(8,128)}, u32[]{:S(2)}) copy-start(f32[2,4,32,1440]{3,2,1,0:T(8,128)} %winds.4) | copy-start | bytes 4423684
  1.7 3.5 %collective-permute-start = (f32[96,128]{1,0:T(8,128)S(1)}, f32[96,128]{1,0:T(8,128)S(1)}, u32[]{:S(2)}, u32[]{:S(2)}) collective-permute-start(f32[96,128]{1,0:T(8,128)S(1)} %get-tuple-element.10), channel_id=1, source_target_pairs={{0,2},{1,3},{2,0},{3,1},{4,6},{5,7},{6,4},{7,5},{8,10},{9,11},{10,... | collective-permute-start | bytes 147464 | tf_op jit(solution)/shard_map/ppermute | solution.py:491
  3.0 4.7 %collective-permute-start.1 = (f32[96,128]{1,0:T(8,128)S(1)}, f32[96,128]{1,0:T(8,128)S(1)}, u32[]{:S(2)}, u32[]{:S(2)}) collective-permute-start(f32[96,128]{1,0:T(8,128)S(1)} %get-tuple-element.11), channel_id=1, source_target_pairs={{0,1},{1,0},{2,4},{3,5},{4,2},{5,3},{6,8},{7,9},{8,6},{9,7},{10,12... | collective-permute-start | bytes 147464 | tf_op jit(solution)/shard_map/ppermute | solution.py:492
  8.6 4.4 %collective-permute-start.2 = (f32[12,40,128]{2,1,0:T(8,128)S(1)}, f32[12,40,128]{2,1,0:T(8,128)S(1)}, u32[]{:S(2)}, u32[]{:S(2)}) collective-permute-start(f32[12,40,128]{2,1,0:T(8,128)S(1)} %get-tuple-element.17), channel_id=1, source_target_pairs={{0,1},{1,0},{2,3},{3,2},{4,5},{5,4},{6,7},{7,6},{8,9},{9,8},{10,11... | collective-permute-start | bytes 737288 | tf_op jit(solution)/shard_map/ppermute | solution.py:497

commit v3 on v2

--- a/solution.py
+++ b/solution.py
@@ -16,6 +16,9 @@
 LANES = 128
 WIDE = 2 * LANES
 HALF_ROOT3 = math.sqrt(3.0) / 2.0
+SPLIT_BATCH = 2
+JOIN_BATCH = 4
+LEVEL_BATCH = 4
 f32 = jnp.float32
 bf16 = jnp.bfloat16
 
@@ -145,7 +148,7 @@
     vmem = pl.BlockSpec(memory_space=pltpu.VMEM)
     hbm = pl.BlockSpec(memory_space=pltpu.HBM)
     assert lon < tiles * LANES
-    edge = jax.ShapeDtypeStruct((2 * levels * tiles, LANES), f32)
+    edge = pltpu.VMEM((2 * levels * tiles, LANES), f32)
     return pl.pallas_call(
         functools.partial(edge_kernel, lat_count),
         out_shape=[edge, edge, pltpu.VMEM((4, rows, LANES), f32), pltpu.VMEM((rows, LANES), f32)],
@@ -163,7 +166,7 @@
     )(in_hbm(winds), in_hbm(thick), in_hbm(cutoff))
 
 
-def forward(v, chunk, y, at, twiddle):
+def forward(v, chunk, twiddle):
     gap, half = LANES - chunk, RADIX // 2
     lane = lane_index(v[0].shape[0])
     c = []
@@ -173,6 +176,7 @@
         c.append(rolled(here, -turn))
     c[-1] = jnp.where(lane < chunk, c[-1], 0.0)
     (y0, y6), *pairs = split_radix(c)
+    found = []
     for k in range(half + 1):
         cos, sin = twiddle[0, 0, k : k + 1, :], twiddle[0, 1, k : k + 1, :]
         if k == 0:
@@ -182,10 +186,15 @@
         else:
             re, im = pairs[k - 1]
             both = (re * cos + im * sin, im * cos - re * sin)
-        for part, value in enumerate(both):
-            hi, lo = two_parts(value)
-            y[k, at, LANES * part : LANES * (part + 1)] = hi
-            y[k, at, WIDE + LANES * part : WIDE + LANES * (part + 1)] = lo
+        re, im = (two_parts(value) for value in both)
+        found.append((re[0], im[0], re[1], im[1]))
+    return found
+
+
+def put_parts(y, at, found):
+    for k, parts in enumerate(found):
+        for i, part in enumerate(parts):
+            y[k, at, LANES * i : LANES * (i + 1)] = part
 
 
 def three(high, low, tables):
@@ -265,15 +274,19 @@
 
 
         def split(n):
-            for f, l, start in members(n):
-                for g in range(rows // 16):
-                    at = pl.ds(start + 16 * g, 16)
-                    forward(own_tiles(f, l, rows_at(16 * g, 16)), chunk, y.at[n], at, twiddle)
+            todo = [(f, l, start, g) for f, l, start in members(n) for g in range(rows // 16)]
+            for i in range(0, len(todo), SPLIT_BATCH):
+                batch = todo[i : i + SPLIT_BATCH]
+                found = [forward(own_tiles(f, l, rows_at(16 * g, 16)), chunk, twiddle) for f, l, _, g in batch]
+                for (f, l, start, g), parts in zip(batch, found):
+                    put_parts(y.at[n], pl.ds(start + 16 * g, 16), parts)
 
         def join(n):
-            for f, l, start in members(n):
-                for g in range(rows // 8):
-                    v = backward(z.at[n], rows_at(start + 8 * g), chunk, twiddle)
+            todo = [(f, l, start, g) for f, l, start in members(n) for g in range(rows // 8)]
+            for i in range(0, len(todo), JOIN_BATCH):
+                batch = todo[i : i + JOIN_BATCH]
+                found = [backward(z.at[n], rows_at(start + 8 * g), chunk, twiddle) for _, _, start, g in batch]
+                for (f, l, _, g), v in zip(batch, found):
                     for j in range(tiles):
                         out[f, l, j, rows_at(1 + 8 * g), :] = v[j]
 
@@ -354,7 +367,7 @@
     @pl.when(filtering)
     def _():
         both = [jnp.concatenate(pair, axis=0) for pair in zip(edge_tiles(got_a), edge_tiles(got_b))]
-        forward(both, chunk, y, pl.ds(0, 16), twiddle)
+        put_parts(y, pl.ds(0, 16), forward(both, chunk, twiddle))
         wide = jnp.concatenate([keep, keep], axis=1)
         low_pass(lon, y, z, tables, wide)
         for side in range(2):
@@ -390,46 +403,45 @@
     return [jnp.where(lane > 0, a, b) for a, b in zip(r, r_before)]
 
 
-def thickness_kernel(lon, fields, trig, thick_hbm, thick, sem):
+def thickness_kernel(lon, fields, trig, thick):
     levels, tiles = fields.shape[1:3]
     rows = trig.shape[1]
     tail = lon - (tiles - 1) * LANES
-    copies = []
     for g in range(rows // 8):
         at = rows_at(8 * g)
         up, here, down = 8 * g, 8 * g + 1, 8 * g + 2
         south, north = trig[2, at, :], trig[3, at, :]
-        for l in range(levels):
-            u, h = ([fields[f, l, j, rows_at(here), :] for j in range(tiles)] for f in (0, 2))
-            he, ue = east(h), east(u)
-            flux = [(h[j] + he[j]) * (u[j] + ue[j]) for j in range(tiles)]
-            flux_west = west(flux, tail)
-            for j in range(tiles):
-                v_up, v, v_down = (fields[1, l, j, rows_at(r), :] for r in (up, here, down))
-                h_up, h_down = (fields[2, l, j, rows_at(r), :] for r in (up, down))
-                merid = (h[j] + h_down) * (v + v_down) * north - (h_up + h[j]) * (v_up + v) * south
-                new = h[j] - (0.25 * time_step) * (flux[j] - flux_west[j] + merid)
+        for start in range(0, levels, LEVEL_BATCH):
+            found = {}
+            for l in range(start, min(start + LEVEL_BATCH, levels)):
+                u, h = ([fields[f, l, j, rows_at(here), :] for j in range(tiles)] for f in (0, 2))
+                he, ue = east(h), east(u)
+                flux = [(h[j] + he[j]) * (u[j] + ue[j]) for j in range(tiles)]
+                flux_west = west(flux, tail)
+                for j in range(tiles):
+                    v_up, v, v_down = (fields[1, l, j, rows_at(r), :] for r in (up, here, down))
+                    h_up, h_down = (fields[2, l, j, rows_at(r), :] for r in (up, down))
+                    merid = (h[j] + h_down) * (v + v_down) * north - (h_up + h[j]) * (v_up + v) * south
+                    found[l, j] = h[j] - (0.25 * time_step) * (flux[j] - flux_west[j] + merid)
+            for (l, j), new in found.items():
                 wide = LANES if j < tiles - 1 else tail
                 thick[l, at, pl.ds(LANES * j, wide)] = new[:, :wide]
-        copies.append(pltpu.make_async_copy(thick.at[:, at], thick_hbm.at[:, at], sem.at[g]))
-        copies[-1].start()
-    for copy in copies:
-        copy.wait()
-
-
-def winds_kernel(lon, fields, trig, *refs):
-    *hops, winds_hbm, winds, sem = refs
+
+
+def winds_kernel(lon, fields, trig, thick, *refs):
+    *hops, winds_hbm, thick_hbm, winds, sem = refs
     levels, tiles = fields.shape[1:3]
     rows = trig.shape[1]
     tail = lon - (tiles - 1) * LANES
     place = lax.axis_index("lev")
     masks = [jnp.where(place + k + 1 <= len(hops), 1.0, 0.0) for k in range(len(hops))]
+    copies = [pltpu.make_async_copy(thick, thick_hbm, sem.at[rows // 8])]
+    copies[0].start()
 
     def below(j, at):
         terms = [ref[j, rows_at(at), :] * mask for ref, mask in zip(hops, masks)]
         return functools.reduce(jnp.add, terms) if terms else jnp.zeros((8, LANES), f32)
 
-    copies = []
     for g in range(rows // 8):
         at = rows_at(8 * g)
         up, here, down = 8 * g, 8 * g + 1, 8 * g + 2
@@ -437,6 +449,7 @@
         s = [below(j, here) for j in range(tiles)]
         sum_x = [a - b for a, b in zip(east(s), west(s, tail))]
         sum_y = [below(j, down) - below(j, up) for j in range(tiles)]
+        found = {}
         for l in reversed(range(levels)):
             h = [fields[2, l, j, rows_at(here), :] for j in range(tiles)]
             he, hw = east(h), west(h, tail)
@@ -448,28 +461,43 @@
                 new_v = v - time_step * (0.5 * cosine * (sum_y[j] + 0.5 * dy) + coriolis * sine * u)
                 sum_x[j] = sum_x[j] + dx
                 sum_y[j] = sum_y[j] + dy
-                wide = LANES if j < tiles - 1 else tail
-                to = pl.ds(LANES * j, wide)
-                winds[0, l, at, to] = new_u[:, :wide]
-                winds[1, l, at, to] = new_v[:, :wide]
+                found[l, j] = (new_u, new_v)
+            if l % LEVEL_BATCH == 0:
+                for (m, j), pair in found.items():
+                    wide = LANES if j < tiles - 1 else tail
+                    for f in range(2):
+                        winds[f, m, at, pl.ds(LANES * j, wide)] = pair[f][:, :wide]
+                found = {}
         copies.append(pltpu.make_async_copy(winds.at[:, :, at], winds_hbm.at[:, :, at], sem.at[g]))
         copies[-1].start()
     for copy in copies:
         copy.wait()
 
 
-def step_call(kernel, name, shape, flops, lon, operands):
-    rows = operands[1].shape[1]
+def stepped_thickness(fields, trig, shape, lon):
+    vmem = pl.BlockSpec(memory_space=pltpu.VMEM)
     return pl.pallas_call(
-        functools.partial(kernel, lon),
-        out_shape=jax.ShapeDtypeStruct(shape, f32),
-        in_specs=[pl.BlockSpec(memory_space=pltpu.VMEM)] * len(operands),
-        out_specs=pl.BlockSpec(memory_space=pltpu.HBM),
-        scratch_shapes=[pltpu.VMEM(shape, f32), pltpu.SemaphoreType.DMA((rows // 8,))],
+        functools.partial(thickness_kernel, lon),
+        out_shape=pltpu.VMEM(shape, f32),
+        in_specs=[vmem] * 2,
+        out_specs=vmem,
         compiler_params=pltpu.CompilerParams(vmem_limit_bytes=24 << 20),
-        cost_estimate=pl.CostEstimate(flops=flops, bytes_accessed=4_000_000, transcendentals=0),
-        name=name,
-    )(*operands)
+        cost_estimate=pl.CostEstimate(flops=4_000_000_000, bytes_accessed=4_000_000, transcendentals=0),
+        name="thickness",
+    )(fields, trig)
+
+
+def stepped_winds(fields, trig, thick, hops, shape, lon):
+    hbm = pl.BlockSpec(memory_space=pltpu.HBM)
+    return pl.pallas_call(
+        functools.partial(winds_kernel, lon),
+        out_shape=[jax.ShapeDtypeStruct(shape, f32), jax.ShapeDtypeStruct(thick.shape, f32)],
+        in_specs=[pl.BlockSpec(memory_space=pltpu.VMEM)] * (3 + len(hops)),
+        out_specs=[hbm, hbm],
+        scratch_shapes=[pltpu.VMEM(shape, f32), pltpu.SemaphoreType.DMA((trig.shape[1] // 8 + 1,))],
+        compiler_params=pltpu.CompilerParams(vmem_limit_bytes=24 << 20),
+        name="winds",
+    )(fields, trig, thick, *hops)
 
 
 def swaps(lat_count, lev_count, first):
@@ -497,9 +525,8 @@
         lax.ppermute(column, "lev", [(i, (i - hop) % lev_count) for i in range(lev_count)])
         for hop in range(1, lev_count)
     ]
-    new_thick = step_call(thickness_kernel, "thickness", thick.shape, 4_000_000_000, lon, (fields, trig))
-    new_winds = step_call(winds_kernel, "winds", winds.shape, 1_000_000_000, lon, (fields, trig, *hops))
-    return new_winds, new_thick
+    new_thick = stepped_thickness(fields, trig, thick.shape, lon)
+    return tuple(stepped_winds(fields, trig, new_thick, hops, winds.shape, lon))
 
 
 def solution(mesh):

time: 14.5 us -> 13.8 us (0.952)
  Pallas kernels: 6.63 us -> 5.93 us
    pallas_call x2, Pallas kernels: 3.63 us -> 2.93 us  [the longest x1 1.48 us: stepped_thickness(): pl.pallas_call(functools.partial(thickness_kernel, lon), out_shape=pltpu....]
  transfers between devices with their start and end apart: 3 -> 3, of which waited for: 1 -> 1; matrix products, arithmetic and copies ran while one was open for 0% -> 0% of each run, Pallas kernels for 23% -> 19%
where the time goes in v3:
time: 13.8 us; the launch traced here: 13.7 us
  Pallas kernels  5.93 us (43%)
  starting transfers between devices  4.54 us (33%)
  waiting for transfers between devices  2.48 us (18%)
  between operations  0.71 us (5%)
    ppermute x1, waiting for transfers between devices, per_device(): got_b = lax.ppermute(sent_b, ('lat', 'lev'), swaps(lat_count, lev_count, 1))  2.47 us
    ppermute x1, starting transfers between devices, per_device(): lax.ppermute(column, 'lev', [(i, (i - hop) % lev_count) for i in range(le...  2.17 us
    pallas_call x1, Pallas kernels, stepped_thickness(): pl.pallas_call(functools.partial(thickness_kernel, lon), out_shape=pltpu....  1.48 us
    pallas_call x1, Pallas kernels, stepped_winds(): pl.pallas_call(functools.partial(winds_kernel, lon), out_shape=[jax.Shape...  1.44 us
    ppermute x1, starting transfers between devices, per_device(): got_a = lax.ppermute(sent_a, ('lat', 'lev'), swaps(lat_count, lev_count, 0))  1.28 us
    pallas_call x1, Pallas kernels, filtered_fields(): pl.pallas_call(filter_kernel, out_shape=[pltpu.VMEM((3, levels, tiles, ro...  1.14 us
    ppermute x1, starting transfers between devices, per_device(): got_b = lax.ppermute(sent_b, ('lat', 'lev'), swaps(lat_count, lev_count, 1))  1.1 us
    pallas_call x1, Pallas kernels, edges(): pl.pallas_call(functools.partial(edge_kernel, lat_count), out_shape=[edge...  1.01 us
  transfers between devices with their start and end apart: 3, of which 1 were waited for; matrix products, arithmetic and copies ran while one was open for 0% of the time, Pallas kernels for 19%

profile of v3, /device:TPU:25, one launch (start us, length us, event | category | flops | bytes accessed | tf_op | source)
XLA Modules:
  0.0 13.7 jit_solution(8007615709685026722)
XLA Ops:
  0.6 0.0 copy-start
  0.6 0.0 copy-start.1
  0.7 0.0 copy-start.3
  0.7 0.0 copy-start.2
  0.7 1.0 %edges.1 = (f32[96,128]{1,0:T(8,128)S(1)}, f32[96,128]{1,0:T(8,128)S(1)}, f32[4,32,128]{2,1,0:T(8,128)S(1)}, f32[32,128]{1,0:T(8,128)S(1)}) custom-call(f32[2,4,32,1440]{3,2,1,0:T(8,128)} %winds.4, f32[4,32,1440]{2,1,0:T(8,128)} %thick.3, s32[32]{0:T(128)} %cutoff_hbm.1), custom_call_target="tpu_custom_call" | custom-call | flops 4000000000 | bytes 8000000 | tf_op jit(solution)/shard_map/edges/pallas_call | solution.py:152
  1.7 1.3 %collective-permute-start = (f32[96,128]{1,0:T(8,128)S(1)}, f32[96,128]{1,0:T(8,128)S(1)}, u32[]{:S(2)}, u32[]{:S(2)}) collective-permute-start(f32[96,128]{1,0:T(8,128)S(1)} %get-tuple-element.10), channel_id=1, source_target_pairs={{0,2},{1,3},{2,0},{3,1},{4,6},{5,7},{6,4},{7,5},{8,10},{9,11},{10,... | collective-permute-start | bytes 147464 | tf_op jit(solution)/shard_map/ppermute | solution.py:519
  3.0 1.1 %collective-permute-start.1 = (f32[96,128]{1,0:T(8,128)S(1)}, f32[96,128]{1,0:T(8,128)S(1)}, u32[]{:S(2)}, u32[]{:S(2)}) collective-permute-start(f32[96,128]{1,0:T(8,128)S(1)} %get-tuple-element.11), channel_id=1, source_target_pairs={{0,1},{1,0},{2,4},{3,5},{4,2},{5,3},{6,8},{7,9},{8,6},{9,7},{10,12... | collective-permute-start | bytes 147464 | tf_op jit(solution)/shard_map/ppermute | solution.py:520
  4.1 0.0 copy-done
  4.1 0.0 copy-done.1
  4.1 0.0 copy-done.3
  4.1 0.0 copy-done.2
  4.1 1.1 %filter.1 = (f32[3,4,12,40,128]{4,3,2,1,0:T(8,128)S(1)}, f32[12,40,128]{2,1,0:T(8,128)S(1)}) custom-call(f32[2,4,32,1440]{3,2,1,0:T(8,128)S(1)} %copy-done.2, f32[4,32,1440]{2,1,0:T(8,128)S(1)} %copy-done.3, bf16[2,256,256]{2,1,0:T(8,128)(2,1)S(1)} %copy-done, f32[2,2,8,128]{3,2,1,0:T(8,128)S(1)} %copy-done.1, f32[32,128]{1,0:T(8,128)S(1)} %get-tuple-element.12.cut), custom_call_target="tpu_custom_call" | custom-call | flops 10000000000 | bytes 8000000 | tf_op jit(solution)/shard_map/filter/pallas_call | solution.py:317
  5.2 0.0 collective-permute-done.got_a
  5.2 2.5 %collective-permute-done.1.got_b = f32[96,128]{1,0:T(8,128)S(1)} collective-permute-done((f32[96,128]{1,0:T(8,128)S(1)}, f32[96,128]{1,0:T(8,128)S(1)}, u32[]{:S(2)}, u32[]{:S(2)}) %collective-permute-start.1) | collective-permute-done | bytes 49184 | tf_op jit(solution)/shard_map/ppermute | solution.py:520
  7.7 0.9 %halo.1 = (f32[3,4,12,40,128]{4,3,2,1,0:T(8,128)S(1)}, f32[12,40,128]{2,1,0:T(8,128)S(1)}) custom-call(f32[96,128]{1,0:T(8,128)S(1)} %collective-permute-done.got_a, f32[96,128]{1,0:T(8,128)S(1)} %collective-permute-done.1.got_b, bf16[2,256,256]{2,1,0:T(8,128)(2,1)S(1)} %copy-done, ...), custom_call_target="tpu_custom_call", output_to_operand_aliasing={{0}: (4, {}), {1}: (5, {})} | custom-call | tf_op jit(solution)/shard_map/halo/pallas_call | solution.py:381
  8.6 2.2 %collective-permute-start.2 = (f32[12,40,128]{2,1,0:T(8,128)S(1)}, f32[12,40,128]{2,1,0:T(8,128)S(1)}, u32[]{:S(2)}, u32[]{:S(2)}) collective-permute-start(f32[12,40,128]{2,1,0:T(8,128)S(1)} %get-tuple-element.17), channel_id=1, source_target_pairs={{0,1},{1,0},{2,3},{3,2},{4,5},{5,4},{6,7},{7,6},{8,9},{9,8},{10,11... | collective-permute-start | bytes 737288 | tf_op jit(solution)/shard_map/ppermute | solution.py:525
  10.7 1.5 %thickness.1.thick = f32[4,32,1440]{2,1,0:T(8,128)S(1)} custom-call(f32[3,4,12,40,128]{4,3,2,1,0:T(8,128)S(1)} %get-tuple-element.15.fields, f32[4,32,128]{2,1,0:T(8,128)S(1)} %get-tuple-element.16.trig), custom_call_target="tpu_custom_call" | custom-call | flops 4000000000 | bytes 4000000 | tf_op jit(solution)/shard_map/thickness/pallas_call | solution.py:479
  12.2 0.0 collective-permute-done.2.refs_0_
  12.2 1.4 %winds.5 = (f32[2,4,32,1440]{3,2,1,0:T(8,128)}, f32[4,32,1440]{2,1,0:T(8,128)}) custom-call(f32[3,4,12,40,128]{4,3,2,1,0:T(8,128)S(1)} %get-tuple-element.15.fields, f32[4,32,128]{2,1,0:T(8,128)S(1)} %get-tuple-element.16.trig, f32[4,32,1440]{2,1,0:T(8,128)S(1)} %thickness.1.thick, f32[12,40,128]{2,1,0:T(8,128)S(1)} %collective-permute-done.2.refs_0_), custom_call_target="tpu_custom_call" | custom-call | tf_op jit(solution)/shard_map/winds/pallas_call | solution.py:492
Async XLA Ops:
  0.6 3.4 %copy-start = (bf16[2,256,256]{2,1,0:T(8,128)(2,1)S(1)}, bf16[2,256,256]{2,1,0:T(8,128)(2,1)}, u32[]{:S(2)}) copy-start(bf16[2,256,256]{2,1,0:T(8,128)(2,1)} %constant.4.clone.tables) | copy-start | bytes 786436
  0.6 3.4 %copy-start.1 = (f32[2,2,8,128]{3,2,1,0:T(8,128)S(1)}, f32[2,2,8,128]{3,2,1,0:T(8,128)}, u32[]{:S(2)}) copy-start(f32[2,2,8,128]{3,2,1,0:T(8,128)} %constant.5.clone.twiddle) | copy-start | bytes 49156
  0.7 3.4 %copy-start.3 = (f32[4,32,1440]{2,1,0:T(8,128)S(1)}, f32[4,32,1440]{2,1,0:T(8,128)}, u32[]{:S(2)}) copy-start(f32[4,32,1440]{2,1,0:T(8,128)} %thick.3) | copy-start | bytes 2211844
  0.7 3.4 %copy-start.2 = (f32[2,4,32,1440]{3,2,1,0:T(8,128)S(1)}, f32[2,4,32,1440]{3,2,1,0:T(8,128)}, u32[]{:S(2)}) copy-start(f32[2,4,32,1440]{3,2,1,0:T(8,128)} %winds.4) | copy-start | bytes 4423684
  1.7 3.5 %collective-permute-start = (f32[96,128]{1,0:T(8,128)S(1)}, f32[96,128]{1,0:T(8,128)S(1)}, u32[]{:S(2)}, u32[]{:S(2)}) collective-permute-start(f32[96,128]{1,0:T(8,128)S(1)} %get-tuple-element.10), channel_id=1, source_target_pairs={{0,2},{1,3},{2,0},{3,1},{4,6},{5,7},{6,4},{7,5},{8,10},{9,11},{10,... | collective-permute-start | bytes 147464 | tf_op jit(solution)/shard_map/ppermute | solution.py:519
  3.0 4.7 %collective-permute-start.1 = (f32[96,128]{1,0:T(8,128)S(1)}, f32[96,128]{1,0:T(8,128)S(1)}, u32[]{:S(2)}, u32[]{:S(2)}) collective-permute-start(f32[96,128]{1,0:T(8,128)S(1)} %get-tuple-element.11), channel_id=1, source_target_pairs={{0,1},{1,0},{2,4},{3,5},{4,2},{5,3},{6,8},{7,9},{8,6},{9,7},{10,12... | collective-permute-start | bytes 147464 | tf_op jit(solution)/shard_map/ppermute | solution.py:520
  8.6 3.7 %collective-permute-start.2 = (f32[12,40,128]{2,1,0:T(8,128)S(1)}, f32[12,40,128]{2,1,0:T(8,128)S(1)}, u32[]{:S(2)}, u32[]{:S(2)}) collective-permute-start(f32[12,40,128]{2,1,0:T(8,128)S(1)} %get-tuple-element.17), channel_id=1, source_target_pairs={{0,1},{1,0},{2,3},{3,2},{4,5},{5,4},{6,7},{7,6},{8,9},{9,8},{10,11... | collective-permute-start | bytes 737288 | tf_op jit(solution)/shard_map/ppermute | solution.py:525

commit v4 on v3

--- a/solution.py
+++ b/solution.py
@@ -235,7 +235,7 @@
     return v[:-1] + [jnp.where(lane_index() < tail, v[-1], rolled(v[0], LANES - tail))]
 
 
-def filter_kernel(winds, thick, tables, twiddle, cut, out, column, y, z):
+def filter_kernel(winds, thick, tables, twiddle, cut, trig, out, column, new_thick, y, z):
     levels, rows, lon = thick.shape
     tiles = out.shape[2]
     chunk = lon // RADIX
@@ -262,6 +262,8 @@
                 return 0
 
             lax.fori_loop(0, levels, as_is, 0)
+        for g in range(1, rows // 8 - 1):
+            thickness_rows(g, lon, out, trig, new_thick)
 
     @pl.when(filtering)
     def _():
@@ -304,7 +306,7 @@
         column[j, at, :] = functools.reduce(jnp.add, [out[2, l, j, at, :] for l in range(levels)])
 
 
-def filtered_fields(winds, thick, cut, tables, twiddle):
+def filtered_fields(winds, thick, cut, trig, tables, twiddle):
     levels, rows, lon = thick.shape
     tiles = -(-lon // LANES)
     assert lon % RADIX == 0 and lon // RADIX <= LANES and tiles == RADIX
@@ -319,9 +321,10 @@
         out_shape=[
             pltpu.VMEM((3, levels, tiles, rows + 8, LANES), f32),
             pltpu.VMEM((tiles, rows + 8, LANES), f32),
+            pltpu.VMEM(thick.shape, f32),
         ],
-        in_specs=[vmem] * 5,
-        out_specs=[vmem] * 2,
+        in_specs=[vmem] * 6,
+        out_specs=[vmem] * 3,
         scratch_shapes=[
             pltpu.VMEM((units, classes, per * rows, 2 * WIDE), bf16),
             pltpu.VMEM((units, classes, per * rows, WIDE), f32),
@@ -329,7 +332,7 @@
         compiler_params=pltpu.CompilerParams(vmem_limit_bytes=24 << 20),
         cost_estimate=pl.CostEstimate(flops=10_000_000_000, bytes_accessed=8_000_000, transcendentals=0),
         name="filter",
-    )(in_vmem(winds), in_vmem(thick), in_vmem(tables), in_vmem(twiddle), cut)
+    )(in_vmem(winds), in_vmem(thick), in_vmem(tables), in_vmem(twiddle), cut, trig)
 
 
 def halo_kernel(lon, lat_count, got_a, got_b, tables, twiddle, _fields, _column, out, column, y, z):
@@ -403,29 +406,38 @@
     return [jnp.where(lane > 0, a, b) for a, b in zip(r, r_before)]
 
 
-def thickness_kernel(lon, fields, trig, thick):
+def thickness_rows(g, lon, fields, trig, thick):
     levels, tiles = fields.shape[1:3]
-    rows = trig.shape[1]
     tail = lon - (tiles - 1) * LANES
-    for g in range(rows // 8):
-        at = rows_at(8 * g)
-        up, here, down = 8 * g, 8 * g + 1, 8 * g + 2
-        south, north = trig[2, at, :], trig[3, at, :]
-        for start in range(0, levels, LEVEL_BATCH):
-            found = {}
-            for l in range(start, min(start + LEVEL_BATCH, levels)):
-                u, h = ([fields[f, l, j, rows_at(here), :] for j in range(tiles)] for f in (0, 2))
-                he, ue = east(h), east(u)
-                flux = [(h[j] + he[j]) * (u[j] + ue[j]) for j in range(tiles)]
-                flux_west = west(flux, tail)
-                for j in range(tiles):
-                    v_up, v, v_down = (fields[1, l, j, rows_at(r), :] for r in (up, here, down))
-                    h_up, h_down = (fields[2, l, j, rows_at(r), :] for r in (up, down))
-                    merid = (h[j] + h_down) * (v + v_down) * north - (h_up + h[j]) * (v_up + v) * south
-                    found[l, j] = h[j] - (0.25 * time_step) * (flux[j] - flux_west[j] + merid)
-            for (l, j), new in found.items():
-                wide = LANES if j < tiles - 1 else tail
-                thick[l, at, pl.ds(LANES * j, wide)] = new[:, :wide]
+    at = rows_at(8 * g)
+    up, mid, down = 8 * g, 8 * g + 1, 8 * g + 2
+    south, north = trig[2, at, :], trig[3, at, :]
+    found = {}
+    for l in range(levels):
+        u, h = ([fields[f, l, j, rows_at(mid), :] for j in range(tiles)] for f in (0, 2))
+        he, ue = east(h), east(u)
+        flux = [(h[j] + he[j]) * (u[j] + ue[j]) for j in range(tiles)]
+        flux_west = west(flux, tail)
+        for j in range(tiles):
+            v_up, v, v_down = (fields[1, l, j, rows_at(r), :] for r in (up, mid, down))
+            h_up, h_down = (fields[2, l, j, rows_at(r), :] for r in (up, down))
+            merid = (h[j] + h_down) * (v + v_down) * north - (h_up + h[j]) * (v_up + v) * south
+            found[l, j] = h[j] - (0.25 * time_step) * (flux[j] - flux_west[j] + merid)
+    for (l, j), new in found.items():
+        wide = LANES if j < tiles - 1 else tail
+        thick[l, at, pl.ds(LANES * j, wide)] = new[:, :wide]
+
+
+def thickness_kernel(lon, fields, trig, cut, _thick, thick):
+    groups = trig.shape[1] // 8
+
+    @pl.when(jnp.min(cut[...]) < lon // 2)
+    def _():
+        for g in range(1, groups - 1):
+            thickness_rows(g, lon, fields, trig, thick)
+
+    for g in sorted({0, groups - 1}):
+        thickness_rows(g, lon, fields, trig, thick)
 
 
 def winds_kernel(lon, fields, trig, thick, *refs):
@@ -474,17 +486,18 @@
         copy.wait()
 
 
-def stepped_thickness(fields, trig, shape, lon):
+def stepped_thickness(fields, trig, cut, thick, lon):
     vmem = pl.BlockSpec(memory_space=pltpu.VMEM)
     return pl.pallas_call(
         functools.partial(thickness_kernel, lon),
-        out_shape=pltpu.VMEM(shape, f32),
-        in_specs=[vmem] * 2,
+        out_shape=pltpu.VMEM(thick.shape, f32),
+        in_specs=[vmem] * 4,
         out_specs=vmem,
+        input_output_aliases={3: 0},
         compiler_params=pltpu.CompilerParams(vmem_limit_bytes=24 << 20),
         cost_estimate=pl.CostEstimate(flops=4_000_000_000, bytes_accessed=4_000_000, transcendentals=0),
         name="thickness",
-    )(fields, trig)
+    )(fields, trig, cut, thick)
 
 
 def stepped_winds(fields, trig, thick, hops, shape, lon):
@@ -519,13 +532,13 @@
     got_a = lax.ppermute(sent_a, ("lat", "lev"), swaps(lat_count, lev_count, 0))
     got_b = lax.ppermute(sent_b, ("lat", "lev"), swaps(lat_count, lev_count, 1))
     tables, twiddle = (jnp.asarray(constant) for constant in filter_tables(lon))
-    fields, column = filtered_fields(winds, thick, cut, tables, twiddle)
+    fields, column, new_thick = filtered_fields(winds, thick, cut, trig, tables, twiddle)
     fields, column = with_halo(fields, column, tables, twiddle, got_a, got_b, lon, lat_count)
     hops = [
         lax.ppermute(column, "lev", [(i, (i - hop) % lev_count) for i in range(lev_count)])
         for hop in range(1, lev_count)
     ]
-    new_thick = stepped_thickness(fields, trig, thick.shape, lon)
+    new_thick = stepped_thickness(fields, trig, cut, new_thick, lon)
     return tuple(stepped_winds(fields, trig, new_thick, hops, winds.shape, lon))
 
 

time: 13.8 us -> 13.5 us (0.978)
  waiting for transfers between devices: 2.48 us -> 2.08 us
    ppermute x1, waiting for transfers between devices: 2.47 us -> 1.76 us  [per_device(): got_b = lax.ppermute(sent_b, ('lat', 'lev'), swaps(lat_count, lev_count, 1))]
    pallas_call x1, Pallas kernels: 1.14 us -> 1.85 us  [filtered_fields(): pl.pallas_call(filter_kernel, out_shape=[pltpu.VMEM((3, levels, tiles, ro...]
    pallas_call x1, Pallas kernels: 1.48 us -> 0.82 us  [stepped_thickness(): pl.pallas_call(functools.partial(thickness_kernel, lon), out_shape=pltpu....]
    ppermute x1, waiting for transfers between devices: 0.01 us -> 0.31 us  [per_device(): lax.ppermute(column, 'lev', [(i, (i - hop) % lev_count) for i in range(le...]
  transfers between devices with their start and end apart: 3 -> 3, of which waited for: 1 -> 2; matrix products, arithmetic and copies ran while one was open for 0% -> 0% of each run, Pallas kernels for 19% -> 20%
where the time goes in v4:
time: 13.5 us; the launch traced here: 13.3 us
  Pallas kernels  5.97 us (44%)
  starting transfers between devices  4.54 us (34%)
  waiting for transfers between devices  2.08 us (15%)
  between operations  0.71 us (5%)
    ppermute x1, starting transfers between devices, per_device(): lax.ppermute(column, 'lev', [(i, (i - hop) % lev_count) for i in range(le...  2.17 us
    pallas_call x1, Pallas kernels, filtered_fields(): pl.pallas_call(filter_kernel, out_shape=[pltpu.VMEM((3, levels, tiles, ro...  1.85 us
    ppermute x1, waiting for transfers between devices, per_device(): got_b = lax.ppermute(sent_b, ('lat', 'lev'), swaps(lat_count, lev_count, 1))  1.76 us
    pallas_call x1, Pallas kernels, stepped_winds(): pl.pallas_call(functools.partial(winds_kernel, lon), out_shape=[jax.Shape...  1.44 us
    ppermute x1, starting transfers between devices, per_device(): got_a = lax.ppermute(sent_a, ('lat', 'lev'), swaps(lat_count, lev_count, 0))  1.28 us
    ppermute x1, starting transfers between devices, per_device(): got_b = lax.ppermute(sent_b, ('lat', 'lev'), swaps(lat_count, lev_count, 1))  1.1 us
    pallas_call x1, Pallas kernels, edges(): pl.pallas_call(functools.partial(edge_kernel, lat_count), out_shape=[edge...  1.01 us
    pallas_call x1, Pallas kernels, with_halo(): pl.pallas_call(functools.partial(halo_kernel, lon, lat_count), out_shape=...  0.85 us
  transfers between devices with their start and end apart: 3, of which 2 were waited for; matrix products, arithmetic and copies ran while one was open for 0% of the time, Pallas kernels for 20%

profile of v4, /device:TPU:25, one launch (start us, length us, event | category | flops | bytes accessed | tf_op | source)
XLA Modules:
  0.0 13.3 jit_solution(17058190966591862648)
XLA Ops:
  0.6 0.0 copy-start
  0.6 0.0 copy-start.1
  0.7 0.0 copy-start.3
  0.7 0.0 copy-start.2
  0.7 1.0 %edges.1 = (f32[96,128]{1,0:T(8,128)S(1)}, f32[96,128]{1,0:T(8,128)S(1)}, f32[4,32,128]{2,1,0:T(8,128)S(1)}, f32[32,128]{1,0:T(8,128)S(1)}) custom-call(f32[2,4,32,1440]{3,2,1,0:T(8,128)} %winds.4, f32[4,32,1440]{2,1,0:T(8,128)} %thick.3, s32[32]{0:T(128)} %cutoff_hbm.1), custom_call_target="tpu_custom_call" | custom-call | flops 4000000000 | bytes 8000000 | tf_op jit(solution)/shard_map/edges/pallas_call | solution.py:152
  1.7 1.3 %collective-permute-start = (f32[96,128]{1,0:T(8,128)S(1)}, f32[96,128]{1,0:T(8,128)S(1)}, u32[]{:S(2)}, u32[]{:S(2)}) collective-permute-start(f32[96,128]{1,0:T(8,128)S(1)} %get-tuple-element.11), channel_id=1, source_target_pairs={{0,2},{1,3},{2,0},{3,1},{4,6},{5,7},{6,4},{7,5},{8,10},{9,11},{10,... | collective-permute-start | bytes 147464 | tf_op jit(solution)/shard_map/ppermute | solution.py:532
  3.0 1.1 %collective-permute-start.1 = (f32[96,128]{1,0:T(8,128)S(1)}, f32[96,128]{1,0:T(8,128)S(1)}, u32[]{:S(2)}, u32[]{:S(2)}) collective-permute-start(f32[96,128]{1,0:T(8,128)S(1)} %get-tuple-element.12), channel_id=1, source_target_pairs={{0,1},{1,0},{2,4},{3,5},{4,2},{5,3},{6,8},{7,9},{8,6},{9,7},{10,12... | collective-permute-start | bytes 147464 | tf_op jit(solution)/shard_map/ppermute | solution.py:533
  4.1 0.0 copy-done
  4.1 0.0 copy-done.1
  4.1 0.0 copy-done.3
  4.1 0.0 copy-done.2
  4.1 1.8 %filter.1 = (f32[3,4,12,40,128]{4,3,2,1,0:T(8,128)S(1)}, f32[12,40,128]{2,1,0:T(8,128)S(1)}, f32[4,32,1440]{2,1,0:T(8,128)S(1)}) custom-call(f32[2,4,32,1440]{3,2,1,0:T(8,128)S(1)} %copy-done.2, f32[4,32,1440]{2,1,0:T(8,128)S(1)} %copy-done.3, bf16[2,256,256]{2,1,0:T(8,128)(2,1)S(1)} %copy-done, f32[2,2,8,128]{3,2,1,0:T(8,128)S(1)} %copy-done.1, ...), custom_call_target="tpu_custom_call" | custom-call | flops 10000000000 | bytes 8000000 | tf_op jit(solution)/shard_map/filter/pallas_call | solution.py:319
  5.9 0.0 collective-permute-done.got_a
  5.9 1.8 %collective-permute-done.1.got_b = f32[96,128]{1,0:T(8,128)S(1)} collective-permute-done((f32[96,128]{1,0:T(8,128)S(1)}, f32[96,128]{1,0:T(8,128)S(1)}, u32[]{:S(2)}, u32[]{:S(2)}) %collective-permute-start.1) | collective-permute-done | bytes 49184 | tf_op jit(solution)/shard_map/ppermute | solution.py:533
  7.7 0.9 %halo.1 = (f32[3,4,12,40,128]{4,3,2,1,0:T(8,128)S(1)}, f32[12,40,128]{2,1,0:T(8,128)S(1)}) custom-call(f32[96,128]{1,0:T(8,128)S(1)} %collective-permute-done.got_a, f32[96,128]{1,0:T(8,128)S(1)} %collective-permute-done.1.got_b, bf16[2,256,256]{2,1,0:T(8,128)(2,1)S(1)} %copy-done, ...), custom_call_target="tpu_custom_call", output_to_operand_aliasing={{0}: (4, {}), {1}: (5, {})} | custom-call | tf_op jit(solution)/shard_map/halo/pallas_call | solution.py:384
  8.6 2.2 %collective-permute-start.2 = (f32[12,40,128]{2,1,0:T(8,128)S(1)}, f32[12,40,128]{2,1,0:T(8,128)S(1)}, u32[]{:S(2)}, u32[]{:S(2)}) collective-permute-start(f32[12,40,128]{2,1,0:T(8,128)S(1)} %get-tuple-element.19), channel_id=1, source_target_pairs={{0,1},{1,0},{2,3},{3,2},{4,5},{5,4},{6,7},{7,6},{8,9},{9,8},{10,11... | collective-permute-start | bytes 737288 | tf_op jit(solution)/shard_map/ppermute | solution.py:538
  10.7 0.8 %thickness.1.thick = f32[4,32,1440]{2,1,0:T(8,128)S(1)} custom-call(f32[3,4,12,40,128]{4,3,2,1,0:T(8,128)S(1)} %get-tuple-element.17.fields, f32[4,32,128]{2,1,0:T(8,128)S(1)} %get-tuple-element.14.trig, f32[32,128]{1,0:T(8,128)S(1)} %get-tuple-element.13.cut, f32[4,32,1440]{2,1,0:T(8,128)S(1)} %get-tuple-element.18._thick), custom_call_target="tpu_custom_call", output_to_operand_aliasing={{}: (3, {})} | custom-call | flops 4000000000 | bytes 4000000 | tf_op jit(solution)/shard_map/thickness/pallas_call | solution.py:491
  11.6 0.3 %collective-permute-done.2.refs_0_ = f32[12,40,128]{2,1,0:T(8,128)S(1)} collective-permute-done((f32[12,40,128]{2,1,0:T(8,128)S(1)}, f32[12,40,128]{2,1,0:T(8,128)S(1)}, u32[]{:S(2)}, u32[]{:S(2)}) %collective-permute-start.2) | collective-permute-done | bytes 245792 | tf_op jit(solution)/shard_map/ppermute | solution.py:538
  11.9 1.4 %winds.5 = (f32[2,4,32,1440]{3,2,1,0:T(8,128)}, f32[4,32,1440]{2,1,0:T(8,128)}) custom-call(f32[3,4,12,40,128]{4,3,2,1,0:T(8,128)S(1)} %get-tuple-element.17.fields, f32[4,32,128]{2,1,0:T(8,128)S(1)} %get-tuple-element.14.trig, f32[4,32,1440]{2,1,0:T(8,128)S(1)} %thickness.1.thick, f32[12,40,128]{2,1,0:T(8,128)S(1)} %collective-permute-done.2.refs_0_), custom_call_target="tpu_custom_call" | custom-call | tf_op jit(solution)/shard_map/winds/pallas_call | solution.py:505
Async XLA Ops:
  0.6 3.4 %copy-start = (bf16[2,256,256]{2,1,0:T(8,128)(2,1)S(1)}, bf16[2,256,256]{2,1,0:T(8,128)(2,1)}, u32[]{:S(2)}) copy-start(bf16[2,256,256]{2,1,0:T(8,128)(2,1)} %constant.4.clone.tables) | copy-start | bytes 786436
  0.6 3.4 %copy-start.1 = (f32[2,2,8,128]{3,2,1,0:T(8,128)S(1)}, f32[2,2,8,128]{3,2,1,0:T(8,128)}, u32[]{:S(2)}) copy-start(f32[2,2,8,128]{3,2,1,0:T(8,128)} %constant.5.clone.twiddle) | copy-start | bytes 49156
  0.7 3.4 %copy-start.3 = (f32[4,32,1440]{2,1,0:T(8,128)S(1)}, f32[4,32,1440]{2,1,0:T(8,128)}, u32[]{:S(2)}) copy-start(f32[4,32,1440]{2,1,0:T(8,128)} %thick.3) | copy-start | bytes 2211844
  0.7 3.4 %copy-start.2 = (f32[2,4,32,1440]{3,2,1,0:T(8,128)S(1)}, f32[2,4,32,1440]{3,2,1,0:T(8,128)}, u32[]{:S(2)}) copy-start(f32[2,4,32,1440]{3,2,1,0:T(8,128)} %winds.4) | copy-start | bytes 4423684
  1.7 4.2 %collective-permute-start = (f32[96,128]{1,0:T(8,128)S(1)}, f32[96,128]{1,0:T(8,128)S(1)}, u32[]{:S(2)}, u32[]{:S(2)}) collective-permute-start(f32[96,128]{1,0:T(8,128)S(1)} %get-tuple-element.11), channel_id=1, source_target_pairs={{0,2},{1,3},{2,0},{3,1},{4,6},{5,7},{6,4},{7,5},{8,10},{9,11},{10,... | collective-permute-start | bytes 147464 | tf_op jit(solution)/shard_map/ppermute | solution.py:532
  3.0 4.7 %collective-permute-start.1 = (f32[96,128]{1,0:T(8,128)S(1)}, f32[96,128]{1,0:T(8,128)S(1)}, u32[]{:S(2)}, u32[]{:S(2)}) collective-permute-start(f32[96,128]{1,0:T(8,128)S(1)} %get-tuple-element.12), channel_id=1, source_target_pairs={{0,1},{1,0},{2,4},{3,5},{4,2},{5,3},{6,8},{7,9},{8,6},{9,7},{10,12... | collective-permute-start | bytes 147464 | tf_op jit(solution)/shard_map/ppermute | solution.py:533
  8.6 3.3 %collective-permute-start.2 = (f32[12,40,128]{2,1,0:T(8,128)S(1)}, f32[12,40,128]{2,1,0:T(8,128)S(1)}, u32[]{:S(2)}, u32[]{:S(2)}) collective-permute-start(f32[12,40,128]{2,1,0:T(8,128)S(1)} %get-tuple-element.19), channel_id=1, source_target_pairs={{0,1},{1,0},{2,3},{3,2},{4,5},{5,4},{6,7},{7,6},{8,9},{9,8},{10,11... | collective-permute-start | bytes 737288 | tf_op jit(solution)/shard_map/ppermute | solution.py:538

commit v5 on v4

--- a/solution.py
+++ b/solution.py
@@ -16,8 +16,6 @@
 LANES = 128
 WIDE = 2 * LANES
 HALF_ROOT3 = math.sqrt(3.0) / 2.0
-SPLIT_BATCH = 2
-JOIN_BATCH = 4
 LEVEL_BATCH = 4
 f32 = jnp.float32
 bf16 = jnp.bfloat16
@@ -203,19 +201,27 @@
     return lax.dot_general(a, b, (((1,), (0,)), ((), ())), preferred_element_type=f32)
 
 
-def low_pass(lon, y, z, tables, keep):
+def products(y, tables):
     classes, count = y.shape[:2]
-    shape = (classes, count, WIDE)
     both = y[...].reshape(classes * count, 2 * WIDE)
-    coeffs = three(both[:, :WIDE], both[:, WIDE:], tables).reshape(shape)
+    return three(both[:, :WIDE], both[:, WIDE:], tables).reshape(classes, count, WIDE)
+
+
+def masked_parts(lon, coeffs, keep):
     at = lax.broadcasted_iota(jnp.int32, (1, WIDE), 1)
     at = jnp.where(at < LANES, at, at - LANES)
-    masked = []
-    for k in range(classes):
+    found = []
+    for k in range(coeffs.shape[0]):
         m = RADIX * at + k
-        masked.append(jnp.where(jnp.minimum(m, lon - m).astype(f32) <= keep, coeffs[k], 0.0))
-    high, low = two_parts(jnp.concatenate(masked, axis=0))
-    z[...] = three(high, low, tables).reshape(shape)
+        inside = jnp.minimum(m, lon - m).astype(f32) <= keep
+        found.append(two_parts(jnp.where(inside, coeffs[k], 0.0)))
+    return found
+
+
+def put_masked(y, found):
+    for k, parts in enumerate(found):
+        for i, part in enumerate(parts):
+            y[k, :, WIDE * i : WIDE * (i + 1)] = part
 
 
 def backward(z, at, chunk, twiddle):
@@ -263,7 +269,7 @@
 
             lax.fori_loop(0, levels, as_is, 0)
         for g in range(1, rows // 8 - 1):
-            thickness_rows(g, lon, out, trig, new_thick)
+            thickness_rows(g, lon, out, None, trig, new_thick)
 
     @pl.when(filtering)
     def _():
@@ -276,34 +282,38 @@
 
 
         def split(n):
-            todo = [(f, l, start, g) for f, l, start in members(n) for g in range(rows // 16)]
-            for i in range(0, len(todo), SPLIT_BATCH):
-                batch = todo[i : i + SPLIT_BATCH]
-                found = [forward(own_tiles(f, l, rows_at(16 * g, 16)), chunk, twiddle) for f, l, _, g in batch]
-                for (f, l, start, g), parts in zip(batch, found):
-                    put_parts(y.at[n], pl.ds(start + 16 * g, 16), parts)
+            found = []
+            for f, l, start in members(n):
+                for g in range(rows // 16):
+                    parts = forward(own_tiles(f, l, rows_at(16 * g, 16)), chunk, twiddle)
+                    found.append((pl.ds(start + 16 * g, 16), parts))
+            return found
 
         def join(n):
-            todo = [(f, l, start, g) for f, l, start in members(n) for g in range(rows // 8)]
-            for i in range(0, len(todo), JOIN_BATCH):
-                batch = todo[i : i + JOIN_BATCH]
-                found = [backward(z.at[n], rows_at(start + 8 * g), chunk, twiddle) for _, _, start, g in batch]
-                for (f, l, _, g), v in zip(batch, found):
-                    for j in range(tiles):
-                        out[f, l, j, rows_at(1 + 8 * g), :] = v[j]
-
-        split(0)
-        for n in range(units):
-            low_pass(lon, y.at[n], z.at[n], tables, wide)
-            if n + 1 < units:
-                split(n + 1)
-            if n > 0:
-                join(n - 1)
-        join(units - 1)
-
-    at = pl.ds(1, rows)
+            found = []
+            for f, l, start in members(n):
+                for g in range(rows // 8):
+                    found.append((f, l, g, backward(z.at[n], rows_at(start + 8 * g), chunk, twiddle)))
+            return found
+
+        for n in range(-1, units + 2):
+            coeffs = products(y.at[n], tables) if 0 <= n < units else None
+            back = products(y.at[n - 1], tables) if 1 <= n <= units else None
+            ahead = split(n + 1) if n + 1 < units else []
+            behind = join(n - 2) if n >= 2 else []
+            masked = masked_parts(lon, coeffs, wide) if 0 <= n < units else []
+            put_masked(y.at[n], masked)
+            if back is not None:
+                z[n - 1] = back
+            for at, parts in ahead:
+                put_parts(y.at[n + 1], at, parts)
+            for f, l, g, v in behind:
+                for j in range(tiles):
+                    out[f, l, j, rows_at(1 + 8 * g), :] = v[j]
+
     for j in range(tiles):
-        column[j, at, :] = functools.reduce(jnp.add, [out[2, l, j, at, :] for l in range(levels)])
+        lines = [out[2, l, j, pl.ds(1, rows), :] for l in range(levels)]
+        column[j, pl.ds(0, rows), :] = functools.reduce(jnp.add, lines)
 
 
 def filtered_fields(winds, thick, cut, trig, tables, twiddle):
@@ -312,7 +322,7 @@
     assert lon % RADIX == 0 and lon // RADIX <= LANES and tiles == RADIX
     assert rows % 16 == 0 and levels % 2 == 0
     classes = RADIX // 2 + 1
-    per = 2
+    per = 1
     units = 3 * levels // per
     vmem = pl.BlockSpec(memory_space=pltpu.VMEM)
     hbm = pl.BlockSpec(memory_space=pltpu.HBM)
@@ -335,62 +345,72 @@
     )(in_vmem(winds), in_vmem(thick), in_vmem(tables), in_vmem(twiddle), cut, trig)
 
 
-def halo_kernel(lon, lat_count, got_a, got_b, tables, twiddle, _fields, _column, out, column, y, z):
-    levels, tiles, rows = out.shape[1], out.shape[2], out.shape[3] - 8
+def halo_kernel(lon, lat_count, got_a, got_b, tables, twiddle, _column, halo, column, y, z):
+    tiles, rows = column.shape[0], column.shape[1] - 8
+    levels = got_a.shape[0] // (2 * tiles)
     chunk = lon // RADIX
     tail = lon - (tiles - 1) * LANES
     place = lax.axis_index("lat")
-    odd = place % 2
+    odd = place % 2 == 1
     refs = (got_a, got_b)
-    at = (jnp.where(odd == 1, 0, rows + 1), jnp.where(odd == 1, rows + 1, 0))
     keep = jnp.concatenate([ref[rows_at(2 * levels * (tiles - 1), 2 * levels), :] for ref in refs], axis=0)
     keep = jnp.where(lane_index(16) < tail, rolled(keep, tail), keep)
+    row = lax.broadcasted_iota(jnp.int32, (8, LANES), 0)
 
     def edge_tiles(ref):
         v = [ref[rows_at(2 * levels * j, 2 * levels), :] for j in range(tiles)]
         return v[:-1] + [jnp.where(lane_index() < tail, v[-1], 0.0)]
 
-    def put(side, v):
-        end = jnp.where(at[side] == 0, place == 0, place == lat_count - 1)
+    def put(v_a, v_b):
         for j in range(tiles):
-            value = jnp.where(end, 0.0, v[j])
-            for f in range(2):
-                lines = [value[f * levels + l : f * levels + l + 1] for l in range(levels)]
-                for l in range(levels):
-                    out[1 + f, l, j, pl.ds(at[side], 1), :] = lines[l]
-            column[j, pl.ds(at[side], 1), :] = functools.reduce(jnp.add, lines)
+            before = jnp.where(place == 0, 0.0, jnp.where(odd, v_a[j], v_b[j]))
+            after = jnp.where(place == lat_count - 1, 0.0, jnp.where(odd, v_b[j], v_a[j]))
+            halo[0, j], halo[1, j] = before, after
+            column[j, rows_at(rows), :] = jnp.where(row < levels, pltpu.roll(before, levels, 0), after)
 
     filtering = jnp.min(keep) < lon // 2
 
     @pl.when(jnp.logical_not(filtering))
     def _():
-        for side in range(2):
-            put(side, extended(edge_tiles(refs[side]), tail))
+        put(*(extended(edge_tiles(ref), tail) for ref in refs))
 
     @pl.when(filtering)
     def _():
         both = [jnp.concatenate(pair, axis=0) for pair in zip(edge_tiles(got_a), edge_tiles(got_b))]
         put_parts(y, pl.ds(0, 16), forward(both, chunk, twiddle))
         wide = jnp.concatenate([keep, keep], axis=1)
-        low_pass(lon, y, z, tables, wide)
-        for side in range(2):
-            put(side, backward(z, rows_at(8 * side), chunk, twiddle))
-
-
-def with_halo(fields, column, tables, twiddle, got_a, got_b, lon, lat_count):
-    assert 2 * fields.shape[1] == 8
+        put_masked(y, masked_parts(lon, products(y, tables), wide))
+        z[...] = products(y, tables)
+        put(*(backward(z, rows_at(8 * side), chunk, twiddle) for side in range(2)))
+
+
+def with_halo(column, tables, twiddle, got_a, got_b, lon, lat_count):
+    tiles = column.shape[0]
+    assert got_a.shape[0] == 8 * tiles
     classes = RADIX // 2 + 1
     vmem = pl.BlockSpec(memory_space=pltpu.VMEM)
     return pl.pallas_call(
         functools.partial(halo_kernel, lon, lat_count),
-        out_shape=[pltpu.VMEM(fields.shape, f32), pltpu.VMEM(column.shape, f32)],
-        in_specs=[vmem] * 6,
+        out_shape=[pltpu.VMEM((2, tiles, 8, LANES), f32), pltpu.VMEM(column.shape, f32)],
+        in_specs=[vmem] * 5,
         out_specs=[vmem] * 2,
         scratch_shapes=[pltpu.VMEM((classes, 16, 2 * WIDE), bf16), pltpu.VMEM((classes, 16, WIDE), f32)],
-        input_output_aliases={4: 0, 5: 1},
+        input_output_aliases={4: 1},
         compiler_params=pltpu.CompilerParams(vmem_limit_bytes=24 << 20),
         name="halo",
-    )(got_a, got_b, tables, twiddle, fields, column)
+    )(got_a, got_b, in_vmem(tables), in_vmem(twiddle), column)
+
+
+def beside(fields, halo, f, l, j, g, toward):
+    levels = fields.shape[1]
+    value = fields[f, l, j, rows_at(8 * g + 1 + toward), :]
+    row = lax.broadcasted_iota(jnp.int32, (8, LANES), 0)
+    slot = pl.ds((f - 1) * levels + l, 1)
+    if toward < 0 and g == 0:
+        return jnp.where(row > 0, value, jnp.broadcast_to(halo[0, j, slot, :], value.shape))
+    if toward > 0 and g == (fields.shape[3] - 8) // 8 - 1:
+        return jnp.where(row < 7, value, jnp.broadcast_to(halo[1, j, slot, :], value.shape))
+    return value
 
 
 def east(v):
@@ -406,11 +426,11 @@
     return [jnp.where(lane > 0, a, b) for a, b in zip(r, r_before)]
 
 
-def thickness_rows(g, lon, fields, trig, thick):
+def thickness_rows(g, lon, fields, halo, trig, thick):
     levels, tiles = fields.shape[1:3]
     tail = lon - (tiles - 1) * LANES
     at = rows_at(8 * g)
-    up, mid, down = 8 * g, 8 * g + 1, 8 * g + 2
+    mid = 8 * g + 1
     south, north = trig[2, at, :], trig[3, at, :]
     found = {}
     for l in range(levels):
@@ -419,8 +439,9 @@
         flux = [(h[j] + he[j]) * (u[j] + ue[j]) for j in range(tiles)]
         flux_west = west(flux, tail)
         for j in range(tiles):
-            v_up, v, v_down = (fields[1, l, j, rows_at(r), :] for r in (up, mid, down))
-            h_up, h_down = (fields[2, l, j, rows_at(r), :] for r in (up, down))
+            v = fields[1, l, j, rows_at(mid), :]
+            v_up, v_down = (beside(fields, halo, 1, l, j, g, to) for to in (-1, 1))
+            h_up, h_down = (beside(fields, halo, 2, l, j, g, to) for to in (-1, 1))
             merid = (h[j] + h_down) * (v + v_down) * north - (h_up + h[j]) * (v_up + v) * south
             found[l, j] = h[j] - (0.25 * time_step) * (flux[j] - flux_west[j] + merid)
     for (l, j), new in found.items():
@@ -428,19 +449,19 @@
         thick[l, at, pl.ds(LANES * j, wide)] = new[:, :wide]
 
 
-def thickness_kernel(lon, fields, trig, cut, _thick, thick):
+def thickness_kernel(lon, fields, halo, trig, cut, _thick, thick):
     groups = trig.shape[1] // 8
 
     @pl.when(jnp.min(cut[...]) < lon // 2)
     def _():
         for g in range(1, groups - 1):
-            thickness_rows(g, lon, fields, trig, thick)
+            thickness_rows(g, lon, fields, halo, trig, thick)
 
     for g in sorted({0, groups - 1}):
-        thickness_rows(g, lon, fields, trig, thick)
-
-
-def winds_kernel(lon, fields, trig, thick, *refs):
+        thickness_rows(g, lon, fields, halo, trig, thick)
+
+
+def winds_kernel(lon, fields, halo, trig, thick, *refs):
     *hops, winds_hbm, thick_hbm, winds, sem = refs
     levels, tiles = fields.shape[1:3]
     rows = trig.shape[1]
@@ -450,17 +471,34 @@
     copies = [pltpu.make_async_copy(thick, thick_hbm, sem.at[rows // 8])]
     copies[0].start()
 
+    row = lax.broadcasted_iota(jnp.int32, (8, LANES), 0)
+
+    def total(load):
+        terms = [load(ref) * mask for ref, mask in zip(hops, masks)]
+        return functools.reduce(jnp.add, terms) if terms else jnp.zeros((8, LANES), f32)
+
     def below(j, at):
-        terms = [ref[j, rows_at(at), :] * mask for ref, mask in zip(hops, masks)]
-        return functools.reduce(jnp.add, terms) if terms else jnp.zeros((8, LANES), f32)
+        return total(lambda ref: ref[j, rows_at(at), :])
+
+    def below_halo(j, side):
+        start = rows + side * levels
+        lines = [total(lambda ref, l=l: ref[j, pl.ds(start + l, 1), :]) for l in range(levels)]
+        return jnp.broadcast_to(functools.reduce(jnp.add, lines), (8, LANES))
+
+    def below_beside(j, g, own, toward):
+        if toward < 0 and g == 0:
+            return jnp.where(row > 0, pltpu.roll(own, 1, 0), below_halo(j, 0))
+        if toward > 0 and g == rows // 8 - 1:
+            return jnp.where(row < 7, pltpu.roll(own, 7, 0), below_halo(j, 1))
+        return below(j, 8 * g + toward)
 
     for g in range(rows // 8):
         at = rows_at(8 * g)
-        up, here, down = 8 * g, 8 * g + 1, 8 * g + 2
+        here = 8 * g + 1
         sine, cosine = trig[0, at, :], trig[1, at, :]
-        s = [below(j, here) for j in range(tiles)]
+        s = [below(j, 8 * g) for j in range(tiles)]
         sum_x = [a - b for a, b in zip(east(s), west(s, tail))]
-        sum_y = [below(j, down) - below(j, up) for j in range(tiles)]
+        sum_y = [below_beside(j, g, s[j], 1) - below_beside(j, g, s[j], -1) for j in range(tiles)]
         found = {}
         for l in reversed(range(levels)):
             h = [fields[2, l, j, rows_at(here), :] for j in range(tiles)]
@@ -468,7 +506,8 @@
             for j in range(tiles):
                 u, v = (fields[f, l, j, rows_at(here), :] for f in range(2))
                 dx = he[j] - hw[j]
-                dy = fields[2, l, j, rows_at(down), :] - fields[2, l, j, rows_at(up), :]
+                h_up, h_down = (beside(fields, halo, 2, l, j, g, to) for to in (-1, 1))
+                dy = h_down - h_up
                 new_u = u - time_step * (0.5 * (sum_x[j] + 0.5 * dx) - coriolis * sine * v)
                 new_v = v - time_step * (0.5 * cosine * (sum_y[j] + 0.5 * dy) + coriolis * sine * u)
                 sum_x[j] = sum_x[j] + dx
@@ -486,31 +525,31 @@
         copy.wait()
 
 
-def stepped_thickness(fields, trig, cut, thick, lon):
+def stepped_thickness(fields, halo, trig, cut, thick, lon):
     vmem = pl.BlockSpec(memory_space=pltpu.VMEM)
     return pl.pallas_call(
         functools.partial(thickness_kernel, lon),
         out_shape=pltpu.VMEM(thick.shape, f32),
-        in_specs=[vmem] * 4,
+        in_specs=[vmem] * 5,
         out_specs=vmem,
-        input_output_aliases={3: 0},
+        input_output_aliases={4: 0},
         compiler_params=pltpu.CompilerParams(vmem_limit_bytes=24 << 20),
         cost_estimate=pl.CostEstimate(flops=4_000_000_000, bytes_accessed=4_000_000, transcendentals=0),
         name="thickness",
-    )(fields, trig, cut, thick)
-
-
-def stepped_winds(fields, trig, thick, hops, shape, lon):
+    )(fields, halo, trig, cut, thick)
+
+
+def stepped_winds(fields, halo, trig, thick, hops, shape, lon):
     hbm = pl.BlockSpec(memory_space=pltpu.HBM)
     return pl.pallas_call(
         functools.partial(winds_kernel, lon),
         out_shape=[jax.ShapeDtypeStruct(shape, f32), jax.ShapeDtypeStruct(thick.shape, f32)],
-        in_specs=[pl.BlockSpec(memory_space=pltpu.VMEM)] * (3 + len(hops)),
+        in_specs=[pl.BlockSpec(memory_space=pltpu.VMEM)] * (4 + len(hops)),
         out_specs=[hbm, hbm],
         scratch_shapes=[pltpu.VMEM(shape, f32), pltpu.SemaphoreType.DMA((trig.shape[1] // 8 + 1,))],
         compiler_params=pltpu.CompilerParams(vmem_limit_bytes=24 << 20),
         name="winds",
-    )(fields, trig, thick, *hops)
+    )(fields, halo, trig, thick, *hops)
 
 
 def swaps(lat_count, lev_count, first):
@@ -533,13 +572,13 @@
     got_b = lax.ppermute(sent_b, ("lat", "lev"), swaps(lat_count, lev_count, 1))
     tables, twiddle = (jnp.asarray(constant) for constant in filter_tables(lon))
     fields, column, new_thick = filtered_fields(winds, thick, cut, trig, tables, twiddle)
-    fields, column = with_halo(fields, column, tables, twiddle, got_a, got_b, lon, lat_count)
+    halo, column = with_halo(column, tables, twiddle, got_a, got_b, lon, lat_count)
     hops = [
         lax.ppermute(column, "lev", [(i, (i - hop) % lev_count) for i in range(lev_count)])
         for hop in range(1, lev_count)
     ]
-    new_thick = stepped_thickness(fields, trig, cut, new_thick, lon)
-    return tuple(stepped_winds(fields, trig, new_thick, hops, winds.shape, lon))
+    new_thick = stepped_thickness(fields, halo, trig, cut, new_thick, lon)
+    return tuple(stepped_winds(fields, halo, trig, new_thick, hops, winds.shape, lon))
 
 
 def solution(mesh):

time: 13.5 us -> 13.4 us (level)
  no operation moved by 1% of the time
where the time goes in v5:
time: 13.4 us; the launch traced here: 13.3 us
  Pallas kernels  5.93 us (44%)
  starting transfers between devices  4.54 us (34%)
  waiting for transfers between devices  2.07 us (15%)
  between operations  0.71 us (5%)
    ppermute x1, starting transfers between devices, per_device(): lax.ppermute(column, 'lev', [(i, (i - hop) % lev_count) for i in range(le...  2.17 us
    pallas_call x1, Pallas kernels, filtered_fields(): pl.pallas_call(filter_kernel, out_shape=[pltpu.VMEM((3, levels, tiles, ro...  1.85 us
    ppermute x1, waiting for transfers between devices, per_device(): got_b = lax.ppermute(sent_b, ('lat', 'lev'), swaps(lat_count, lev_count, 1))  1.76 us
    pallas_call x1, Pallas kernels, stepped_winds(): pl.pallas_call(functools.partial(winds_kernel, lon), out_shape=[jax.Shape...  1.46 us
    ppermute x1, starting transfers between devices, per_device(): got_a = lax.ppermute(sent_a, ('lat', 'lev'), swaps(lat_count, lev_count, 0))  1.28 us
    ppermute x1, starting transfers between devices, per_device(): got_b = lax.ppermute(sent_b, ('lat', 'lev'), swaps(lat_count, lev_count, 1))  1.1 us
    pallas_call x1, Pallas kernels, edges(): pl.pallas_call(functools.partial(edge_kernel, lat_count), out_shape=[edge...  1.01 us
    pallas_call x1, Pallas kernels, stepped_thickness(): pl.pallas_call(functools.partial(thickness_kernel, lon), out_shape=pltpu....  0.83 us
  transfers between devices with their start and end apart: 3, of which 2 were waited for; matrix products, arithmetic and copies ran while one was open for 0% of the time, Pallas kernels for 20%

profile of v5, /device:TPU:25, one launch (start us, length us, event | category | flops | bytes accessed | tf_op | source)
XLA Modules:
  0.0 13.3 jit_solution(2188825689228963565)
XLA Ops:
  0.6 0.0 copy-start
  0.6 0.0 copy-start.1
  0.7 0.0 copy-start.3
  0.7 0.0 copy-start.2
  0.7 1.0 %edges.1 = (f32[96,128]{1,0:T(8,128)S(1)}, f32[96,128]{1,0:T(8,128)S(1)}, f32[4,32,128]{2,1,0:T(8,128)S(1)}, f32[32,128]{1,0:T(8,128)S(1)}) custom-call(f32[2,4,32,1440]{3,2,1,0:T(8,128)} %winds.4, f32[4,32,1440]{2,1,0:T(8,128)} %thick.3, s32[32]{0:T(128)} %cutoff_hbm.1), custom_call_target="tpu_custom_call" | custom-call | flops 4000000000 | bytes 8000000 | tf_op jit(solution)/shard_map/edges/pallas_call | solution.py:150
  1.7 1.3 %collective-permute-start = (f32[96,128]{1,0:T(8,128)S(1)}, f32[96,128]{1,0:T(8,128)S(1)}, u32[]{:S(2)}, u32[]{:S(2)}) collective-permute-start(f32[96,128]{1,0:T(8,128)S(1)} %get-tuple-element.14), channel_id=1, source_target_pairs={{0,2},{1,3},{2,0},{3,1},{4,6},{5,7},{6,4},{7,5},{8,10},{9,11},{10,... | collective-permute-start | bytes 147464 | tf_op jit(solution)/shard_map/ppermute | solution.py:571
  3.0 1.1 %collective-permute-start.1 = (f32[96,128]{1,0:T(8,128)S(1)}, f32[96,128]{1,0:T(8,128)S(1)}, u32[]{:S(2)}, u32[]{:S(2)}) collective-permute-start(f32[96,128]{1,0:T(8,128)S(1)} %get-tuple-element.15), channel_id=1, source_target_pairs={{0,1},{1,0},{2,4},{3,5},{4,2},{5,3},{6,8},{7,9},{8,6},{9,7},{10,12... | collective-permute-start | bytes 147464 | tf_op jit(solution)/shard_map/ppermute | solution.py:572
  4.1 0.0 copy-done
  4.1 0.0 copy-done.1
  4.1 0.0 copy-done.3
  4.1 0.0 copy-done.2
  4.1 1.8 %filter.1 = (f32[3,4,12,40,128]{4,3,2,1,0:T(8,128)S(1)}, f32[12,40,128]{2,1,0:T(8,128)S(1)}, f32[4,32,1440]{2,1,0:T(8,128)S(1)}) custom-call(f32[2,4,32,1440]{3,2,1,0:T(8,128)S(1)} %copy-done.2, f32[4,32,1440]{2,1,0:T(8,128)S(1)} %copy-done.3, bf16[2,256,256]{2,1,0:T(8,128)(2,1)S(1)} %copy-done, f32[2,2,8,128]{3,2,1,0:T(8,128)S(1)} %copy-done.1, ...), custom_call_target="tpu_custom_call" | custom-call | flops 10000000000 | bytes 8000000 | tf_op jit(solution)/shard_map/filter/pallas_call | solution.py:329
  5.9 0.0 collective-permute-done.got_a
  5.9 1.8 %collective-permute-done.1.got_b = f32[96,128]{1,0:T(8,128)S(1)} collective-permute-done((f32[96,128]{1,0:T(8,128)S(1)}, f32[96,128]{1,0:T(8,128)S(1)}, u32[]{:S(2)}, u32[]{:S(2)}) %collective-permute-start.1) | collective-permute-done | bytes 49184 | tf_op jit(solution)/shard_map/ppermute | solution.py:572
  7.7 0.8 %halo.1 = (f32[2,12,8,128]{3,2,1,0:T(8,128)S(1)}, f32[12,40,128]{2,1,0:T(8,128)S(1)}) custom-call(f32[96,128]{1,0:T(8,128)S(1)} %collective-permute-done.got_a, f32[96,128]{1,0:T(8,128)S(1)} %collective-permute-done.1.got_b, bf16[2,256,256]{2,1,0:T(8,128)(2,1)S(1)} %copy-done, f32[2,2,8,128]{3,2,1,0:T(8,128)S(1)} %copy-done.1, ...), custom_call_target="tpu_custom_call", output_to_operand_aliasing={{1}: (4, {})} | custom-call | tf_op jit(solution)/shard_map/halo/pallas_call | solution.py:392
  8.5 2.2 %collective-permute-start.2 = (f32[12,40,128]{2,1,0:T(8,128)S(1)}, f32[12,40,128]{2,1,0:T(8,128)S(1)}, u32[]{:S(2)}, u32[]{:S(2)}) collective-permute-start(f32[12,40,128]{2,1,0:T(8,128)S(1)} %get-tuple-element.19), channel_id=1, source_target_pairs={{0,1},{1,0},{2,3},{3,2},{4,5},{5,4},{6,7},{7,6},{8,9},{9,8},{10,11... | collective-permute-start | bytes 737288 | tf_op jit(solution)/shard_map/ppermute | solution.py:577
  10.7 0.8 %thickness.1.thick = f32[4,32,1440]{2,1,0:T(8,128)S(1)} custom-call(f32[3,4,12,40,128]{4,3,2,1,0:T(8,128)S(1)} %get-tuple-element.13.fields, f32[2,12,8,128]{3,2,1,0:T(8,128)S(1)} %get-tuple-element.17.halo, f32[4,32,128]{2,1,0:T(8,128)S(1)} %get-tuple-element.12.trig, f32[32,128]{1,0:T(8,128)S(1)} %get-tuple-element.11.cut, ...), custom_call_target="tpu_custom_call", output_to_operand_aliasing={{}: (4, {})} | custom-call | flops 4000000000 | bytes 4000000 | tf_op jit(solution)/shard_map/thickness/pallas_call | solution.py:530
  11.5 0.3 %collective-permute-done.2.refs_0_ = f32[12,40,128]{2,1,0:T(8,128)S(1)} collective-permute-done((f32[12,40,128]{2,1,0:T(8,128)S(1)}, f32[12,40,128]{2,1,0:T(8,128)S(1)}, u32[]{:S(2)}, u32[]{:S(2)}) %collective-permute-start.2) | collective-permute-done | bytes 245792 | tf_op jit(solution)/shard_map/ppermute | solution.py:577
  11.8 1.5 %winds.5 = (f32[2,4,32,1440]{3,2,1,0:T(8,128)}, f32[4,32,1440]{2,1,0:T(8,128)}) custom-call(f32[3,4,12,40,128]{4,3,2,1,0:T(8,128)S(1)} %get-tuple-element.13.fields, f32[2,12,8,128]{3,2,1,0:T(8,128)S(1)} %get-tuple-element.17.halo, f32[4,32,128]{2,1,0:T(8,128)S(1)} %get-tuple-element.12.trig, f32[4,32,1440]{2,1,0:T(8,128)S(1)} %thickness.1.thick, ...), custom_call_target="tpu_custom_call" | custom-call | tf_op jit(solution)/shard_map/winds/pallas_call | solution.py:544
Async XLA Ops:
  0.6 3.4 %copy-start = (bf16[2,256,256]{2,1,0:T(8,128)(2,1)S(1)}, bf16[2,256,256]{2,1,0:T(8,128)(2,1)}, u32[]{:S(2)}) copy-start(bf16[2,256,256]{2,1,0:T(8,128)(2,1)} %constant.4.clone.tables) | copy-start | bytes 786436
  0.6 3.4 %copy-start.1 = (f32[2,2,8,128]{3,2,1,0:T(8,128)S(1)}, f32[2,2,8,128]{3,2,1,0:T(8,128)}, u32[]{:S(2)}) copy-start(f32[2,2,8,128]{3,2,1,0:T(8,128)} %constant.5.clone.twiddle) | copy-start | bytes 49156
  0.7 3.4 %copy-start.3 = (f32[4,32,1440]{2,1,0:T(8,128)S(1)}, f32[4,32,1440]{2,1,0:T(8,128)}, u32[]{:S(2)}) copy-start(f32[4,32,1440]{2,1,0:T(8,128)} %thick.3) | copy-start | bytes 2211844
  0.7 3.4 %copy-start.2 = (f32[2,4,32,1440]{3,2,1,0:T(8,128)S(1)}, f32[2,4,32,1440]{3,2,1,0:T(8,128)}, u32[]{:S(2)}) copy-start(f32[2,4,32,1440]{3,2,1,0:T(8,128)} %winds.4) | copy-start | bytes 4423684
  1.7 4.2 %collective-permute-start = (f32[96,128]{1,0:T(8,128)S(1)}, f32[96,128]{1,0:T(8,128)S(1)}, u32[]{:S(2)}, u32[]{:S(2)}) collective-permute-start(f32[96,128]{1,0:T(8,128)S(1)} %get-tuple-element.14), channel_id=1, source_target_pairs={{0,2},{1,3},{2,0},{3,1},{4,6},{5,7},{6,4},{7,5},{8,10},{9,11},{10,... | collective-permute-start | bytes 147464 | tf_op jit(solution)/shard_map/ppermute | solution.py:571
  3.0 4.7 %collective-permute-start.1 = (f32[96,128]{1,0:T(8,128)S(1)}, f32[96,128]{1,0:T(8,128)S(1)}, u32[]{:S(2)}, u32[]{:S(2)}) collective-permute-start(f32[96,128]{1,0:T(8,128)S(1)} %get-tuple-element.15), channel_id=1, source_target_pairs={{0,1},{1,0},{2,4},{3,5},{4,2},{5,3},{6,8},{7,9},{8,6},{9,7},{10,12... | collective-permute-start | bytes 147464 | tf_op jit(solution)/shard_map/ppermute | solution.py:572
  8.5 3.3 %collective-permute-start.2 = (f32[12,40,128]{2,1,0:T(8,128)S(1)}, f32[12,40,128]{2,1,0:T(8,128)S(1)}, u32[]{:S(2)}, u32[]{:S(2)}) collective-permute-start(f32[12,40,128]{2,1,0:T(8,128)S(1)} %get-tuple-element.19), channel_id=1, source_target_pairs={{0,1},{1,0},{2,3},{3,2},{4,5},{5,4},{6,7},{7,6},{8,9},{9,8},{10,11... | collective-permute-start | bytes 737288 | tf_op jit(solution)/shard_map/ppermute | solution.py:577

commit v6 on v5

--- a/solution.py
+++ b/solution.py
@@ -345,21 +345,56 @@
     )(in_vmem(winds), in_vmem(thick), in_vmem(tables), in_vmem(twiddle), cut, trig)
 
 
-def halo_kernel(lon, lat_count, got_a, got_b, tables, twiddle, _column, halo, column, y, z):
+def edge_tiles(ref, tiles, tail):
+    v = [ref[rows_at(8 * j), :] for j in range(tiles)]
+    spare = lane_index() < tail
+    return v[:-1] + [jnp.where(spare, v[-1], 0.0)], jnp.where(spare, rolled(v[-1], tail), v[-1])
+
+
+def filtered_edges(lon, pair, tables, twiddle, y, z):
+    chunk = lon // RADIX
+    both = [jnp.concatenate(rows, axis=0) for rows in zip(*(v for v, _ in pair))]
+    put_parts(y, pl.ds(0, 16), forward(both, chunk, twiddle))
+    keep = jnp.concatenate([keep for _, keep in pair], axis=0)
+    wide = jnp.concatenate([keep, keep], axis=1)
+    put_masked(y, masked_parts(lon, products(y, tables), wide))
+    z[...] = products(y, tables)
+    return [backward(z, rows_at(8 * side), chunk, twiddle) for side in range(2)]
+
+
+def near_kernel(lon, got_a, tables, twiddle, cut, near, y, z):
+    tiles = near.shape[0]
+    tail = lon - (tiles - 1) * LANES
+    edge = edge_tiles(got_a, tiles, tail)
+    idle = jnp.min(cut[...]) >= lon // 2
+    filtering = jnp.min(edge[1]) < lon // 2
+
+    @pl.when(jnp.logical_and(idle, filtering))
+    def _():
+        v = filtered_edges(lon, (edge, edge), tables, twiddle, y, z)[0]
+        for j in range(tiles):
+            near[j] = v[j]
+
+    @pl.when(jnp.logical_and(idle, jnp.logical_not(filtering)))
+    def _():
+        for j, value in enumerate(extended(edge[0], tail)):
+            near[j] = value
+
+
+def halo_kernel(lon, lat_count, got_a, got_b, tables, twiddle, cut, near, _column, halo, column, y, z):
     tiles, rows = column.shape[0], column.shape[1] - 8
     levels = got_a.shape[0] // (2 * tiles)
-    chunk = lon // RADIX
     tail = lon - (tiles - 1) * LANES
     place = lax.axis_index("lat")
     odd = place % 2 == 1
-    refs = (got_a, got_b)
-    keep = jnp.concatenate([ref[rows_at(2 * levels * (tiles - 1), 2 * levels), :] for ref in refs], axis=0)
-    keep = jnp.where(lane_index(16) < tail, rolled(keep, tail), keep)
+    edges_got = [edge_tiles(ref, tiles, tail) for ref in (got_a, got_b)]
     row = lax.broadcasted_iota(jnp.int32, (8, LANES), 0)
-
-    def edge_tiles(ref):
-        v = [ref[rows_at(2 * levels * j, 2 * levels), :] for j in range(tiles)]
-        return v[:-1] + [jnp.where(lane_index() < tail, v[-1], 0.0)]
+    idle = jnp.min(cut[...]) >= lon // 2
+    filtering = [jnp.min(keep) < lon // 2 for _, keep in edges_got]
+    done = jnp.logical_and(idle, jnp.logical_not(filtering[1]))
+    either = jnp.logical_or(*filtering)
+    both = jnp.logical_and(jnp.logical_not(done), either)
+    neither = jnp.logical_and(jnp.logical_not(done), jnp.logical_not(either))
 
     def put(v_a, v_b):
         for j in range(tiles):
@@ -368,37 +403,49 @@
             halo[0, j], halo[1, j] = before, after
             column[j, rows_at(rows), :] = jnp.where(row < levels, pltpu.roll(before, levels, 0), after)
 
-    filtering = jnp.min(keep) < lon // 2
-
-    @pl.when(jnp.logical_not(filtering))
-    def _():
-        put(*(extended(edge_tiles(ref), tail) for ref in refs))
-
-    @pl.when(filtering)
-    def _():
-        both = [jnp.concatenate(pair, axis=0) for pair in zip(edge_tiles(got_a), edge_tiles(got_b))]
-        put_parts(y, pl.ds(0, 16), forward(both, chunk, twiddle))
-        wide = jnp.concatenate([keep, keep], axis=1)
-        put_masked(y, masked_parts(lon, products(y, tables), wide))
-        z[...] = products(y, tables)
-        put(*(backward(z, rows_at(8 * side), chunk, twiddle) for side in range(2)))
-
-
-def with_halo(column, tables, twiddle, got_a, got_b, lon, lat_count):
+    @pl.when(done)
+    def _():
+        put([near[j] for j in range(tiles)], extended(edges_got[1][0], tail))
+
+    @pl.when(neither)
+    def _():
+        put(*(extended(v, tail) for v, _ in edges_got))
+
+    @pl.when(both)
+    def _():
+        put(*filtered_edges(lon, edges_got, tables, twiddle, y, z))
+
+
+def near_edge(got_a, tables, twiddle, cut, lon):
+    vmem = pl.BlockSpec(memory_space=pltpu.VMEM)
+    classes = RADIX // 2 + 1
+    return pl.pallas_call(
+        functools.partial(near_kernel, lon),
+        out_shape=pltpu.VMEM((got_a.shape[0] // 8, 8, LANES), f32),
+        in_specs=[vmem] * 4,
+        out_specs=vmem,
+        scratch_shapes=[pltpu.VMEM((classes, 16, 2 * WIDE), bf16), pltpu.VMEM((classes, 16, WIDE), f32)],
+        compiler_params=pltpu.CompilerParams(vmem_limit_bytes=24 << 20),
+        name="near",
+    )(got_a, in_vmem(tables), in_vmem(twiddle), cut)
+
+
+def with_halo(column, tables, twiddle, cut, got_a, got_b, lon, lat_count):
     tiles = column.shape[0]
     assert got_a.shape[0] == 8 * tiles
+    near = near_edge(got_a, tables, twiddle, cut, lon)
     classes = RADIX // 2 + 1
     vmem = pl.BlockSpec(memory_space=pltpu.VMEM)
     return pl.pallas_call(
         functools.partial(halo_kernel, lon, lat_count),
         out_shape=[pltpu.VMEM((2, tiles, 8, LANES), f32), pltpu.VMEM(column.shape, f32)],
-        in_specs=[vmem] * 5,
+        in_specs=[vmem] * 7,
         out_specs=[vmem] * 2,
         scratch_shapes=[pltpu.VMEM((classes, 16, 2 * WIDE), bf16), pltpu.VMEM((classes, 16, WIDE), f32)],
-        input_output_aliases={4: 1},
+        input_output_aliases={6: 1},
         compiler_params=pltpu.CompilerParams(vmem_limit_bytes=24 << 20),
         name="halo",
-    )(got_a, got_b, in_vmem(tables), in_vmem(twiddle), column)
+    )(got_a, got_b, in_vmem(tables), in_vmem(twiddle), cut, near, column)
 
 
 def beside(fields, halo, f, l, j, g, toward):
@@ -572,7 +619,7 @@
     got_b = lax.ppermute(sent_b, ("lat", "lev"), swaps(lat_count, lev_count, 1))
     tables, twiddle = (jnp.asarray(constant) for constant in filter_tables(lon))
     fields, column, new_thick = filtered_fields(winds, thick, cut, trig, tables, twiddle)
-    halo, column = with_halo(column, tables, twiddle, got_a, got_b, lon, lat_count)
+    halo, column = with_halo(column, tables, twiddle, cut, got_a, got_b, lon, lat_count)
     hops = [
         lax.ppermute(column, "lev", [(i, (i - hop) % lev_count) for i in range(lev_count)])
         for hop in range(1, lev_count)

time: 13.4 us -> 13.1 us (0.978)
  the two profiles are of different devices: /device:TPU:25 before, /device:TPU:3 now
where the time goes in v6:
time: 13.1 us; the launch traced here: 12.9 us
  Pallas kernels  8.39 us (64%)
  starting transfers between devices  3.78 us (29%)
  between operations  0.74 us (6%)
    pallas_call x1, Pallas kernels, filtered_fields(): pl.pallas_call(filter_kernel, out_shape=[pltpu.VMEM((3, levels, tiles, ro...  3.39 us
    ppermute x1, starting transfers between devices, per_device(): got_b = lax.ppermute(sent_b, ('lat', 'lev'), swaps(lat_count, lev_count, 1))  2.41 us
    pallas_call x1, Pallas kernels, stepped_thickness(): pl.pallas_call(functools.partial(thickness_kernel, lon), out_shape=pltpu....  1.53 us
    pallas_call x1, Pallas kernels, stepped_winds(): pl.pallas_call(functools.partial(winds_kernel, lon), out_shape=[jax.Shape...  1.47 us
    ppermute x1, starting transfers between devices, per_device(): lax.ppermute(column, 'lev', [(i, (i - hop) % lev_count) for i in range(le...  1.3 us
    pallas_call x1, Pallas kernels, edges(): pl.pallas_call(functools.partial(edge_kernel, lat_count), out_shape=[edge...  1.01 us
    pallas_call x1, Pallas kernels, with_halo(): pl.pallas_call(functools.partial(halo_kernel, lon, lat_count), out_shape=...  0.8 us
  transfers between devices with their start and end apart: 3, of which 0 were waited for; matrix products, arithmetic and copies ran while one was open for 0% of the time, Pallas kernels for 40%

profile of v6, /device:TPU:3, one launch (start us, length us, event | category | flops | bytes accessed | tf_op | source)
XLA Modules:
  0.0 12.9 jit_solution(879996730441503681)
XLA Ops:
  0.6 0.0 copy-start
  0.6 0.0 copy-start.1
  0.7 0.0 copy-start.3
  0.7 0.0 copy-start.2
  0.7 1.0 %edges.1 = (f32[96,128]{1,0:T(8,128)S(1)}, f32[96,128]{1,0:T(8,128)S(1)}, f32[4,32,128]{2,1,0:T(8,128)S(1)}, f32[32,128]{1,0:T(8,128)S(1)}) custom-call(f32[2,4,32,1440]{3,2,1,0:T(8,128)} %winds.4, f32[4,32,1440]{2,1,0:T(8,128)} %thick.3, s32[32]{0:T(128)} %cutoff_hbm.1), custom_call_target="tpu_custom_call" | custom-call | flops 4000000000 | bytes 8000000 | tf_op jit(solution)/shard_map/edges/pallas_call | solution.py:150
  1.7 0.1 collective-permute-start
  1.8 2.4 %collective-permute-start.1 = (f32[96,128]{1,0:T(8,128)S(1)}, f32[96,128]{1,0:T(8,128)S(1)}, u32[]{:S(2)}, u32[]{:S(2)}) collective-permute-start(f32[96,128]{1,0:T(8,128)S(1)} %get-tuple-element.15), channel_id=1, source_target_pairs={{0,1},{1,0},{2,4},{3,5},{4,2},{5,3},{6,8},{7,9},{8,6},{9,7},{10,12... | collective-permute-start | bytes 147464 | tf_op jit(solution)/shard_map/ppermute | solution.py:619
  4.2 0.0 copy-done
  4.2 0.0 copy-done.1
  4.2 0.0 copy-done.3
  4.2 0.0 copy-done.2
  4.2 3.4 %filter.1 = (f32[3,4,12,40,128]{4,3,2,1,0:T(8,128)S(1)}, f32[12,40,128]{2,1,0:T(8,128)S(1)}, f32[4,32,1440]{2,1,0:T(8,128)S(1)}) custom-call(f32[2,4,32,1440]{3,2,1,0:T(8,128)S(1)} %copy-done.2, f32[4,32,1440]{2,1,0:T(8,128)S(1)} %copy-done.3, bf16[2,256,256]{2,1,0:T(8,128)(2,1)S(1)} %copy-done, f32[2,2,8,128]{3,2,1,0:T(8,128)S(1)} %copy-done.1, ...), custom_call_target="tpu_custom_call" | custom-call | flops 10000000000 | bytes 8000000 | tf_op jit(solution)/shard_map/filter/pallas_call | solution.py:329
  7.6 0.0 collective-permute-done.got_a
  7.6 0.2 %near.1 = f32[12,8,128]{2,1,0:T(8,128)S(1)} custom-call(f32[96,128]{1,0:T(8,128)S(1)} %collective-permute-done.got_a, bf16[2,256,256]{2,1,0:T(8,128)(2,1)S(1)} %copy-done, f32[2,2,8,128]{3,2,1,0:T(8,128)S(1)} %copy-done.1, f32[32,128]{1,0:T(8,128)S(1)} %get-tuple-element.11.cut), custom_call_target="tpu_custom_call" | custom-call | tf_op jit(solution)/shard_map/near/pallas_call | solution.py:422
  7.8 0.0 collective-permute-done.1.got_b
  7.8 0.8 %halo.1 = (f32[2,12,8,128]{3,2,1,0:T(8,128)S(1)}, f32[12,40,128]{2,1,0:T(8,128)S(1)}) custom-call(f32[96,128]{1,0:T(8,128)S(1)} %collective-permute-done.got_a, f32[96,128]{1,0:T(8,128)S(1)} %collective-permute-done.1.got_b, bf16[2,256,256]{2,1,0:T(8,128)(2,1)S(1)} %copy-done, f32[2,2,8,128]{3,2,1,0:T(8,128)S(1)} %copy-done.1, ...), custom_call_target="tpu_custom_call", output_to_operand_aliasing={{1}: (6, {})} | custom-call | tf_op jit(solution)/shard_map/halo/pallas_call | solution.py:439
  8.6 1.3 %collective-permute-start.2 = (f32[12,40,128]{2,1,0:T(8,128)S(1)}, f32[12,40,128]{2,1,0:T(8,128)S(1)}, u32[]{:S(2)}, u32[]{:S(2)}) collective-permute-start(f32[12,40,128]{2,1,0:T(8,128)S(1)} %get-tuple-element.19), channel_id=1, source_target_pairs={{0,1},{1,0},{2,3},{3,2},{4,5},{5,4},{6,7},{7,6},{8,9},{9,8},{10,11... | collective-permute-start | bytes 737288 | tf_op jit(solution)/shard_map/ppermute | solution.py:624
  9.9 1.5 %thickness.1.thick = f32[4,32,1440]{2,1,0:T(8,128)S(1)} custom-call(f32[3,4,12,40,128]{4,3,2,1,0:T(8,128)S(1)} %get-tuple-element.13.fields, f32[2,12,8,128]{3,2,1,0:T(8,128)S(1)} %get-tuple-element.17.halo, f32[4,32,128]{2,1,0:T(8,128)S(1)} %get-tuple-element.12.trig, f32[32,128]{1,0:T(8,128)S(1)} %get-tuple-element.11.cut, ...), custom_call_target="tpu_custom_call", output_to_operand_aliasing={{}: (4, {})} | custom-call | flops 4000000000 | bytes 4000000 | tf_op jit(solution)/shard_map/thickness/pallas_call | solution.py:577
  11.5 0.0 collective-permute-done.2.refs_0_
  11.5 1.5 %winds.5 = (f32[2,4,32,1440]{3,2,1,0:T(8,128)}, f32[4,32,1440]{2,1,0:T(8,128)}) custom-call(f32[3,4,12,40,128]{4,3,2,1,0:T(8,128)S(1)} %get-tuple-element.13.fields, f32[2,12,8,128]{3,2,1,0:T(8,128)S(1)} %get-tuple-element.17.halo, f32[4,32,128]{2,1,0:T(8,128)S(1)} %get-tuple-element.12.trig, f32[4,32,1440]{2,1,0:T(8,128)S(1)} %thickness.1.thick, ...), custom_call_target="tpu_custom_call" | custom-call | tf_op jit(solution)/shard_map/winds/pallas_call | solution.py:591
Async XLA Ops:
  0.6 3.6 %copy-start = (bf16[2,256,256]{2,1,0:T(8,128)(2,1)S(1)}, bf16[2,256,256]{2,1,0:T(8,128)(2,1)}, u32[]{:S(2)}) copy-start(bf16[2,256,256]{2,1,0:T(8,128)(2,1)} %constant.4.clone.tables) | copy-start | bytes 786436
  0.6 3.5 %copy-start.1 = (f32[2,2,8,128]{3,2,1,0:T(8,128)S(1)}, f32[2,2,8,128]{3,2,1,0:T(8,128)}, u32[]{:S(2)}) copy-start(f32[2,2,8,128]{3,2,1,0:T(8,128)} %constant.5.clone.twiddle) | copy-start | bytes 49156
  0.7 3.5 %copy-start.3 = (f32[4,32,1440]{2,1,0:T(8,128)S(1)}, f32[4,32,1440]{2,1,0:T(8,128)}, u32[]{:S(2)}) copy-start(f32[4,32,1440]{2,1,0:T(8,128)} %thick.3) | copy-start | bytes 2211844
  0.7 3.5 %copy-start.2 = (f32[2,4,32,1440]{3,2,1,0:T(8,128)S(1)}, f32[2,4,32,1440]{3,2,1,0:T(8,128)}, u32[]{:S(2)}) copy-start(f32[2,4,32,1440]{3,2,1,0:T(8,128)} %winds.4) | copy-start | bytes 4423684
  1.7 5.9 %collective-permute-start = (f32[96,128]{1,0:T(8,128)S(1)}, f32[96,128]{1,0:T(8,128)S(1)}, u32[]{:S(2)}, u32[]{:S(2)}) collective-permute-start(f32[96,128]{1,0:T(8,128)S(1)} %get-tuple-element.14), channel_id=1, source_target_pairs={{0,2},{1,3},{2,0},{3,1},{4,6},{5,7},{6,4},{7,5},{8,10},{9,11},{10,... | collective-permute-start | bytes 147464 | tf_op jit(solution)/shard_map/ppermute | solution.py:618
  1.8 6.0 %collective-permute-start.1 = (f32[96,128]{1,0:T(8,128)S(1)}, f32[96,128]{1,0:T(8,128)S(1)}, u32[]{:S(2)}, u32[]{:S(2)}) collective-permute-start(f32[96,128]{1,0:T(8,128)S(1)} %get-tuple-element.15), channel_id=1, source_target_pairs={{0,1},{1,0},{2,4},{3,5},{4,2},{5,3},{6,8},{7,9},{8,6},{9,7},{10,12... | collective-permute-start | bytes 147464 | tf_op jit(solution)/shard_map/ppermute | solution.py:619
  8.6 2.8 %collective-permute-start.2 = (f32[12,40,128]{2,1,0:T(8,128)S(1)}, f32[12,40,128]{2,1,0:T(8,128)S(1)}, u32[]{:S(2)}, u32[]{:S(2)}) collective-permute-start(f32[12,40,128]{2,1,0:T(8,128)S(1)} %get-tuple-element.19), channel_id=1, source_target_pairs={{0,1},{1,0},{2,3},{3,2},{4,5},{5,4},{6,7},{7,6},{8,9},{9,8},{10,11... | collective-permute-start | bytes 737288 | tf_op jit(solution)/shard_map/ppermute | solution.py:624

commit v7 on v6

--- a/solution.py
+++ b/solution.py
@@ -365,20 +365,22 @@
 def near_kernel(lon, got_a, tables, twiddle, cut, near, y, z):
     tiles = near.shape[0]
     tail = lon - (tiles - 1) * LANES
-    edge = edge_tiles(got_a, tiles, tail)
-    idle = jnp.min(cut[...]) >= lon // 2
-    filtering = jnp.min(edge[1]) < lon // 2
-
-    @pl.when(jnp.logical_and(idle, filtering))
+
+    @pl.when(jnp.min(cut[...]) >= lon // 2)
     def _():
-        v = filtered_edges(lon, (edge, edge), tables, twiddle, y, z)[0]
-        for j in range(tiles):
-            near[j] = v[j]
-
-    @pl.when(jnp.logical_and(idle, jnp.logical_not(filtering)))
-    def _():
-        for j, value in enumerate(extended(edge[0], tail)):
-            near[j] = value
+        edge = edge_tiles(got_a, tiles, tail)
+        filtering = jnp.min(edge[1]) < lon // 2
+
+        @pl.when(filtering)
+        def _():
+            v = filtered_edges(lon, (edge, edge), tables, twiddle, y, z)[0]
+            for j in range(tiles):
+                near[j] = v[j]
+
+        @pl.when(jnp.logical_not(filtering))
+        def _():
+            for j, value in enumerate(extended(edge[0], tail)):
+                near[j] = value
 
 
 def halo_kernel(lon, lat_count, got_a, got_b, tables, twiddle, cut, near, _column, halo, column, y, z):

time: 13.1 us -> 13 us (level)
  transfers between devices with their start and end apart: 3 -> 3, of which waited for: 0 -> 0; matrix products, arithmetic and copies ran while one was open for 0% -> 0% of each run, Pallas kernels for 40% -> 39%
where the time goes in v7:
time: 13 us; the launch traced here: 12.9 us
  Pallas kernels  8.32 us (64%)
  starting transfers between devices  3.78 us (29%)
  between operations  0.74 us (6%)
    pallas_call x1, Pallas kernels, filtered_fields(): pl.pallas_call(filter_kernel, out_shape=[pltpu.VMEM((3, levels, tiles, ro...  3.39 us
    ppermute x1, starting transfers between devices, per_device(): got_b = lax.ppermute(sent_b, ('lat', 'lev'), swaps(lat_count, lev_count, 1))  2.41 us
    pallas_call x1, Pallas kernels, stepped_thickness(): pl.pallas_call(functools.partial(thickness_kernel, lon), out_shape=pltpu....  1.53 us
    pallas_call x1, Pallas kernels, stepped_winds(): pl.pallas_call(functools.partial(winds_kernel, lon), out_shape=[jax.Shape...  1.47 us
    ppermute x1, starting transfers between devices, per_device(): lax.ppermute(column, 'lev', [(i, (i - hop) % lev_count) for i in range(le...  1.3 us
    pallas_call x1, Pallas kernels, edges(): pl.pallas_call(functools.partial(edge_kernel, lat_count), out_shape=[edge...  1.01 us
    pallas_call x1, Pallas kernels, with_halo(): pl.pallas_call(functools.partial(halo_kernel, lon, lat_count), out_shape=...  0.8 us
  transfers between devices with their start and end apart: 3, of which 0 were waited for; matrix products, arithmetic and copies ran while one was open for 0% of the time, Pallas kernels for 39%

profile of v7, /device:TPU:3, one launch (start us, length us, event | category | flops | bytes accessed | tf_op | source)
XLA Modules:
  0.0 12.9 jit_solution(3821579113763213922)
XLA Ops:
  0.6 0.0 copy-start
  0.6 0.0 copy-start.1
  0.7 0.0 copy-start.3
  0.7 0.0 copy-start.2
  0.7 1.0 %edges.1 = (f32[96,128]{1,0:T(8,128)S(1)}, f32[96,128]{1,0:T(8,128)S(1)}, f32[4,32,128]{2,1,0:T(8,128)S(1)}, f32[32,128]{1,0:T(8,128)S(1)}) custom-call(f32[2,4,32,1440]{3,2,1,0:T(8,128)} %winds.4, f32[4,32,1440]{2,1,0:T(8,128)} %thick.3, s32[32]{0:T(128)} %cutoff_hbm.1), custom_call_target="tpu_custom_call" | custom-call | flops 4000000000 | bytes 8000000 | tf_op jit(solution)/shard_map/edges/pallas_call | solution.py:150
  1.7 0.1 collective-permute-start
  1.8 2.4 %collective-permute-start.1 = (f32[96,128]{1,0:T(8,128)S(1)}, f32[96,128]{1,0:T(8,128)S(1)}, u32[]{:S(2)}, u32[]{:S(2)}) collective-permute-start(f32[96,128]{1,0:T(8,128)S(1)} %get-tuple-element.15), channel_id=1, source_target_pairs={{0,1},{1,0},{2,4},{3,5},{4,2},{5,3},{6,8},{7,9},{8,6},{9,7},{10,12... | collective-permute-start | bytes 147464 | tf_op jit(solution)/shard_map/ppermute | solution.py:621
  4.2 0.0 copy-done
  4.2 0.0 copy-done.1
  4.2 0.0 copy-done.3
  4.2 0.0 copy-done.2
  4.2 3.4 %filter.1 = (f32[3,4,12,40,128]{4,3,2,1,0:T(8,128)S(1)}, f32[12,40,128]{2,1,0:T(8,128)S(1)}, f32[4,32,1440]{2,1,0:T(8,128)S(1)}) custom-call(f32[2,4,32,1440]{3,2,1,0:T(8,128)S(1)} %copy-done.2, f32[4,32,1440]{2,1,0:T(8,128)S(1)} %copy-done.3, bf16[2,256,256]{2,1,0:T(8,128)(2,1)S(1)} %copy-done, f32[2,2,8,128]{3,2,1,0:T(8,128)S(1)} %copy-done.1, ...), custom_call_target="tpu_custom_call" | custom-call | flops 10000000000 | bytes 8000000 | tf_op jit(solution)/shard_map/filter/pallas_call | solution.py:329
  7.6 0.0 collective-permute-done.got_a
  7.6 0.1 near.1
  7.7 0.0 collective-permute-done.1.got_b
  7.7 0.8 %halo.1 = (f32[2,12,8,128]{3,2,1,0:T(8,128)S(1)}, f32[12,40,128]{2,1,0:T(8,128)S(1)}) custom-call(f32[96,128]{1,0:T(8,128)S(1)} %collective-permute-done.got_a, f32[96,128]{1,0:T(8,128)S(1)} %collective-permute-done.1.got_b, bf16[2,256,256]{2,1,0:T(8,128)(2,1)S(1)} %copy-done, f32[2,2,8,128]{3,2,1,0:T(8,128)S(1)} %copy-done.1, ...), custom_call_target="tpu_custom_call", output_to_operand_aliasing={{1}: (6, {})} | custom-call | tf_op jit(solution)/shard_map/halo/pallas_call | solution.py:441
  8.6 1.3 %collective-permute-start.2 = (f32[12,40,128]{2,1,0:T(8,128)S(1)}, f32[12,40,128]{2,1,0:T(8,128)S(1)}, u32[]{:S(2)}, u32[]{:S(2)}) collective-permute-start(f32[12,40,128]{2,1,0:T(8,128)S(1)} %get-tuple-element.19), channel_id=1, source_target_pairs={{0,1},{1,0},{2,3},{3,2},{4,5},{5,4},{6,7},{7,6},{8,9},{9,8},{10,11... | collective-permute-start | bytes 737288 | tf_op jit(solution)/shard_map/ppermute | solution.py:626
  9.9 1.5 %thickness.1.thick = f32[4,32,1440]{2,1,0:T(8,128)S(1)} custom-call(f32[3,4,12,40,128]{4,3,2,1,0:T(8,128)S(1)} %get-tuple-element.13.fields, f32[2,12,8,128]{3,2,1,0:T(8,128)S(1)} %get-tuple-element.17.halo, f32[4,32,128]{2,1,0:T(8,128)S(1)} %get-tuple-element.12.trig, f32[32,128]{1,0:T(8,128)S(1)} %get-tuple-element.11.cut, ...), custom_call_target="tpu_custom_call", output_to_operand_aliasing={{}: (4, {})} | custom-call | flops 4000000000 | bytes 4000000 | tf_op jit(solution)/shard_map/thickness/pallas_call | solution.py:579
  11.4 0.0 collective-permute-done.2.refs_0_
  11.4 1.5 %winds.5 = (f32[2,4,32,1440]{3,2,1,0:T(8,128)}, f32[4,32,1440]{2,1,0:T(8,128)}) custom-call(f32[3,4,12,40,128]{4,3,2,1,0:T(8,128)S(1)} %get-tuple-element.13.fields, f32[2,12,8,128]{3,2,1,0:T(8,128)S(1)} %get-tuple-element.17.halo, f32[4,32,128]{2,1,0:T(8,128)S(1)} %get-tuple-element.12.trig, f32[4,32,1440]{2,1,0:T(8,128)S(1)} %thickness.1.thick, ...), custom_call_target="tpu_custom_call" | custom-call | tf_op jit(solution)/shard_map/winds/pallas_call | solution.py:593
Async XLA Ops:
  0.6 3.6 %copy-start = (bf16[2,256,256]{2,1,0:T(8,128)(2,1)S(1)}, bf16[2,256,256]{2,1,0:T(8,128)(2,1)}, u32[]{:S(2)}) copy-start(bf16[2,256,256]{2,1,0:T(8,128)(2,1)} %constant.4.clone.tables) | copy-start | bytes 786436
  0.6 3.5 %copy-start.1 = (f32[2,2,8,128]{3,2,1,0:T(8,128)S(1)}, f32[2,2,8,128]{3,2,1,0:T(8,128)}, u32[]{:S(2)}) copy-start(f32[2,2,8,128]{3,2,1,0:T(8,128)} %constant.5.clone.twiddle) | copy-start | bytes 49156
  0.7 3.5 %copy-start.3 = (f32[4,32,1440]{2,1,0:T(8,128)S(1)}, f32[4,32,1440]{2,1,0:T(8,128)}, u32[]{:S(2)}) copy-start(f32[4,32,1440]{2,1,0:T(8,128)} %thick.3) | copy-start | bytes 2211844
  0.7 3.5 %copy-start.2 = (f32[2,4,32,1440]{3,2,1,0:T(8,128)S(1)}, f32[2,4,32,1440]{3,2,1,0:T(8,128)}, u32[]{:S(2)}) copy-start(f32[2,4,32,1440]{3,2,1,0:T(8,128)} %winds.4) | copy-start | bytes 4423684
  1.7 5.9 %collective-permute-start = (f32[96,128]{1,0:T(8,128)S(1)}, f32[96,128]{1,0:T(8,128)S(1)}, u32[]{:S(2)}, u32[]{:S(2)}) collective-permute-start(f32[96,128]{1,0:T(8,128)S(1)} %get-tuple-element.14), channel_id=1, source_target_pairs={{0,2},{1,3},{2,0},{3,1},{4,6},{5,7},{6,4},{7,5},{8,10},{9,11},{10,... | collective-permute-start | bytes 147464 | tf_op jit(solution)/shard_map/ppermute | solution.py:620
  1.8 6.0 %collective-permute-start.1 = (f32[96,128]{1,0:T(8,128)S(1)}, f32[96,128]{1,0:T(8,128)S(1)}, u32[]{:S(2)}, u32[]{:S(2)}) collective-permute-start(f32[96,128]{1,0:T(8,128)S(1)} %get-tuple-element.15), channel_id=1, source_target_pairs={{0,1},{1,0},{2,4},{3,5},{4,2},{5,3},{6,8},{7,9},{8,6},{9,7},{10,12... | collective-permute-start | bytes 147464 | tf_op jit(solution)/shard_map/ppermute | solution.py:621
  8.6 2.8 %collective-permute-start.2 = (f32[12,40,128]{2,1,0:T(8,128)S(1)}, f32[12,40,128]{2,1,0:T(8,128)S(1)}, u32[]{:S(2)}, u32[]{:S(2)}) collective-permute-start(f32[12,40,128]{2,1,0:T(8,128)S(1)} %get-tuple-element.19), channel_id=1, source_target_pairs={{0,1},{1,0},{2,3},{3,2},{4,5},{5,4},{6,7},{7,6},{8,9},{9,8},{10,11... | collective-permute-start | bytes 737288 | tf_op jit(solution)/shard_map/ppermute | solution.py:626
